TPU v7x, 512 devices: a whole 4x8x8 slice. The times are simulated.
512 devices in a mesh: exp: 64 (over x, y, core), rep: 8 (over z).
Axes of the slice: x: 4, y: 8, z: 8, core: 2. Of those that a mesh axis runs over, the one named last changes fastest.
Arguments:
- passages_in: bfloat16 [92160, 2048], P(('exp', 'rep')), may hold values from -24 to 32
- routes: int32 [92160, 2], P(('exp', 'rep')), may hold values from 0 to 63, all different within a row; in each aligned block of 180 rows (0 to 179, 180 to 359, ...) at most 11 rows name the same one
- route_weights: float32 [92160, 2], P(('exp', 'rep')), may hold values from 0.2 to 1
- gate_weight: bfloat16 [64, 2048, 704], P('exp', 'rep'), may hold values from -0.125 to 0.125
- up_weight: bfloat16 [64, 2048, 704], P('exp', 'rep'), may hold values from -0.125 to 0.125
- down_weight: bfloat16 [64, 704, 2048], P('exp', None, 'rep'), may hold values from -0.21875 to 0.21875
- projection: bfloat16 [2048, 128], replicated, may hold values from -2 to 2
- queries: bfloat16 [128, 32, 128], P('rep'), may hold values from -6 to 6
- positives: int32 [128], replicated, may hold values from 0 to 511, as said below
Outputs:
- states: bfloat16 [92160, 2048], P(('exp', 'rep'))
- grad_projection: float32 [2048, 128], P('exp')
- mean_loss: float32 [], replicated
Inputs may be any that keep to these rules, and one draw needn't show every extreme that they name: `routes`: the two experts of a token differ. Among the rows of one device, no expert is named more than 11 times, and in some device's rows some expert is named exactly 11 times; every expert is named somewhere. `positives`: distinct queries have distinct positive passages.
All inputs are finite; a program needn't handle non-finite values.
Results may differ from a plain program's by a relative error of at most 0.0065.
Values may be sent and summed in bfloat16 or wider, within the bound.
No kernel may reach another device: no remote copies, remote signals or barrier semaphores. Data moves between devices by JAX's collectives and lax.ppermute only.
A program may use at most 64 MiB of HBM per device.

v0:
```python
import jax
import jax.numpy as jnp
from jax import lax
from jax.sharding import PartitionSpec as P

PAS_LEN = 180


soft_temp = 0.05
logit_gain = 1.5
norm_eps = 1e-06


def unit_rows(values):
    values = values.astype(jnp.float32)
    radius = jnp.sqrt(jnp.sum(values * values, axis=-1, keepdims=True) + norm_eps)
    return (values / radius, radius)


def token_scores(unit_block, query_rows, passage_count, query_count):
    scores = lax.dot_general(
        unit_block, query_rows, (((1,), (1,)), ((), ())), preferred_element_type=jnp.float32
    )
    weights = jnp.exp(scores / soft_temp)
    passage_len = unit_block.shape[0] // passage_count
    totals = jnp.sum(weights.reshape(passage_count, passage_len, -1), axis=1)
    logits = logit_gain * jnp.sum(
        (soft_temp * jnp.log(totals)).reshape(passage_count, query_count, -1), axis=2
    )
    return (weights, totals, logits)


def unit_grads(weights, totals, factor, query_rows, passage_count, query_count):
    passage_len = weights.shape[0] // passage_count
    query_len = weights.shape[1] // query_count
    shaped = weights.reshape(passage_count, passage_len, query_count, query_len) / totals.reshape(
        passage_count, 1, query_count, query_len
    )
    coeffs = (shaped * (logit_gain * factor)[:, None, :, None]).astype(jnp.bfloat16)
    coeffs = coeffs.reshape(passage_count * passage_len, query_count * query_len)
    return jnp.dot(coeffs, query_rows, preferred_element_type=jnp.float32)


def body(
    passages_in,
    routes,
    route_weights,
    gate_weight,
    up_weight,
    down_weight,
    projection,
    queries,
    positives,
):
    tok_count, model_width = passages_in.shape
    top_count = routes.shape[1]
    experts = lax.axis_size("exp")
    rep_count = lax.axis_size("rep")
    capacity = max(2, 2 * tok_count * top_count // experts)
    flat_route = routes.reshape(-1)
    onehot = (flat_route[:, None] == jnp.arange(experts, dtype=jnp.int32)[None, :]).astype(
        jnp.int32
    )
    slot_rank = jnp.sum((jnp.cumsum(onehot, axis=0) - onehot) * onehot, axis=1)
    places = flat_route * capacity + slot_rank
    sources = jnp.arange(tok_count * top_count, dtype=jnp.int32) // top_count
    outgoing = (
        jnp.zeros((experts * capacity, model_width), jnp.bfloat16)
        .at[places]
        .set(passages_in[sources])
    )
    arrived = lax.all_to_all(
        outgoing.reshape(experts, capacity, model_width),
        "exp",
        split_axis=0,
        concat_axis=0,
        tiled=True,
    )
    expert_rows = arrived.reshape(experts * capacity, model_width)

    def add_rows(shard_part):
        return jnp.dot(expert_rows, shard_part[0], preferred_element_type=jnp.float32)

    gate_sum = add_rows(lax.all_gather(gate_weight, "rep", axis=1, tiled=True))
    up_sum = add_rows(lax.all_gather(up_weight, "rep", axis=1, tiled=True))
    hidden = (jax.nn.silu(gate_sum) * up_sum).astype(jnp.bfloat16)
    expert_out = jnp.dot(
        hidden,
        lax.all_gather(down_weight, "rep", axis=2, tiled=True)[0],
        preferred_element_type=jnp.float32,
    ).astype(jnp.bfloat16)
    returned = lax.all_to_all(
        expert_out.reshape(experts, capacity, model_width),
        "exp",
        split_axis=0,
        concat_axis=0,
        tiled=True,
    )
    picked = returned.reshape(experts * capacity, model_width)[places].reshape(
        tok_count, top_count, model_width
    )
    mixed_sum = passages_in.astype(jnp.float32) + jnp.sum(
        route_weights[:, :, None] * picked.astype(jnp.float32), axis=1
    )
    states = mixed_sum.astype(jnp.bfloat16)
    projected = jnp.dot(states, projection, preferred_element_type=jnp.float32)
    unit_f32, radius = unit_rows(projected)
    unit_vec = unit_f32.astype(jnp.bfloat16)
    query_unit = unit_rows(queries)[0].astype(jnp.bfloat16)
    query_block, query_len, unit_width = queries.shape
    pas_count = tok_count // PAS_LEN
    total_queries = query_block * rep_count
    all_queries = lax.all_gather(query_unit, "rep", axis=0, tiled=True)
    query_rows = all_queries.reshape(total_queries * query_len, unit_width)
    owners = lax.axis_index(("exp", "rep")) * pas_count + jnp.arange(pas_count, dtype=jnp.int32)
    weights, totals, logits = token_scores(unit_vec, query_rows, pas_count, total_queries)
    positive_hit = owners[:, None] == positives[None, :]
    exp_logits = jnp.exp(logits)
    partition, pos_sum = lax.psum(
        (jnp.sum(exp_logits, axis=0), jnp.sum(jnp.where(positive_hit, logits, 0.0))), ("exp", "rep")
    )
    mean_loss = (jnp.sum(jnp.log(partition)) - pos_sum) / total_queries
    factor = exp_logits / partition[None, :] - positive_hit.astype(jnp.float32)
    grad_unit = unit_grads(weights, totals, factor, query_rows, pas_count, total_queries)
    grad_vec = (
        (grad_unit - unit_f32 * jnp.sum(unit_f32 * grad_unit, axis=1, keepdims=True)) / radius
    ).astype(jnp.bfloat16)
    row_sums = lax.psum_scatter(
        lax.dot_general(
            states, grad_vec, (((0,), (0,)), ((), ())), preferred_element_type=jnp.float32
        ),
        "exp",
        scatter_dimension=0,
        tiled=True,
    )
    grad_projection = lax.psum(row_sums, "rep")
    return (states, grad_projection, mean_loss)


def solution(mesh):
    in_specs = (
        P(("exp", "rep"), None),
        P(("exp", "rep"), None),
        P(("exp", "rep"), None),
        P("exp", "rep", None),
        P("exp", "rep", None),
        P("exp", None, "rep"),
        P(),
        P("rep", None, None),
        P(),
    )
    out_specs = (P(("exp", "rep"), None), P("exp", None), P())
    return jax.shard_map(body, mesh=mesh, in_specs=in_specs, out_specs=out_specs, check_vma=False)
```

profile of v0, /device:TPU:6, one launch (start us, length us, event | category | flops | bytes accessed | tf_op | source)
XLA Modules:
  0.0 604.7 jit_solution(8828364484753994428)
XLA Ops:
  7.2 0.7 all-gather.5.cloned.1.call-update
  8.0 0.7 all-gather.7.cloned.1.call-update
  8.7 0.8 copy.20
  9.7 0.9 reduce-window.6
  10.8 0.7 broadcast_multiply_fusion
  12.0 8.1 %scatter_custom_fusion = bf16[704,2048]{1,0:T(8,128)(2,1)S(1)} fusion(s32[360]{0:T(512)S(1)} %fusion.22, bf16[180,2048]{1,0:T(8,128)(2,1)} %param.9, s32[1024]{0:T(1024)S(1)} %pad_clamp_fusion.1, bf16[]{:T(256)} %constant.21.clone.1), kind=kCustom, calls=%fused_computation.16 | custom fusion | bytes 2884096 | tf_op jit(solution)/shard_map/scatter | solution.py:70
  20.1 2.9 reshape.185
  23.0 11.2 %all-to-all-start = ((bf16[64,11,2048]{2,1,0:T(8,128)(2,1)}), bf16[64,11,2048]{2,1,0:T(8,128)(2,1)}, u32[]{:S(2)}, u32[]{:S(2)}) async-start(bf16[64,11,2048]{2,1,0:T(8,128)(2,1)} %reshape.185), calls=%async_computation | async-start | bytes 8388608 | tf_op jit(solution)/shard_map/all_to_all | solution.py:72
  34.4 0.5 all-gather.9.cloned.1.call-update
  34.9 93.1 %all-to-all-done = bf16[64,11,2048]{2,1,0:T(8,128)(2,1)} async-done(((bf16[64,11,2048]{2,1,0:T(8,128)(2,1)}), bf16[64,11,2048]{2,1,0:T(8,128)(2,1)}, u32[]{:S(2)}, u32[]{:S(2)}) %all-to-all-start) | async-done | bytes 2883616 | tf_op jit(solution)/shard_map/all_to_all | solution.py:72
  128.0 3.4 reshape.186
  131.4 5.6 fusion.4
  137.1 45.0 %all-gather.9.cloned.1.call-done = bf16[1,704,2048]{2,1,0:T(8,128)(2,1)} async-done(((bf16[1,704,256]{2,1,0:T(8,128)(2,1)}), bf16[1,704,2048]{2,1,0:T(8,128)(2,1)}) %all-gather.9.cloned.1.call-update) | async-done | bytes 2883600 | tf_op jit(solution)/shard_map/all_gather | solution.py:89
  182.1 10.4 %convolution_convert_fusion = bf16[704,2048]{1,0:T(8,128)(2,1)} fusion(bf16[1,704,2048]{2,1,0:T(8,128)(2,1)} %all-gather.9.cloned.1.call-done, f32[704,704]{1,0:T(8,128)} %fusion.4, bf16[704,2048]{1,0:T(8,128)(2,1)S(1)} %reshape.186, bf16[1,2048,704]{1,2,0:T(8,128)(2,1)} %all-gather.7.cloned.1.call-done), kind=kOutput, calls=%fused_computation.5 | convolution fusion | flops 4064501760 | bytes 13516800 | tf_op jit(solution)/shard_map/dot_general | solution.py:87
  192.4 4.8 reshape.187
  197.2 10.8 %all-to-all-start.1 = ((bf16[64,11,2048]{2,1,0:T(8,128)(2,1)}), bf16[64,11,2048]{2,1,0:T(8,128)(2,1)}, u32[]{:S(2)}, u32[]{:S(2)}) async-start(bf16[64,11,2048]{2,1,0:T(8,128)(2,1)} %reshape.187), calls=%async_computation.1 | async-start | bytes 8388608 | tf_op jit(solution)/shard_map/all_to_all | solution.py:92
  208.2 0.8 fusion.15
  209.3 0.8 copy.18
  210.1 91.7 %all-to-all-done.1 = bf16[64,11,2048]{2,1,0:T(8,128)(2,1)} async-done(((bf16[64,11,2048]{2,1,0:T(8,128)(2,1)}), bf16[64,11,2048]{2,1,0:T(8,128)(2,1)}, u32[]{:S(2)}, u32[]{:S(2)}) %all-to-all-start.1) | async-done | bytes 2883616 | tf_op jit(solution)/shard_map/all_to_all | solution.py:92
  301.8 3.4 reshape.188
  305.2 3.1 gather_fusion
  308.3 3.4 reshape.191
  311.7 5.6 multiply_reduce_fusion
  317.5 0.5 multiply_reduce_fusion.2
  318.0 3.8 fusion.28
  322.0 0.6 fusion.26
  322.6 96.4 %all-reduce.1 = (f32[128]{0:T(128)S(1)}, f32[]{:T(128)}) all-reduce(f32[128]{0:T(128)S(1)} %get-tuple-element.8, f32[]{:T(128)} %get-tuple-element.7), channel_id=1, replica_groups=mesh['exp'=64,'rep'=8] {'exp','rep'}, use_global_device_ids=true, to_apply=%region_9.10 | all-reduce | flops 129 | bytes 1032 | tf_op jit(solution)/shard_map/psum | solution.py:119
  419.0 0.6 log_reduce_fusion
  419.8 2.5 multiply_reduce_fusion.1
  422.3 1.6 fusion.18
  425.2 140.3 %reduce-scatter.2.cloned.1.call-done = f32[32,128]{1,0:T(8,128)} async-done(((f32[2048,128]{1,0:T(8,128)}), f32[32,128]{1,0:T(8,128)}) %reduce-scatter.2.cloned.1.call-update) | async-done | bytes 16400 | tf_op jit(solution)/shard_map/reduce_scatter | solution.py:128
  565.5 31.5 %psum.22 = f32[32,128]{1,0:T(8,128)} all-reduce(f32[32,128]{1,0:T(8,128)} %reduce-scatter.2.cloned.1.call-done), channel_id=1, replica_groups=mesh['exp'=64,'rep'=8] {'rep'}, use_global_device_ids=true, to_apply=%region_12.13 | all-reduce | flops 4096 | bytes 32768 | tf_op jit(solution)/shard_map/psum | solution.py:136
  (46 shorter events, 2.3 us)
Async XLA Ops:
  7.2 310.3 %copy-start = (bf16[2048,128]{1,0:T(8,128)(2,1)S(1)}, bf16[2048,128]{1,0:T(8,128)(2,1)}, u32[]{:S(2)}) copy-start(bf16[2048,128]{1,0:T(8,128)(2,1)} %param.15) | copy-start | bytes 1572868
  7.2 124.3 %all-gather.5.cloned.1.call-start = ((), (), s32[]{:S(2)}) async-start(), calls=%async_computation.3 | async-start | bytes 3244032 | tf_op jit(solution)/shard_map/all_gather | solution.py:84
  7.9 129.1 %all-gather.7.cloned.1.call-start = ((), (), s32[]{:S(2)}) async-start(), calls=%async_computation.4 | async-start | bytes 3244032 | tf_op jit(solution)/shard_map/all_gather | solution.py:85
  23.0 105.0 %all-to-all-start = ((bf16[64,11,2048]{2,1,0:T(8,128)(2,1)}), bf16[64,11,2048]{2,1,0:T(8,128)(2,1)}, u32[]{:S(2)}, u32[]{:S(2)}) async-start(bf16[64,11,2048]{2,1,0:T(8,128)(2,1)} %reshape.185), calls=%async_computation | async-start | bytes 8388608 | tf_op jit(solution)/shard_map/all_to_all | solution.py:72
  34.2 147.9 %all-gather.9.cloned.1.call-start = ((), (), s32[]{:S(2)}) async-start(), calls=%async_computation.5 | async-start | bytes 3244032 | tf_op jit(solution)/shard_map/all_gather | solution.py:89
  197.2 10.9 %copy-start.4 = (bf16[16,32,128]{2,1,0:T(8,128)(2,1)S(1)}, bf16[16,32,128]{2,1,0:T(8,128)(2,1)}, u32[]{:S(2)}) copy-start(bf16[16,32,128]{2,1,0:T(8,128)(2,1)} %param.16) | copy-start | bytes 393220
  197.2 12.1 %copy-start.5 = (f32[180,2]{0,1:T(2,128)S(1)}, f32[180,2]{0,1:T(2,128)}, u32[]{:S(2)}) copy-start(f32[180,2]{0,1:T(2,128)} %param.11) | copy-start | bytes 4324
  197.2 104.6 %all-to-all-start.1 = ((bf16[64,11,2048]{2,1,0:T(8,128)(2,1)}), bf16[64,11,2048]{2,1,0:T(8,128)(2,1)}, u32[]{:S(2)}, u32[]{:S(2)}) async-start(bf16[64,11,2048]{2,1,0:T(8,128)(2,1)} %reshape.187), calls=%async_computation.1 | async-start | bytes 8388608 | tf_op jit(solution)/shard_map/all_to_all | solution.py:92
  208.0 110.0 %all-gather.11.cloned.1.call-start = ((), (), s32[]{:S(2)}) async-start(), calls=%async_computation.6 | async-start | bytes 1179648 | tf_op jit(solution)/shard_map/all_gather | solution.py:113
  209.0 356.5 %reduce-scatter.2.cloned.1.call-start = ((), (), s32[]{:S(2)}) async-start(), calls=%async_computation.7 | async-start | bytes 1064960 | tf_op jit(solution)/shard_map/reduce_scatter | solution.py:128
  311.7 5.6 copy-start.3
  317.5 104.9 %copy-start.1 = (bf16[180,2048]{1,0:T(8,128)(2,1)}, bf16[180,2048]{1,0:T(8,128)(2,1)S(1)}, u32[]{:S(2)}) copy-start(bf16[180,2048]{1,0:T(8,128)(2,1)S(1)} %add_convert_fusion) | copy-start | bytes 2211844
  317.5 4.5 copy-start.6
  318.0 101.8 %copy-start.2 = (bf16[128,32,128]{2,1,0:T(8,128)(2,1)S(1)}, bf16[128,32,128]{2,1,0:T(8,128)(2,1)}, u32[]{:S(2)}) copy-start(bf16[128,32,128]{2,1,0:T(8,128)(2,1)} %all-gather.11.cloned.1.call-done) | copy-start | bytes 3145732
Sparse Core Ops, SparseCore 0:
  10.0 59.8 all-gather.4
  71.9 53.6 all-gather.6
  127.6 54.4 all-gather.8
  210.6 39.9 all-gather.10
  424.0 141.4 reduce-scatter.1
where the time goes:
time: 606 us; the launch traced here: 605 us
  waiting for transfers between devices  372 us (61%)
  blocking collectives  128 us (21%)
  local copies, waits for them, and re-layouts  31.4 us (5%)
  matrix products  24.3 us (4%)
  starting transfers between devices  22.6 us (4%)
  between operations  16.5 us (3%)
  other arithmetic  9.89 us (2%)
    reduce_scatter x1, waiting for transfers between devices, body(): lax.psum_scatter(lax.dot_general(states, grad_vec, (((0,), (0,)), ((), ()...  140 us
    psum x1, blocking collectives, body(): lax.psum((jnp.sum(exp_logits, axis=0), jnp.sum(jnp.where(positive_hit, lo...  96.4 us
    all_to_all x1, waiting for transfers between devices, body(): lax.all_to_all(outgoing.reshape(experts, capacity, model_width), 'exp', s...  93.1 us
    all_to_all x1, waiting for transfers between devices, body(): lax.all_to_all(expert_out.reshape(experts, capacity, model_width), 'exp',...  91.7 us
    all_gather x1, waiting for transfers between devices, body(): lax.all_gather(down_weight, 'rep', axis=2, tiled=True)[0]  45 us
    psum x1, blocking collectives, body(): grad_projection = lax.psum(row_sums, 'rep')  31.5 us
  transfers between devices with their start and end apart: 7, of which 4 were waited for; matrix products, arithmetic and copies ran while one was open for 7% of the time, Pallas kernels for 0%

commit v1 on v0

v1 whole, which is shorter than its diff:
```python
import jax
import jax.numpy as jnp
from jax import lax
from jax.experimental import pallas as pl
from jax.experimental.pallas import tpu as pltpu
from jax.sharding import PartitionSpec as P

PAS_LEN = 180
HEAD = 8

soft_temp = 0.05
logit_gain = 1.5
norm_eps = 1e-06
F32 = jnp.float32
BF16 = jnp.bfloat16


def unit_rows(values):
    values = values.astype(F32)
    radius = jnp.sqrt(jnp.sum(values * values, axis=-1, keepdims=True) + norm_eps)
    return (values / radius, radius)


def hidden_kernel(x_ref, w_ref, h_ref, acc_ref):
    step = pl.program_id(0)
    part = lax.dot_general(
        x_ref[...], w_ref[0], (((1,), (1,)), ((), ())), preferred_element_type=F32
    )

    @pl.when(step == 0)
    def _():
        acc_ref[...] = part

    @pl.when(step > 0)
    def _():
        acc_ref[...] += part

    @pl.when(step == pl.num_programs(0) - 1)
    def _():
        half = acc_ref.shape[1] // 2
        gate = acc_ref[:, :half]
        up = acc_ref[:, half:]
        h_ref[...] = (gate / (1.0 + jnp.exp(-gate)) * up).astype(BF16)


def hidden_rows(rows, gate_up):
    count, model = rows.shape
    reps, wide, width = gate_up.shape
    return pl.pallas_call(
        hidden_kernel,
        grid=(reps,),
        in_specs=[
            pl.BlockSpec((count, width), lambda r: (0, r)),
            pl.BlockSpec((1, wide, width), lambda r: (r, 0, 0)),
        ],
        out_specs=pl.BlockSpec((count, wide // 2), lambda r: (0, 0)),
        out_shape=jax.ShapeDtypeStruct((count, wide // 2), BF16),
        scratch_shapes=[pltpu.VMEM((count, wide), F32)],
        compiler_params=pltpu.CompilerParams(vmem_limit_bytes=40 * 2**20),
        cost_estimate=pl.CostEstimate(
            flops=2 * count * model * wide, bytes_accessed=2 * wide * model, transcendentals=0
        ),
    )(rows, gate_up)


def out_kernel(h_ref, w_ref, o_ref):
    o_ref[...] = jnp.dot(h_ref[...], w_ref[0], preferred_element_type=F32).astype(BF16)


def out_rows(hidden, down):
    count, ff = hidden.shape
    reps, _, width = down.shape
    return pl.pallas_call(
        out_kernel,
        grid=(reps,),
        in_specs=[
            pl.BlockSpec((count, ff), lambda r: (0, 0)),
            pl.BlockSpec((1, ff, width), lambda r: (r, 0, 0)),
        ],
        out_specs=pl.BlockSpec((count, width), lambda r: (0, r)),
        out_shape=jax.ShapeDtypeStruct((count, reps * width), BF16),
        compiler_params=pltpu.CompilerParams(vmem_limit_bytes=40 * 2**20),
        cost_estimate=pl.CostEstimate(
            flops=2 * count * ff * reps * width, bytes_accessed=2 * ff * reps * width, transcendentals=0
        ),
    )(hidden, down)


def body(
    passages_in,
    routes,
    route_weights,
    gate_weight,
    up_weight,
    down_weight,
    projection,
    queries,
    positives,
):
    tok_count, model_width = passages_in.shape
    top_count = routes.shape[1]
    experts = lax.axis_size("exp")
    rep_count = lax.axis_size("rep")
    capacity = max(2, 2 * tok_count * top_count // experts)
    tail = capacity - HEAD
    pieces = model_width // 128

    gate_up = jnp.concatenate([gate_weight[0].T, up_weight[0].T], axis=0)
    gate_up = lax.all_gather(gate_up, "rep", axis=0, tiled=False)
    down = lax.all_gather(down_weight[0], "rep", axis=0, tiled=False)

    flat = routes.T.reshape(-1)
    onehot = flat[:, None] == jnp.arange(experts, dtype=jnp.int32)[None, :]
    count = flat.shape[0]
    before = jnp.arange(count)[:, None] > jnp.arange(count)[None, :]
    earlier = jnp.dot(before.astype(BF16), onehot.astype(BF16), preferred_element_type=F32)
    rank = jnp.sum(jnp.where(onehot, earlier, 0.0), axis=1).astype(jnp.int32)
    head_place = jnp.where(rank < HEAD, flat * HEAD + rank, -1).reshape(top_count, tok_count)
    tail_place = jnp.where(rank >= HEAD, flat * tail + rank - HEAD, -1).reshape(top_count, tok_count)

    def dispatch(place, slots):
        hit = place[:, None, :] == jnp.arange(slots, dtype=jnp.int32)[None, :, None]
        return jnp.dot(
            jnp.any(hit, axis=0).astype(BF16), passages_in, preferred_element_type=F32
        ).astype(BF16)

    def exchange(rows, shape):
        moved = lax.all_to_all(rows.reshape(shape), "exp", split_axis=0, concat_axis=0, tiled=True)
        return moved.reshape(rows.shape)

    head_shape = (experts, HEAD, model_width)
    tail_shape = (experts, tail * pieces, 128)
    head_in = exchange(dispatch(head_place, experts * HEAD), head_shape)
    tail_in = exchange(dispatch(tail_place, experts * tail), tail_shape)
    head_hidden = hidden_rows(head_in, gate_up)
    tail_hidden = hidden_rows(tail_in, gate_up)
    head_back = exchange(out_rows(head_hidden, down), head_shape)
    tail_back = exchange(out_rows(tail_hidden, down), tail_shape)

    def combine(place, back):
        slots = back.shape[0]
        hit = place[:, :, None] == jnp.arange(slots, dtype=jnp.int32)[None, None, :]
        mix = jnp.sum(jnp.where(hit, route_weights.T[:, :, None], 0.0), axis=0)
        high = mix.astype(BF16)
        low = (mix - high.astype(F32)).astype(BF16)
        return jnp.dot(high, back, preferred_element_type=F32) + jnp.dot(
            low, back, preferred_element_type=F32
        )

    states = (
        passages_in.astype(F32) + combine(head_place, head_back) + combine(tail_place, tail_back)
    ).astype(BF16)

    projected = jnp.dot(states, projection, preferred_element_type=F32)
    unit_f32, radius = unit_rows(projected)
    unit_vec = unit_f32.astype(BF16)
    query_unit = unit_rows(queries)[0].astype(BF16)
    query_block, query_len, unit_width = queries.shape
    total_queries = query_block * rep_count
    all_queries = lax.all_gather(query_unit, "rep", axis=0, tiled=True)
    query_rows = all_queries.reshape(total_queries * query_len, unit_width)
    owner = lax.axis_index(("exp", "rep"))

    scores = lax.dot_general(
        unit_vec, query_rows, (((1,), (1,)), ((), ())), preferred_element_type=F32
    )
    weights = jnp.exp(scores / soft_temp)
    totals = jnp.sum(weights, axis=0)
    logits = logit_gain * jnp.sum(
        (soft_temp * jnp.log(totals)).reshape(total_queries, query_len), axis=1
    )
    positive_hit = owner == positives
    exp_logits = jnp.exp(logits)

    def total_over(values, axis):
        size = lax.axis_size(axis)
        sent = jnp.broadcast_to(values[None], (size,) + values.shape)
        return jnp.sum(lax.all_to_all(sent, axis, 0, 0, tiled=True), axis=0)

    shares = jnp.stack([exp_logits, jnp.where(positive_hit, logits, 0.0)])
    sums = total_over(total_over(shares, "exp"), "rep")
    partition = sums[0]
    mean_loss = (jnp.sum(jnp.log(partition)) - jnp.sum(sums[1])) / total_queries
    factor = exp_logits / partition - positive_hit.astype(F32)
    scale = (logit_gain * factor)[:, None] / totals.reshape(total_queries, query_len)
    coeffs = (weights * scale.reshape(1, -1)).astype(BF16)
    grad_unit = jnp.dot(coeffs, query_rows, preferred_element_type=F32)
    grad_vec = (
        (grad_unit - unit_f32 * jnp.sum(unit_f32 * grad_unit, axis=1, keepdims=True)) / radius
    ).astype(BF16)
    share = lax.dot_general(
        states, grad_vec, (((0,), (0,)), ((), ())), preferred_element_type=F32
    ).astype(BF16)
    rows_out = model_width // experts
    parts = lax.all_to_all(
        share.reshape(experts, rows_out, unit_width), "exp", split_axis=0, concat_axis=0, tiled=True
    )
    grad_projection = total_over(jnp.sum(parts.astype(F32), axis=0), "rep")
    return (states, grad_projection, mean_loss)


def solution(mesh):
    in_specs = (
        P(("exp", "rep"), None),
        P(("exp", "rep"), None),
        P(("exp", "rep"), None),
        P("exp", "rep", None),
        P("exp", "rep", None),
        P("exp", None, "rep"),
        P(),
        P("rep", None, None),
        P(),
    )
    out_specs = (P(("exp", "rep"), None), P("exp", None), P())
    return jax.shard_map(body, mesh=mesh, in_specs=in_specs, out_specs=out_specs, check_vma=False)
```

time: 606 us -> 328 us (0.54)
  waiting for transfers between devices: 372 us -> 148 us
  blocking collectives: 128 us -> 50.2 us
  Pallas kernels: 0 us -> 19.2 us
  starting transfers between devices: 22.6 us -> 39.5 us
  matrix products: 24.3 us -> 13.6 us
  local copies, waits for them, and re-layouts: 31.4 us -> 23.1 us
  other arithmetic: 9.89 us -> 16.6 us
    reduce_scatter x1 -> x0, waiting for transfers between devices: 140 us -> none  [body(): lax.psum_scatter(lax.dot_general(states, grad_vec, (((0,), (0,)), ((), ()...]
    psum x2 -> x0, blocking collectives: 128 us -> none  [the longest x1 96.4 us: body(): lax.psum((jnp.sum(exp_logits, axis=0), jnp.sum(jnp.where(positive_hit, lo...]
    all_to_all x2 -> x5, waiting for transfers between devices: 185 us -> 73.2 us  [the longest x4 65.1 us: exchange(): lax.all_to_all(rows.reshape(shape), 'exp', split_axis=0, concat_axis=0, t...]
    all_to_all x0 -> x3, blocking collectives: none -> 50.2 us  [the longest x2 27.6 us: total_over(): return jnp.sum(lax.all_to_all(sent, axis, 0, 0, tiled=True), axis=0)]
    all_gather x3 -> x2, waiting for transfers between devices: 45 us -> 73.8 us  [the longest x1 39.4 us: body(): down = lax.all_gather(down_weight[0], 'rep', axis=0, tiled=False)]
    pallas_call x0 -> x4, Pallas kernels: none -> 19.2 us  [the longest x2 12.3 us: hidden_rows(): pl.pallas_call(hidden_kernel, grid=(reps,), in_specs=[pl.BlockSpec((count...]
    all_to_all x2 -> x5, starting transfers between devices: 22 us -> 39.2 us  [the longest x4 35.8 us: exchange(): lax.all_to_all(rows.reshape(shape), 'exp', split_axis=0, concat_axis=0, t...]
    unnamed x16 -> x44, local copies, waits for them, and re-layouts: 1.6 us -> 12.2 us
  transfers between devices with their start and end apart: 7 -> 8, of which waited for: 4 -> 6; matrix products, arithmetic and copies ran while one was open for 7% -> 6% of each run, Pallas kernels for 0% -> 6%
where the time goes in v1:
time: 328 us; the launch traced here: 326 us
  waiting for transfers between devices  148 us (45%)
  blocking collectives  50.2 us (15%)
  starting transfers between devices  39.5 us (12%)
  local copies, waits for them, and re-layouts  23.1 us (7%)
  Pallas kernels  19.2 us (6%)
  other arithmetic  16.6 us (5%)
  between operations  16.6 us (5%)
  matrix products  13.6 us (4%)
    all_to_all x4, waiting for transfers between devices, exchange(): lax.all_to_all(rows.reshape(shape), 'exp', split_axis=0, concat_axis=0, t...  65.1 us
    all_gather x1, waiting for transfers between devices, body(): down = lax.all_gather(down_weight[0], 'rep', axis=0, tiled=False)  39.4 us
    all_to_all x4, starting transfers between devices, exchange(): lax.all_to_all(rows.reshape(shape), 'exp', split_axis=0, concat_axis=0, t...  35.8 us
    all_gather x1, waiting for transfers between devices, body(): gate_up = lax.all_gather(gate_up, 'rep', axis=0, tiled=False)  34.4 us
    all_to_all x2, blocking collectives, total_over(): return jnp.sum(lax.all_to_all(sent, axis, 0, 0, tiled=True), axis=0)  27.6 us
    all_to_all x1, blocking collectives, body(): lax.all_to_all(share.reshape(experts, rows_out, unit_width), 'exp', split...  22.6 us
    pallas_call x2, Pallas kernels, hidden_rows(): pl.pallas_call(hidden_kernel, grid=(reps,), in_specs=[pl.BlockSpec((count...  12.3 us
    unnamed x44, local copies, waits for them, and re-layouts  12.2 us
  transfers between devices with their start and end apart: 8, of which 6 were waited for; matrix products, arithmetic and copies ran while one was open for 6% of the time, Pallas kernels for 6%

profile of v1, /device:TPU:6, one launch (start us, length us, event | category | flops | bytes accessed | tf_op | source)
XLA Modules:
  0.0 326.5 jit_solution(3392022203161192409)
XLA Ops:
  7.2 2.1 pad_maximum_fusion
  11.6 10.8 %all-to-all-start.2 = ((bf16[64,48,128]{2,1,0:T(8,128)(2,1)}), bf16[64,48,128]{2,1,0:T(8,128)(2,1)S(1)}, u32[]{:S(2)}, u32[]{:S(2)}) async-start(bf16[64,48,128]{2,1,0:T(8,128)(2,1)} %reshape.124), calls=%async_computation.2 | async-start | bytes 1572864 | tf_op jit(solution)/shard_map/all_to_all | solution.py:128
  23.3 2.1 fusion.1
  25.4 18.9 %all-to-all-done.2 = bf16[64,48,128]{2,1,0:T(8,128)(2,1)S(1)} async-done(((bf16[64,48,128]{2,1,0:T(8,128)(2,1)}), bf16[64,48,128]{2,1,0:T(8,128)(2,1)S(1)}, u32[]{:S(2)}, u32[]{:S(2)}) %all-to-all-start.2) | async-done | bytes 786464 | tf_op jit(solution)/shard_map/all_to_all | solution.py:128
  45.2 7.3 %all-to-all-start = ((bf16[64,8,2048]{2,1,0:T(8,128)(2,1)}), bf16[64,8,2048]{2,1,0:T(8,128)(2,1)S(1)}, u32[]{:S(2)}, u32[]{:S(2)}) async-start(bf16[64,8,2048]{2,1,0:T(8,128)(2,1)} %fusion.1), calls=%async_computation | async-start | bytes 4194304 | tf_op jit(solution)/shard_map/all_to_all | solution.py:128
  53.9 34.4 %all-gather.9.cloned.1.call-done = bf16[11264,256]{1,0:T(8,128)(2,1)} async-done(((bf16[1408,256]{1,0:T(8,128)(2,1)}), bf16[11264,256]{1,0:T(8,128)(2,1)}) %all-gather.9.cloned.1.call-update) | async-done | bytes 5767184 | tf_op jit(solution)/shard_map/all_gather | solution.py:109
  88.3 2.6 copy-done.3
  91.0 4.4 %shard_map.114.h_ref = bf16[192,704]{1,0:T(8,128)(2,1)S(1)} custom-call(bf16[192,2048]{1,0:T(8,128)(2,1)S(1)} %reshape.125.x_ref, bf16[8,1408,256]{2,1,0:T(8,128)(2,1)S(1)} %bitcast.44), custom_call_target="tpu_custom_call" | custom-call | flops 1107296256 | bytes 5767168 | tf_op jit(solution)/shard_map/pallas_call | solution.py:49
  96.1 39.4 %all-gather.5.cloned.1.call-done.w_ref = bf16[8,704,256]{2,1,0:T(8,128)(2,1)} async-done(((bf16[1,704,256]{2,1,0:T(8,128)(2,1)}), bf16[8,704,256]{2,1,0:T(8,128)(2,1)}) %all-gather.5.cloned.1.call-update) | async-done | bytes 2883600 | tf_op jit(solution)/shard_map/all_gather | solution.py:110
  135.5 1.8 copy-done.1
  138.2 2.1 shard_map.115
  141.6 10.5 %all-to-all-start.3 = ((bf16[64,48,128]{2,1,0:T(8,128)(2,1)}), bf16[64,48,128]{2,1,0:T(8,128)(2,1)S(1)}, u32[]{:S(2)}, u32[]{:S(2)}) async-start(bf16[64,48,128]{2,1,0:T(8,128)(2,1)} %reshape.126), calls=%async_computation.3 | async-start | bytes 1572864 | tf_op jit(solution)/shard_map/all_to_all | solution.py:128
  152.1 2.6 copy-done.4
  154.7 7.9 %shard_map.112.h_ref = bf16[512,704]{1,0:T(8,128)(2,1)S(1)} custom-call(bf16[512,2048]{1,0:T(8,128)(2,1)S(1)} %bitcast.46, bf16[8,1408,256]{2,1,0:T(8,128)(2,1)S(1)} %bitcast.45), custom_call_target="tpu_custom_call" | custom-call | flops 2952790016 | bytes 5767168 | tf_op jit(solution)/shard_map/pallas_call | solution.py:49
  162.6 4.8 %shard_map.113 = bf16[512,2048]{1,0:T(8,128)(2,1)} custom-call(bf16[512,704]{1,0:T(8,128)(2,1)S(1)} %shard_map.112.h_ref, bf16[8,704,256]{2,1,0:T(8,128)(2,1)S(1)} %copy-done.2), custom_call_target="tpu_custom_call" | custom-call | flops 1476395008 | bytes 2883584 | tf_op jit(solution)/shard_map/pallas_call | solution.py:73
  167.4 6.5 %all-to-all-done.3 = bf16[64,48,128]{2,1,0:T(8,128)(2,1)S(1)} async-done(((bf16[64,48,128]{2,1,0:T(8,128)(2,1)}), bf16[64,48,128]{2,1,0:T(8,128)(2,1)S(1)}, u32[]{:S(2)}, u32[]{:S(2)}) %all-to-all-start.3) | async-done | bytes 786464 | tf_op jit(solution)/shard_map/all_to_all | solution.py:128
  174.9 7.3 %all-to-all-start.1 = ((bf16[64,8,2048]{2,1,0:T(8,128)(2,1)}), bf16[64,8,2048]{2,1,0:T(8,128)(2,1)S(1)}, u32[]{:S(2)}, u32[]{:S(2)}) async-start(bf16[64,8,2048]{2,1,0:T(8,128)(2,1)} %bitcast.9), calls=%async_computation.1 | async-start | bytes 4194304 | tf_op jit(solution)/shard_map/all_to_all | solution.py:128
  183.8 2.0 fusion.12
  185.8 1.8 fusion.14
  189.0 2.4 fusion.24
  191.4 39.7 %all-to-all-done.1 = bf16[64,8,2048]{2,1,0:T(8,128)(2,1)S(1)} async-done(((bf16[64,8,2048]{2,1,0:T(8,128)(2,1)}), bf16[64,8,2048]{2,1,0:T(8,128)(2,1)S(1)}, u32[]{:S(2)}, u32[]{:S(2)}) %all-to-all-start.1) | async-done | bytes 2097184 | tf_op jit(solution)/shard_map/all_to_all | solution.py:128
  231.1 1.6 fusion.6
  237.0 2.2 fusion.30
  241.2 1.5 reduce_sum.132
  243.4 15.8 %all_to_all.40 = f32[64,2,128]{2,1,0:T(2,128)} all-to-all(f32[64,2,128]{2,1,0:T(2,128)S(1)} %broadcast_in_dim.75), channel_id=1, replica_groups=mesh['exp'=64,'rep'=8] {'exp'}, dimensions={0} | all-to-all | bytes 131072 | tf_op jit(solution)/shard_map/all_to_all | solution.py:178
  259.2 1.5 reduce_sum.133
  261.4 11.9 %all_to_all.41 = f32[8,2,128]{2,1,0:T(2,128)} all-to-all(f32[8,2,128]{2,1,0:T(2,128)S(1)} %broadcast_in_dim.76), channel_id=1, replica_groups=mesh['exp'=64,'rep'=8] {'rep'}, dimensions={0} | all-to-all | bytes 16384 | tf_op jit(solution)/shard_map/all_to_all | solution.py:178
  276.6 1.5 div.56
  278.8 2.0 multiply_reduce_fusion
  281.5 22.6 %all_to_all.42 = bf16[64,32,128]{2,1,0:T(8,128)(2,1)S(1)} all-to-all(bf16[64,32,128]{2,1,0:T(8,128)(2,1)S(1)} %bitcast.49), channel_id=1, replica_groups=mesh['exp'=64,'rep'=8] {'exp'}, dimensions={0} | all-to-all | bytes 1048576 | tf_op jit(solution)/shard_map/all_to_all | solution.py:195
  304.8 3.4 %all-to-all-start.7 = ((f32[8,32,128]{2,1,0:T(8,128)}), f32[8,32,128]{2,1,0:T(8,128)S(1)}, u32[]{:S(2)}, u32[]{:S(2)}) async-start(f32[8,32,128]{2,1,0:T(8,128)} %broadcast_in_dim.77), calls=%async_computation.7 | async-start | bytes 262144 | tf_op jit(solution)/shard_map/all_to_all | solution.py:178
  310.1 8.1 %all-to-all-done.7 = f32[8,32,128]{2,1,0:T(8,128)S(1)} async-done(((f32[8,32,128]{2,1,0:T(8,128)}), f32[8,32,128]{2,1,0:T(8,128)S(1)}, u32[]{:S(2)}, u32[]{:S(2)}) %all-to-all-start.7) | async-done | bytes 131104 | tf_op jit(solution)/shard_map/all_to_all | solution.py:178
  (86 shorter events, 26.5 us)
Async XLA Ops:
  7.2 228.3 %copy-start = (bf16[2048,128]{1,0:T(8,128)(2,1)S(1)}, bf16[2048,128]{1,0:T(8,128)(2,1)}, u32[]{:S(2)}) copy-start(bf16[2048,128]{1,0:T(8,128)(2,1)} %param.15) | copy-start | bytes 1572868
  7.2 2.2 copy-start.19
  7.2 2.7 copy-start.7
  7.2 81.1 %all-gather.9.cloned.1.call-start = ((), (), s32[]{:S(2)}) async-start(), calls=%async_computation.10 | async-start | bytes 6488064 | tf_op jit(solution)/shard_map/all_gather | solution.py:109
  11.6 32.7 %all-to-all-start.2 = ((bf16[64,48,128]{2,1,0:T(8,128)(2,1)}), bf16[64,48,128]{2,1,0:T(8,128)(2,1)S(1)}, u32[]{:S(2)}, u32[]{:S(2)}) async-start(bf16[64,48,128]{2,1,0:T(8,128)(2,1)} %reshape.124), calls=%async_computation.2 | async-start | bytes 1572864 | tf_op jit(solution)/shard_map/all_to_all | solution.py:128
  22.4 113.0 %all-gather.5.cloned.1.call-start = ((), (), s32[]{:S(2)}) async-start(), calls=%async_computation.8 | async-start | bytes 3244032 | tf_op jit(solution)/shard_map/all_gather | solution.py:110
  44.3 0.9 copy-start.12
  45.2 96.4 %all-to-all-start = ((bf16[64,8,2048]{2,1,0:T(8,128)(2,1)}), bf16[64,8,2048]{2,1,0:T(8,128)(2,1)S(1)}, u32[]{:S(2)}, u32[]{:S(2)}) async-start(bf16[64,8,2048]{2,1,0:T(8,128)(2,1)} %fusion.1), calls=%async_computation | async-start | bytes 4194304 | tf_op jit(solution)/shard_map/all_to_all | solution.py:128
  88.3 2.6 copy-start.3
  95.4 0.7 copy-start.5
  135.5 1.8 copy-start.1
  137.3 1.0 copy-start.6
  141.6 32.4 %all-to-all-start.3 = ((bf16[64,48,128]{2,1,0:T(8,128)(2,1)}), bf16[64,48,128]{2,1,0:T(8,128)(2,1)S(1)}, u32[]{:S(2)}, u32[]{:S(2)}) async-start(bf16[64,48,128]{2,1,0:T(8,128)(2,1)} %reshape.126), calls=%async_computation.3 | async-start | bytes 1572864 | tf_op jit(solution)/shard_map/all_to_all | solution.py:128
  152.1 2.6 copy-start.4
  154.7 7.9 %copy-start.2 = (bf16[8,704,256]{2,1,0:T(8,128)(2,1)S(1)}, bf16[8,704,256]{2,1,0:T(8,128)(2,1)}, u32[]{:S(2)}) copy-start(bf16[8,704,256]{2,1,0:T(8,128)(2,1)} %all-gather.5.cloned.1.call-done.w_ref) | copy-start | bytes 8650756
  174.0 0.9 copy-start.11
  174.0 8.4 %copy-start.17 = (bf16[16,32,128]{2,1,0:T(8,128)(2,1)S(1)}, bf16[16,32,128]{2,1,0:T(8,128)(2,1)}, u32[]{:S(2)}) copy-start(bf16[16,32,128]{2,1,0:T(8,128)(2,1)} %param.16) | copy-start | bytes 393220
  174.0 9.7 %copy-start.21 = (f32[180,2]{0,1:T(2,128)S(1)}, f32[180,2]{0,1:T(2,128)}, u32[]{:S(2)}) copy-start(f32[180,2]{0,1:T(2,128)} %param.11) | copy-start | bytes 4324
  174.9 56.2 %all-to-all-start.1 = ((bf16[64,8,2048]{2,1,0:T(8,128)(2,1)}), bf16[64,8,2048]{2,1,0:T(8,128)(2,1)S(1)}, u32[]{:S(2)}, u32[]{:S(2)}) async-start(bf16[64,8,2048]{2,1,0:T(8,128)(2,1)} %bitcast.9), calls=%async_computation.1 | async-start | bytes 4194304 | tf_op jit(solution)/shard_map/all_to_all | solution.py:128
  182.2 54.9 %all-gather.7.cloned.1.call-start = ((), (), s32[]{:S(2)}) async-start(), calls=%async_computation.9 | async-start | bytes 1179648 | tf_op jit(solution)/shard_map/all_gather | solution.py:160
  231.1 1.7 copy-start.8
  231.1 1.7 copy-start.10
  232.8 1.4 copy-start.9
  232.8 1.4 copy-start.15
  234.6 0.9 copy-start.13
  278.8 2.1 copy-start.14
  278.8 2.1 copy-start.16
  278.8 2.1 copy-start.18
  280.8 27.3 %copy-start.20 = (f32[2,128]{1,0:T(2,128)S(1)}, f32[2,128]{1,0:T(2,128)}, u32[]{:S(2)}) copy-start(f32[2,128]{1,0:T(2,128)} %reduce_sum.134) | copy-start | bytes 3076
  304.8 13.4 %all-to-all-start.7 = ((f32[8,32,128]{2,1,0:T(8,128)}), f32[8,32,128]{2,1,0:T(8,128)S(1)}, u32[]{:S(2)}, u32[]{:S(2)}) async-start(f32[8,32,128]{2,1,0:T(8,128)} %broadcast_in_dim.77), calls=%async_computation.7 | async-start | bytes 262144 | tf_op jit(solution)/shard_map/all_to_all | solution.py:178
Sparse Core Ops, SparseCore 0:
  10.7 77.5 all-gather.8
  90.4 45.0 all-gather.4
  185.1 40.0 all-gather.6

commit v2 on v0

v2 whole, which is shorter than its diff:
```python
import jax
import jax.numpy as jnp
from jax import lax
from jax.experimental import pallas as pl
from jax.experimental.pallas import tpu as pltpu
from jax.sharding import PartitionSpec as P

HEAD = 8
LANES = 128

soft_temp = 0.05
logit_gain = 1.5
norm_eps = 1e-06
F32 = jnp.float32
BF16 = jnp.bfloat16
NT = (((1,), (1,)), ((), ()))
VMEM = pl.BlockSpec(memory_space=pltpu.VMEM)
HBM = pl.BlockSpec(memory_space=pl.ANY)
SMEM = pl.BlockSpec(memory_space=pltpu.SMEM)
PARAMS = pltpu.CompilerParams(vmem_limit_bytes=56 * 2**20)


def kernel_call(kernel, outs, ins, args, scratch=(), flops=0, moved=0):
    return pl.pallas_call(
        kernel,
        in_specs=ins,
        out_specs=[VMEM] * len(outs),
        out_shape=[jax.ShapeDtypeStruct(*o) for o in outs],
        scratch_shapes=scratch,
        compiler_params=PARAMS,
        cost_estimate=pl.CostEstimate(flops=flops, bytes_accessed=moved, transcendentals=0),
    )(*args)


def lane_block(c):
    return slice(c * LANES, (c + 1) * LANES)


def put_head(out_ref, c, values):
    out_ref[:, c, :, :] = values.reshape(-1, HEAD, LANES).astype(BF16)


def get_head(in_ref, c):
    return in_ref[:, c, :, :].astype(F32).reshape(-1, LANES).astype(BF16)


def put_tail(fold_ref, c, values):
    rows = values.shape[0]
    fold_ref[pl.ds((c // 8) * rows * 8 + c % 8, rows, stride=8), :] = values


def get_tail(fold_ref, c, rows):
    return fold_ref[pl.ds((c // 8) * rows * 8 + c % 8, rows, stride=8), :].astype(BF16)


def store_tail(out_ref, fold_ref, blocks, tail):
    experts = out_ref.shape[0]
    span = experts * tail * 8
    for group in range(blocks // 8):
        first = blocks + group * tail
        out_ref[:, first : first + tail, :, :] = (
            fold_ref[group * span : (group + 1) * span, :].reshape(experts, tail, 8, LANES).astype(BF16)
        )


def load_tail(in_ref, fold_ref, blocks, tail):
    experts = in_ref.shape[0]
    span = experts * tail * 8
    for group in range(blocks // 8):
        first = blocks + group * tail
        fold_ref[group * span : (group + 1) * span, :] = (
            in_ref[:, first : first + tail, :, :].astype(F32).reshape(span, LANES)
        )


def pack_kernel(tail, routes_ref, x_ref, out_ref, fold_ref):
    experts = out_ref.shape[0]
    tokens, width = x_ref.shape
    blocks = width // LANES
    routes = routes_ref[...]
    expert_id = lax.broadcasted_iota(jnp.int32, (experts, tokens), 0)
    earlier = lax.broadcasted_iota(jnp.int32, (tokens, tokens), 0) < lax.broadcasted_iota(
        jnp.int32, (tokens, tokens), 1
    )
    earlier = earlier.astype(F32).astype(BF16)
    seen = jnp.zeros((experts, 1), F32)
    picks = []
    for k in range(routes.shape[0]):
        route = routes[k : k + 1, :]
        hit = (expert_id == route).astype(F32)
        ahead = jnp.dot(hit.astype(BF16), earlier, preferred_element_type=F32) + seen
        rank = jnp.sum(hit * ahead, axis=0, keepdims=True).astype(jnp.int32)
        seen = seen + jnp.sum(hit, axis=1, keepdims=True)
        picks.append((route, rank))
    head_row = lax.broadcasted_iota(jnp.int32, (experts * HEAD, tokens), 0)
    tail_row = lax.broadcasted_iota(jnp.int32, (experts * tail, tokens), 0)
    head_pick = jnp.zeros(head_row.shape, F32)
    tail_pick = jnp.zeros(tail_row.shape, F32)
    for route, rank in picks:
        head_place = jnp.where(rank < HEAD, route * HEAD + rank, -1)
        tail_place = jnp.where(rank >= HEAD, route * tail + rank - HEAD, -1)
        head_pick = head_pick + (head_row == head_place).astype(F32)
        tail_pick = tail_pick + (tail_row == tail_place).astype(F32)
    head_pick = head_pick.astype(BF16)
    tail_pick = tail_pick.astype(BF16)
    for c in range(0, blocks, 2):
        columns = x_ref[:, c * LANES : (c + 2) * LANES]
        rows = jnp.dot(head_pick, columns, preferred_element_type=F32)
        put_head(out_ref, c, rows[:, :LANES])
        put_head(out_ref, c + 1, rows[:, LANES:])
        rows = jnp.dot(tail_pick, columns, preferred_element_type=F32)
        put_tail(fold_ref, c, rows[:, :LANES])
        put_tail(fold_ref, c + 1, rows[:, LANES:])
    store_tail(out_ref, fold_ref, blocks, tail)


def pack(routes_t, x, experts, tail):
    blocks = x.shape[1] // LANES
    tiles = blocks + blocks // 8 * tail
    (out,) = kernel_call(
        lambda *refs: pack_kernel(tail, *refs),
        [((experts, tiles, 8, LANES), BF16)],
        [VMEM, VMEM],
        (routes_t, x),
        [pltpu.VMEM((blocks * experts * tail, LANES), F32)],
    )
    return out


def down_half(tail, hidden, wd_ref, out_ref, fold_ref):
    experts = out_ref.shape[0]
    pairs = wd_ref.shape[0]
    for p in range(pairs):
        rows = jnp.dot(hidden, wd_ref[p], preferred_element_type=F32)
        for j in range(2):
            c = 2 * p + j
            put_head(out_ref, c, rows[: experts * HEAD, lane_block(j)])
            put_tail(fold_ref, c, rows[experts * HEAD :, lane_block(j)])
    store_tail(out_ref, fold_ref, 2 * pairs, tail)


def down_copies(w_ref, base, wd_ref, sems):
    reps = w_ref.shape[0]
    half = wd_ref.shape[1] // 2
    return [
        pltpu.make_async_copy(
            w_ref.at[r, pl.ds(base, half), pl.ds(j * LANES, LANES)],
            wd_ref.at[r // 2, pl.ds(j * half, half), pl.ds((r % 2) * LANES, LANES)],
            sems.at[2 * r + j],
        )
        for r in range(reps)
        for j in range(2)
    ]


def expert_kernel(tail, in_ref, w_ref, hid_ref, out_ref, rows_ref, wv_ref, wd_ref, fold_ref, back_ref, sems, down_sems):
    reps, wide, depth = wv_ref.shape
    ff = wide // 2
    experts = in_ref.shape[0]
    blocks = rows_ref.shape[1] // LANES
    first = experts * HEAD
    count = rows_ref.shape[0]
    copies = [
        pltpu.make_async_copy(w_ref.at[r, pl.ds(0, wide)], wv_ref.at[r], sems.at[r]) for r in range(reps)
    ]
    downs = down_copies(w_ref, wide, wd_ref, down_sems)
    for copy in copies + downs:
        copy.start()
    load_tail(in_ref, fold_ref, blocks, tail)
    for c in range(blocks):
        rows_ref[:first, lane_block(c)] = get_head(in_ref, c)
        rows_ref[first:, lane_block(c)] = get_tail(fold_ref, c, count - first)
    step = count // 2
    for i in range(2):
        part = slice(i * step, (i + 1) * step)
        gate = up = None
        for r in range(reps):
            if i == 0:
                copies[r].wait()
            rows = rows_ref[part, r * depth : (r + 1) * depth]
            g = lax.dot_general(rows, wv_ref[r, :ff, :], NT, preferred_element_type=F32)
            u = lax.dot_general(rows, wv_ref[r, ff:, :], NT, preferred_element_type=F32)
            gate = g if gate is None else gate + g
            up = u if up is None else up + u
        hid_ref[part, :] = (gate / (1.0 + jnp.exp(-gate)) * up).astype(BF16)
    for copy in downs:
        copy.wait()
    down_half(tail, hid_ref[...], wd_ref, out_ref, back_ref)


def second_kernel(tail, hid_ref, w_ref, out_ref, wd_ref, back_ref, down_sems):
    downs = down_copies(w_ref, 0, wd_ref, down_sems)
    for copy in downs:
        copy.start()
    for copy in downs:
        copy.wait()
    down_half(tail, hid_ref[...], wd_ref, out_ref, back_ref)


def mix_half(half, back_ref, high_ref, low_ref, x_ref, proj_ref, fold_ref, tail, store):
    experts = back_ref.shape[0]
    blocks = x_ref.shape[1] // (2 * LANES)
    first = experts * HEAD
    load_tail(back_ref, fold_ref, blocks, tail)
    projected = None
    for p in range(blocks // 2):
        cs = (2 * p, 2 * p + 1)
        head = jnp.concatenate([get_head(back_ref, c) for c in cs], axis=1)
        rest = jnp.concatenate([get_tail(fold_ref, c, experts * tail) for c in cs], axis=1)
        added = (
            jnp.dot(high_ref[:, :first], head, preferred_element_type=F32)
            + jnp.dot(low_ref[:, :first], head, preferred_element_type=F32)
            + jnp.dot(high_ref[:, first:], rest, preferred_element_type=F32)
            + jnp.dot(low_ref[:, first:], rest, preferred_element_type=F32)
        )
        states = []
        projs = []
        for j, c in enumerate(cs):
            columns = lane_block(2 * c + half)
            value = (x_ref[:, columns].astype(F32) + added[:, lane_block(j)]).astype(BF16)
            store(c, value)
            states.append(value)
            projs.append(proj_ref[columns, :])
        part = jnp.dot(
            jnp.concatenate(states, axis=1), jnp.concatenate(projs, axis=0), preferred_element_type=F32
        )
        projected = part if projected is None else projected + part
    return projected


def mix_kernel(tail, back_ref, high_ref, low_ref, x_ref, proj_ref, half_ref, sum_ref, fold_ref):
    def store(c, value):
        half_ref[:, lane_block(c)] = value

    sum_ref[...] = mix_half(0, back_ref, high_ref, low_ref, x_ref, proj_ref, fold_ref, tail, store)


def score_kernel(
    tail, gain, owner_ref, back_ref, high_ref, low_ref, x_ref, proj_ref, half_ref, sum_ref, query_ref, positive_ref,
    states_ref, weights_ref, unit_ref, radius_ref, totals_ref, logits_ref, shares_ref, fold_ref,
):
    def store(c, value):
        states_ref[:, lane_block(2 * c)] = half_ref[:, lane_block(c)]
        states_ref[:, lane_block(2 * c + 1)] = value

    projected = sum_ref[...] + mix_half(
        1, back_ref, high_ref, low_ref, x_ref, proj_ref, fold_ref, tail, store
    )
    radius = jnp.sqrt(jnp.sum(projected * projected, axis=1, keepdims=True) + norm_eps)
    unit = projected / radius
    unit_ref[...] = unit
    radius_ref[...] = jnp.broadcast_to(radius, radius_ref.shape)
    unit_vec = unit.astype(BF16)
    step = 4 * LANES
    logits = jnp.zeros((1, LANES), F32)
    for n in range(0, query_ref.shape[0], step):
        scores = lax.dot_general(unit_vec, query_ref[n : n + step, :], NT, preferred_element_type=F32)
        weights = jnp.exp(scores / soft_temp)
        weights_ref[:, n : n + step] = weights
        totals = jnp.sum(weights, axis=0, keepdims=True)
        totals_ref[:, n : n + step] = totals
        logs = soft_temp * jnp.log(totals)
        for j in range(step // LANES):
            logits = logits + logs[:, lane_block(j)]
    logits = gain * logits
    logits_ref[...] = logits
    held = jnp.where(positive_ref[...] == owner_ref[0, 0], logits, 0.0)
    odd = lax.broadcasted_iota(jnp.int32, shares_ref.shape, 0) % 2
    shares_ref[...] = jnp.where(odd == 0, jnp.exp(logits), held)


def grad_kernel(
    gain, owner_ref, sums_ref, logits_ref, positive_ref, weights_ref, totals_ref, query_ref, unit_ref, radius_ref,
    states_ref, share_ref, loss_ref,
):
    senders = sums_ref.shape[0] // 2
    partition = jnp.sum(sums_ref[pl.ds(0, senders, stride=2), :], axis=0, keepdims=True)
    held = jnp.sum(sums_ref[pl.ds(1, senders, stride=2), :], axis=0, keepdims=True)
    loss = jnp.sum(jnp.log(partition) - held, axis=1, keepdims=True) / partition.shape[1]
    loss_ref[...] = jnp.broadcast_to(loss, loss_ref.shape)
    positive = (positive_ref[...] == owner_ref[0, 0]).astype(F32)
    factor = gain * (jnp.exp(logits_ref[...]) / partition - positive)
    step = 4 * LANES
    grad = None
    for n in range(0, query_ref.shape[0], step):
        scale = jnp.concatenate([factor] * (step // LANES), axis=1) / totals_ref[:, n : n + step]
        coeffs = (weights_ref[:, n : n + step] * scale).astype(BF16)
        part = jnp.dot(coeffs, query_ref[n : n + step, :], preferred_element_type=F32)
        grad = part if grad is None else grad + part
    unit = unit_ref[...]
    along = jnp.sum(unit * grad, axis=1, keepdims=True)
    grad_vec = ((grad - unit * along) / radius_ref[...]).astype(BF16)
    share_ref[...] = lax.dot_general(
        states_ref[...], grad_vec, (((0,), (0,)), ((), ())), preferred_element_type=F32
    ).astype(BF16)


def body(
    passages_in,
    routes,
    route_weights,
    gate_weight,
    up_weight,
    down_weight,
    projection,
    queries,
    positives,
):
    tok_count, model_width = passages_in.shape
    top_count = routes.shape[1]
    experts = lax.axis_size("exp")
    rep_count = lax.axis_size("rep")
    ff = gate_weight.shape[2]
    capacity = max(2, 2 * tok_count * top_count // experts)
    tail = capacity - HEAD
    slots = experts * capacity
    blocks = model_width // LANES
    fold = experts * tail * 8

    down = down_weight[0]
    down_halves = [
        jnp.concatenate([down[: ff // 2, lane_block(h)], down[ff // 2 :, lane_block(h)]], axis=1) for h in range(2)
    ]
    first_part = jnp.concatenate([gate_weight[0].T, up_weight[0].T, down_halves[0]], axis=0)
    first_all = lax.all_gather(first_part, "rep", axis=0, tiled=False)
    second_all = lax.all_gather(down_halves[1], "rep", axis=0, tiled=False)

    def exchange(tiles):
        return lax.all_to_all(tiles, "exp", split_axis=0, concat_axis=0, tiled=True)

    packed = pack(routes.T, passages_in, experts, tail)
    arrived = exchange(packed)

    half_tiles = ((experts, blocks // 2 + blocks // 16 * tail, 8, LANES), BF16)
    hidden, send_a = kernel_call(
        lambda *refs: expert_kernel(tail, *refs),
        [((slots, ff), BF16), half_tiles],
        [VMEM, HBM],
        (arrived, first_all),
        [
            pltpu.VMEM((slots, model_width), BF16),
            pltpu.VMEM((rep_count, 2 * ff, model_width // rep_count), BF16),
            pltpu.VMEM((rep_count // 2, ff, 2 * LANES), BF16),
            pltpu.VMEM((2 * fold, LANES), F32),
            pltpu.VMEM((fold, LANES), F32),
            pltpu.SemaphoreType.DMA((rep_count,)),
            pltpu.SemaphoreType.DMA((2 * rep_count,)),
        ],
    )
    back_a = exchange(send_a)
    (send_b,) = kernel_call(
        lambda *refs: second_kernel(tail, *refs),
        [half_tiles],
        [VMEM, HBM],
        (hidden, second_all),
        [
            pltpu.VMEM((rep_count // 2, ff, 2 * LANES), BF16),
            pltpu.VMEM((fold, LANES), F32),
            pltpu.SemaphoreType.DMA((2 * rep_count,)),
        ],
    )
    back_b = exchange(send_b)

    later_routes, _ = lax.optimization_barrier((routes, packed))
    flat = later_routes.T.reshape(-1)
    count = flat.shape[0]
    onehot = flat[:, None] == jnp.arange(experts, dtype=jnp.int32)[None, :]
    before = jnp.arange(count)[:, None] > jnp.arange(count)[None, :]
    earlier = jnp.dot(before.astype(BF16), onehot.astype(BF16), preferred_element_type=F32)
    rank = jnp.sum(jnp.where(onehot, earlier, 0.0), axis=1).astype(jnp.int32)
    place = jnp.where(rank < HEAD, flat * HEAD + rank, experts * HEAD + flat * tail + rank - HEAD)
    place = place.reshape(top_count, tok_count)
    hit = place[:, :, None] == jnp.arange(slots, dtype=jnp.int32)[None, None, :]
    mix = jnp.sum(jnp.where(hit, route_weights.T[:, :, None], 0.0), axis=0)
    high = mix.astype(BF16)
    low = (mix - high.astype(F32)).astype(BF16)

    wide_queries = queries.astype(F32)
    query_radius = jnp.sqrt(jnp.sum(wide_queries * wide_queries, axis=-1, keepdims=True) + norm_eps)
    query_unit = (wide_queries / query_radius).astype(BF16)
    query_block, query_len, unit_width = queries.shape
    total_queries = query_block * rep_count
    all_queries = lax.all_gather(query_unit.transpose(1, 0, 2), "rep", axis=0, tiled=False)
    query_rows = all_queries.transpose(1, 0, 2, 3).reshape(query_len * total_queries, unit_width)

    owner = lax.axis_index(("exp", "rep")).astype(jnp.int32).reshape(1, 1)
    positive_row = positives.reshape(1, total_queries)

    states_a, sum_a = kernel_call(
        lambda *refs: mix_kernel(tail, *refs),
        [((tok_count, model_width // 2), BF16), ((tok_count, unit_width), F32)],
        [VMEM] * 5,
        (back_a, high, low, passages_in, projection),
        [pltpu.VMEM((fold, LANES), F32)],
    )
    devices = experts * rep_count
    columns = query_len * total_queries
    states, weights, unit, radius, totals, logits, shares = kernel_call(
        lambda *refs: score_kernel(tail, logit_gain, *refs),
        [
            ((tok_count, model_width), BF16),
            ((tok_count, columns), F32),
            ((tok_count, unit_width), F32),
            ((tok_count, unit_width), F32),
            ((1, columns), F32),
            ((1, total_queries), F32),
            ((2 * devices, total_queries), F32),
        ],
        [SMEM] + [VMEM] * 9,
        (owner, back_b, high, low, passages_in, projection, states_a, sum_a, query_rows, positive_row),
        [pltpu.VMEM((fold, LANES), F32)],
    )
    sums = lax.all_to_all(
        shares.reshape(devices, 2, total_queries), ("exp", "rep"), split_axis=0, concat_axis=0, tiled=True
    ).reshape(2 * devices, total_queries)
    share, loss = kernel_call(
        lambda *refs: grad_kernel(logit_gain, *refs),
        [((model_width, unit_width), BF16), ((1, LANES), F32)],
        [SMEM] + [VMEM] * 9,
        (owner, sums, logits, positive_row, weights, totals, query_rows, unit, radius, states),
    )
    rows_out = model_width // experts
    parts = exchange(share.reshape(experts, rows_out, unit_width))
    part_sum = jnp.sum(parts.astype(F32), axis=0)
    sent = jnp.broadcast_to(part_sum[None], (rep_count,) + part_sum.shape)
    grad_projection = jnp.sum(lax.all_to_all(sent, "rep", split_axis=0, concat_axis=0, tiled=True), axis=0)
    return (states, grad_projection, loss[0, 0])


def solution(mesh):
    in_specs = (
        P(("exp", "rep"), None),
        P(("exp", "rep"), None),
        P(("exp", "rep"), None),
        P("exp", "rep", None),
        P("exp", "rep", None),
        P("exp", None, "rep"),
        P(),
        P("rep", None, None),
        P(),
    )
    out_specs = (P(("exp", "rep"), None), P("exp", None), P())
    return jax.shard_map(body, mesh=mesh, in_specs=in_specs, out_specs=out_specs, check_vma=False)
```

time: 606 us -> 327 us (0.54)
  waiting for transfers between devices: 372 us -> 92.1 us
  Pallas kernels: 0 us -> 36.1 us
  local copies, waits for them, and re-layouts: 31.4 us -> 5.49 us
  matrix products: 24.3 us -> 0.22 us
  blocking collectives: 128 us -> 150 us
    all_to_all x2, waiting for transfers between devices: 185 us -> 0.01 us  [exchange(): return lax.all_to_all(tiles, 'exp', split_axis=0, concat_axis=0, tiled=True)]
    all_to_all x0 -> x4, blocking collectives: none -> 150 us  [the longest x2 101 us: exchange(): return lax.all_to_all(tiles, 'exp', split_axis=0, concat_axis=0, tiled=True)]
    reduce_scatter x1 -> x0, waiting for transfers between devices: 140 us -> none  [body(): lax.psum_scatter(lax.dot_general(states, grad_vec, (((0,), (0,)), ((), ()...]
    psum x2 -> x0, blocking collectives: 128 us -> none  [the longest x1 96.4 us: body(): lax.psum((jnp.sum(exp_logits, axis=0), jnp.sum(jnp.where(positive_hit, lo...]
    all_gather x4 -> x3, waiting for transfers between devices: 45 us -> 92.1 us  [the longest x1 43.9 us: body(): second_all = lax.all_gather(down_halves[1], 'rep', axis=0, tiled=False)]
    pallas_call x0 -> x6, Pallas kernels: none -> 36.1 us  [kernel_call(): pl.pallas_call(kernel, in_specs=ins, out_specs=[VMEM] * len(outs), out_sh...]
    dot_general x6 -> x1, matrix products: 24.3 us -> 0.22 us  [body(): jnp.dot(before.astype(BF16), onehot.astype(BF16), preferred_element_type=...]
    reshape x4 -> x0, local copies, waits for them, and re-layouts: 14.4 us -> none  [the longest x1 4.76 us: body(): expert_out.reshape(experts, capacity, model_width)]
  transfers between devices with their start and end apart: 7 -> 5, of which waited for: 4 -> 3; matrix products, arithmetic and copies ran while one was open for 7% -> 2% of each run, Pallas kernels for 0% -> 4%
where the time goes in v2:
time: 327 us; the launch traced here: 326 us
  blocking collectives  150 us (46%)
  waiting for transfers between devices  92.1 us (28%)
  Pallas kernels  36.1 us (11%)
  starting transfers between devices  21.4 us (7%)
  between operations  13.9 us (4%)
  other arithmetic  7.05 us (2%)
  local copies, waits for them, and re-layouts  5.49 us (2%)
    all_to_all x2, blocking collectives, exchange(): return lax.all_to_all(tiles, 'exp', split_axis=0, concat_axis=0, tiled=True)  101 us
    all_gather x1, waiting for transfers between devices, body(): second_all = lax.all_gather(down_halves[1], 'rep', axis=0, tiled=False)  43.9 us
    all_gather x1, waiting for transfers between devices, body(): lax.all_gather(query_unit.transpose(1, 0, 2), 'rep', axis=0, tiled=False)  39 us
    pallas_call x6, Pallas kernels, kernel_call(): pl.pallas_call(kernel, in_specs=ins, out_specs=[VMEM] * len(outs), out_sh...  36.1 us
    all_to_all x1, blocking collectives, body(): lax.all_to_all(shares.reshape(devices, 2, total_queries), ('exp', 'rep'),...  35.6 us
    all_to_all x2, starting transfers between devices, exchange(): return lax.all_to_all(tiles, 'exp', split_axis=0, concat_axis=0, tiled=True)  21.1 us
    all_to_all x1, blocking collectives, body(): lax.all_to_all(sent, 'rep', split_axis=0, concat_axis=0, tiled=True)  12.7 us
    all_gather x1, waiting for transfers between devices, body(): first_all = lax.all_gather(first_part, 'rep', axis=0, tiled=False)  9.2 us
  transfers between devices with their start and end apart: 5, of which 3 were waited for; matrix products, arithmetic and copies ran while one was open for 2% of the time, Pallas kernels for 4%

profile of v2, /device:TPU:6, one launch (start us, length us, event | category | flops | bytes accessed | tf_op | source)
XLA Modules:
  0.0 326.1 jit_solution(14160683543110132403)
XLA Ops:
  7.2 1.0 fusion.6
  8.3 2.1 maximum_maximum_fusion
  10.4 3.9 %shard_map.112 = bf16[64,22,8,128]{3,2,1,0:T(8,128)(2,1)} custom-call(s32[2,180]{1,0:T(2,128)} %bitcast.37, bf16[180,2048]{1,0:T(8,128)(2,1)} %refs_4_.3), custom_call_target="tpu_custom_call" | custom-call | tf_op jit(solution)/shard_map/pallas_call | solution.py:24
  14.4 78.1 %all_to_all.30.refs_0_ = bf16[64,22,8,128]{3,2,1,0:T(8,128)(2,1)} all-to-all(bf16[64,22,8,128]{3,2,1,0:T(8,128)(2,1)} %shard_map.112), channel_id=1, replica_groups=mesh['exp'=64,'rep'=8] {'exp'}, dimensions={0} | all-to-all | bytes 5767168 | tf_op jit(solution)/shard_map/all_to_all | solution.py:329
  92.5 9.2 %all-gather.7.cloned.1.call-done = bf16[14080,256]{1,0:T(8,128)(2,1)} async-done(((bf16[1760,256]{1,0:T(8,128)(2,1)}), bf16[14080,256]{1,0:T(8,128)(2,1)}) %all-gather.7.cloned.1.call-update) | async-done | bytes 7208976 | tf_op jit(solution)/shard_map/all_gather | solution.py:325
  101.7 11.8 %shard_map.113 = (bf16[704,704]{1,0:T(8,128)(2,1)}, bf16[64,11,8,128]{3,2,1,0:T(8,128)(2,1)}) custom-call(bf16[64,22,8,128]{3,2,1,0:T(8,128)(2,1)} %all_to_all.30.refs_0_, bf16[8,1760,256]{2,1,0:T(8,128)(2,1)} %bitcast.28), custom_call_target="tpu_custom_call" | custom-call | tf_op jit(solution)/shard_map/pallas_call | solution.py:24
  113.5 10.5 %all-to-all-start.2 = ((bf16[64,11,8,128]{3,2,1,0:T(8,128)(2,1)}), bf16[64,11,8,128]{3,2,1,0:T(8,128)(2,1)S(1)}, u32[]{:S(2)}, u32[]{:S(2)}) async-start(bf16[64,11,8,128]{3,2,1,0:T(8,128)(2,1)} %get-tuple-element.19), calls=%async_computation.2 | async-start | bytes 2883584 | tf_op jit(solution)/shard_map/all_to_all | solution.py:329
  124.1 0.7 pad_maximum_fusion
  124.8 43.9 %all-gather.9.cloned.1.call-done = bf16[2816,256]{1,0:T(8,128)(2,1)} async-done(((bf16[352,256]{1,0:T(8,128)(2,1)}), bf16[2816,256]{1,0:T(8,128)(2,1)}) %all-gather.9.cloned.1.call-update) | async-done | bytes 1441808 | tf_op jit(solution)/shard_map/all_gather | solution.py:326
  168.6 5.2 %shard_map.114 = bf16[64,11,8,128]{3,2,1,0:T(8,128)(2,1)} custom-call(bf16[704,704]{1,0:T(8,128)(2,1)} %get-tuple-element.17.refs_0_, bf16[8,352,256]{2,1,0:T(8,128)(2,1)} %bitcast.30), custom_call_target="tpu_custom_call" | custom-call | tf_op jit(solution)/shard_map/pallas_call | solution.py:24
  173.9 10.6 %all-to-all-start.1 = ((bf16[64,11,8,128]{3,2,1,0:T(8,128)(2,1)}), bf16[64,11,8,128]{3,2,1,0:T(8,128)(2,1)S(1)}, u32[]{:S(2)}, u32[]{:S(2)}) async-start(bf16[64,11,8,128]{3,2,1,0:T(8,128)(2,1)} %shard_map.114), calls=%async_computation.1 | async-start | bytes 2883584 | tf_op jit(solution)/shard_map/all_to_all | solution.py:329
  184.5 0.2 all-gather.11.cloned.1.call-start
  184.8 0.1 fusion.2
  184.9 0.8 fusion.4
  185.8 0.1 copy.14
  185.9 0.1 eq.28
  186.0 0.2 fusion
  186.2 0.1 convert_element_type.29
  186.3 0.1 copy.13
  186.5 1.7 fusion.1
  188.2 0.9 subtract_convert_fusion
  189.0 39.0 %all-gather.11.cloned.1.call-done = bf16[256,16,128]{2,0,1:T(8,128)(2,1)} async-done(((bf16[32,16,128]{2,0,1:T(8,128)(2,1)}), bf16[256,16,128]{2,0,1:T(8,128)(2,1)}) %all-gather.11.cloned.1.call-update) | async-done | bytes 1048592 | tf_op jit(solution)/shard_map/all_gather | solution.py:383
  228.0 2.9 copy.15
  230.9 4.0 %shard_map.115 = (bf16[180,1024]{1,0:T(8,128)(2,1)}, f32[180,128]{1,0:T(8,128)}) custom-call(bf16[64,11,8,128]{3,2,1,0:T(8,128)(2,1)} %copy-done, bf16[180,704]{1,0:T(8,128)(2,1)} %get-tuple-element.32.refs_1_.refs_2_, bf16[180,704]{1,0:T(8,128)(2,1)} %get-tuple-element.31.refs_2_.refs_3_, bf16[180,2048]{1,0:T(8,128)(2,1)} %refs_4_.3, bf16[2048,128]{1,0:T(8,128)(2,1)} %refs_5_.1), custom_call_target="tpu_custom_call" | custom-call | tf_op jit(solution)/shard_map/pallas_call | solution.py:24
  235.0 1.1 copy-done.1
  236.1 6.6 %shard_map.116 = (bf16[180,2048]{1,0:T(8,128)(2,1)}, f32[180,4096]{1,0:T(8,128)}, f32[180,128]{1,0:T(8,128)}, f32[180,128]{1,0:T(8,128)}, f32[1,4096]{1,0:T(1,12...) custom-call(s32[1,1]{1,0:T(1,128)} %bitcast.refs_0_, bf16[64,11,8,128]{3,2,1,0:T(8,128)(2,1)} %copy-done.1, ...), custom_call_target="tpu_custom_call" | custom-call | tf_op jit(solution)/shard_map/pallas_call | solution.py:24
  242.6 35.6 %all_to_all.31 = f32[512,2,128]{2,1,0:T(2,128)} all-to-all(f32[512,2,128]{2,1,0:T(2,128)} %bitcast.32), channel_id=1, replica_groups=mesh['exp'=64,'rep'=8] {'exp','rep'}, dimensions={0} | all-to-all | bytes 1048576 | tf_op jit(solution)/shard_map/all_to_all | solution.py:413
  278.3 4.6 %shard_map.117 = (bf16[2048,128]{1,0:T(8,128)(2,1)}, f32[1,128]{1,0:T(1,128)}) custom-call(s32[1,1]{1,0:T(1,128)} %bitcast.refs_0_, f32[1024,128]{1,0:T(8,128)} %bitcast.29, f32[1,128]{1,0:T(1,128)} %get-tuple-element.24.refs_2_, s32[1,128]{1,0:T(1,128)} %bitcast.40, f32[180,4096]{1,0:T(8,128)} %get-tuple-element.25.refs_4_, ...), custom_call_target="tpu_custom_call" | custom-call | tf_op jit(solution)/shard_map/pallas_call | solution.py:24
  282.8 23.2 %all_to_all.32 = bf16[64,32,128]{2,1,0:T(8,128)(2,1)S(1)} all-to-all(bf16[64,32,128]{2,1,0:T(8,128)(2,1)} %bitcast.33), channel_id=1, replica_groups=mesh['exp'=64,'rep'=8] {'exp'}, dimensions={0} | all-to-all | bytes 1048576 | tf_op jit(solution)/shard_map/all_to_all | solution.py:329
  306.1 0.1 convert_reduce_fusion
  306.2 12.7 %all_to_all.33 = f32[8,32,128]{2,1,0:T(8,128)S(1)} all-to-all(f32[8,32,128]{2,1,0:T(8,128)S(1)} %broadcast_in_dim.31), channel_id=1, replica_groups=mesh['exp'=64,'rep'=8] {'rep'}, dimensions={0} | all-to-all | bytes 262144 | tf_op jit(solution)/shard_map/all_to_all | solution.py:426
  318.9 0.6 reduce_sum.49
  (20 shorter events, 0.2 us)
Async XLA Ops:
  7.2 94.5 %all-gather.7.cloned.1.call-start = ((), (), s32[]{:S(2)}) async-start(), calls=%async_computation.6 | async-start | bytes 8110080 | tf_op jit(solution)/shard_map/all_gather | solution.py:325
  113.5 60.4 %all-to-all-start.2 = ((bf16[64,11,8,128]{3,2,1,0:T(8,128)(2,1)}), bf16[64,11,8,128]{3,2,1,0:T(8,128)(2,1)S(1)}, u32[]{:S(2)}, u32[]{:S(2)}) async-start(bf16[64,11,8,128]{3,2,1,0:T(8,128)(2,1)} %get-tuple-element.19), calls=%async_computation.2 | async-start | bytes 2883584 | tf_op jit(solution)/shard_map/all_to_all | solution.py:329
  124.0 44.6 %all-gather.9.cloned.1.call-start = ((), (), s32[]{:S(2)}) async-start(), calls=%async_computation.7 | async-start | bytes 1622016 | tf_op jit(solution)/shard_map/all_gather | solution.py:326
  173.9 10.9 %copy-start.2 = (bf16[16,32,128]{2,1,0:T(8,128)(2,1)S(1)}, bf16[16,32,128]{2,1,0:T(8,128)(2,1)}, u32[]{:S(2)}) copy-start(bf16[16,32,128]{2,1,0:T(8,128)(2,1)} %param.16) | copy-start | bytes 393220
  173.9 11.9 %copy-start.4 = (f32[180,2]{0,1:T(2,128)S(1)}, f32[180,2]{0,1:T(2,128)}, u32[]{:S(2)}) copy-start(f32[180,2]{0,1:T(2,128)} %param.11) | copy-start | bytes 4324
  173.9 12.0 %copy-start.3 = (s32[180,2]{0,1:T(2,128)S(1)}, s32[180,2]{0,1:T(2,128)}, u32[]{:S(2)}) copy-start(s32[180,2]{0,1:T(2,128)} %param.10) | copy-start | bytes 4324
  173.9 12.3 %copy-start = (bf16[64,11,8,128]{3,2,1,0:T(8,128)(2,1)}, bf16[64,11,8,128]{3,2,1,0:T(8,128)(2,1)S(1)}, u32[]{:S(2)}) copy-start(bf16[64,11,8,128]{3,2,1,0:T(8,128)(2,1)S(1)} %all-to-all-done.2.refs_0_) | copy-start | bytes 4325380
  173.9 61.0 %all-to-all-start.1 = ((bf16[64,11,8,128]{3,2,1,0:T(8,128)(2,1)}), bf16[64,11,8,128]{3,2,1,0:T(8,128)(2,1)S(1)}, u32[]{:S(2)}, u32[]{:S(2)}) async-start(bf16[64,11,8,128]{3,2,1,0:T(8,128)(2,1)} %shard_map.114), calls=%async_computation.1 | async-start | bytes 2883584 | tf_op jit(solution)/shard_map/all_to_all | solution.py:329
  184.5 43.5 %all-gather.11.cloned.1.call-start = ((), (), s32[]{:S(2)}) async-start(), calls=%async_computation.8 | async-start | bytes 1179648 | tf_op jit(solution)/shard_map/all_gather | solution.py:383
  235.0 1.1 copy-start.1
Sparse Core Ops, SparseCore 0:
  10.5 91.0 all-gather.6
  127.5 41.0 all-gather.8
  188.0 39.9 all-gather.10

commit v3 on v2

--- a/solution.py
+++ b/solution.py
@@ -20,15 +20,14 @@
 PARAMS = pltpu.CompilerParams(vmem_limit_bytes=56 * 2**20)
 
 
-def kernel_call(kernel, outs, ins, args, scratch=(), flops=0, moved=0):
+def kernel_call(kernel, outs, ins, args, scratch=(), room=24):
     return pl.pallas_call(
         kernel,
         in_specs=ins,
         out_specs=[VMEM] * len(outs),
         out_shape=[jax.ShapeDtypeStruct(*o) for o in outs],
         scratch_shapes=scratch,
-        compiler_params=PARAMS,
-        cost_estimate=pl.CostEstimate(flops=flops, bytes_accessed=moved, transcendentals=0),
+        compiler_params=pltpu.CompilerParams(vmem_limit_bytes=room * 2**20),
     )(*args)
 
 
@@ -255,7 +254,7 @@
     logits = jnp.zeros((1, LANES), F32)
     for n in range(0, query_ref.shape[0], step):
         scores = lax.dot_general(unit_vec, query_ref[n : n + step, :], NT, preferred_element_type=F32)
-        weights = jnp.exp(scores / soft_temp)
+        weights = jnp.exp(scores * (1.0 / soft_temp))
         weights_ref[:, n : n + step] = weights
         totals = jnp.sum(weights, axis=0, keepdims=True)
         totals_ref[:, n : n + step] = totals
@@ -295,6 +294,34 @@
     ).astype(BF16)
 
 
+def join_kernel(gate_ref, up_ref, down_ref, out_ref, sems):
+    ff = gate_ref.shape[0]
+    half = ff // 2
+    left = pl.ds(0, LANES)
+    copies = [
+        pltpu.make_async_copy(gate_ref, out_ref.at[pl.ds(0, ff)], sems.at[0]),
+        pltpu.make_async_copy(up_ref, out_ref.at[pl.ds(ff, ff)], sems.at[1]),
+        pltpu.make_async_copy(
+            down_ref.at[pl.ds(0, half), left], out_ref.at[pl.ds(2 * ff, half), left], sems.at[2]
+        ),
+        pltpu.make_async_copy(
+            down_ref.at[pl.ds(half, half), left], out_ref.at[pl.ds(2 * ff, half), pl.ds(LANES, LANES)], sems.at[3]
+        ),
+    ]
+    for copy in copies:
+        copy.start()
+    for copy in copies:
+        copy.wait()
+
+
+def fan_kernel(copies, in_ref, out_ref):
+    rows = in_ref.shape[0] // 2
+    even = jnp.sum(in_ref[pl.ds(0, rows, stride=2), :], axis=0, keepdims=True)
+    odd = jnp.sum(in_ref[pl.ds(1, rows, stride=2), :], axis=0, keepdims=True)
+    parity = lax.broadcasted_iota(jnp.int32, out_ref.shape, 0) % 2
+    out_ref[...] = jnp.where(parity == 0, even, odd)
+
+
 def body(
     passages_in,
     routes,
@@ -318,12 +345,36 @@
     fold = experts * tail * 8
 
     down = down_weight[0]
-    down_halves = [
-        jnp.concatenate([down[: ff // 2, lane_block(h)], down[ff // 2 :, lane_block(h)]], axis=1) for h in range(2)
-    ]
-    first_part = jnp.concatenate([gate_weight[0].T, up_weight[0].T, down_halves[0]], axis=0)
+    first_part = pl.pallas_call(
+        join_kernel,
+        in_specs=[HBM] * 3,
+        out_specs=HBM,
+        out_shape=jax.ShapeDtypeStruct((5 * ff // 2, 2 * LANES), BF16),
+        scratch_shapes=[pltpu.SemaphoreType.DMA((4,))],
+        compiler_params=PARAMS,
+    )(gate_weight[0].T, up_weight[0].T, down)
     first_all = lax.all_gather(first_part, "rep", axis=0, tiled=False)
-    second_all = lax.all_gather(down_halves[1], "rep", axis=0, tiled=False)
+    wide_queries = queries.astype(F32)
+    query_radius = jnp.sqrt(jnp.sum(wide_queries * wide_queries, axis=-1, keepdims=True) + norm_eps)
+    query_unit = (wide_queries / query_radius).astype(BF16)
+    query_block, query_len, unit_width = queries.shape
+    total_queries = query_block * rep_count
+    own_rows = query_unit.transpose(1, 0, 2).reshape(query_len * query_block, unit_width)
+    own_half = own_rows.shape[0] // 2
+    second_part = jnp.concatenate(
+        [
+            jnp.concatenate([down[: ff // 2, LANES:], own_rows[:own_half]], axis=0),
+            jnp.concatenate([down[ff // 2 :, LANES:], own_rows[own_half:]], axis=0),
+        ],
+        axis=1,
+    )
+    second_all = lax.all_gather(second_part, "rep", axis=0, tiled=False)
+    query_rows = (
+        jnp.concatenate([second_all[:, ff // 2 :, lane_block(h)] for h in range(2)], axis=1)
+        .reshape(rep_count, query_len, query_block, unit_width)
+        .transpose(1, 0, 2, 3)
+        .reshape(query_len * total_queries, unit_width)
+    )
 
     def exchange(tiles):
         return lax.all_to_all(tiles, "exp", split_axis=0, concat_axis=0, tiled=True)
@@ -346,6 +397,7 @@
             pltpu.SemaphoreType.DMA((rep_count,)),
             pltpu.SemaphoreType.DMA((2 * rep_count,)),
         ],
+        room=56,
     )
     back_a = exchange(send_a)
     (send_b,) = kernel_call(
@@ -358,6 +410,7 @@
             pltpu.VMEM((fold, LANES), F32),
             pltpu.SemaphoreType.DMA((2 * rep_count,)),
         ],
+        room=56,
     )
     back_b = exchange(send_b)
 
@@ -375,14 +428,6 @@
     high = mix.astype(BF16)
     low = (mix - high.astype(F32)).astype(BF16)
 
-    wide_queries = queries.astype(F32)
-    query_radius = jnp.sqrt(jnp.sum(wide_queries * wide_queries, axis=-1, keepdims=True) + norm_eps)
-    query_unit = (wide_queries / query_radius).astype(BF16)
-    query_block, query_len, unit_width = queries.shape
-    total_queries = query_block * rep_count
-    all_queries = lax.all_gather(query_unit.transpose(1, 0, 2), "rep", axis=0, tiled=False)
-    query_rows = all_queries.transpose(1, 0, 2, 3).reshape(query_len * total_queries, unit_width)
-
     owner = lax.axis_index(("exp", "rep")).astype(jnp.int32).reshape(1, 1)
     positive_row = positives.reshape(1, total_queries)
 
@@ -393,7 +438,6 @@
         (back_a, high, low, passages_in, projection),
         [pltpu.VMEM((fold, LANES), F32)],
     )
-    devices = experts * rep_count
     columns = query_len * total_queries
     states, weights, unit, radius, totals, logits, shares = kernel_call(
         lambda *refs: score_kernel(tail, logit_gain, *refs),
@@ -404,15 +448,23 @@
             ((tok_count, unit_width), F32),
             ((1, columns), F32),
             ((1, total_queries), F32),
-            ((2 * devices, total_queries), F32),
+            ((2 * experts, total_queries), F32),
         ],
         [SMEM] + [VMEM] * 9,
         (owner, back_b, high, low, passages_in, projection, states_a, sum_a, query_rows, positive_row),
         [pltpu.VMEM((fold, LANES), F32)],
     )
-    sums = lax.all_to_all(
-        shares.reshape(devices, 2, total_queries), ("exp", "rep"), split_axis=0, concat_axis=0, tiled=True
-    ).reshape(2 * devices, total_queries)
+    def share_out(rows, axis):
+        pairs = rows.reshape(-1, 2, total_queries)
+        return lax.all_to_all(pairs, axis, split_axis=0, concat_axis=0, tiled=True).reshape(rows.shape)
+
+    (fanned,) = kernel_call(
+        lambda *refs: fan_kernel(rep_count, *refs),
+        [((2 * rep_count, total_queries), F32)],
+        [VMEM],
+        (share_out(shares, "exp"),),
+    )
+    sums = share_out(fanned, "rep")
     share, loss = kernel_call(
         lambda *refs: grad_kernel(logit_gain, *refs),
         [((model_width, unit_width), BF16), ((1, LANES), F32)],

time: 327 us -> 310 us (0.948)
  blocking collectives: 150 us -> 62.5 us
  waiting for transfers between devices: 92.1 us -> 133 us
  Pallas kernels: 36.1 us -> 55.8 us
  starting transfers between devices: 21.4 us -> 30.2 us
  local copies, waits for them, and re-layouts: 5.49 us -> 9.27 us
  other arithmetic: 7.05 us -> 3.58 us
    all_to_all x2 -> x3, waiting for transfers between devices: 0.01 us -> 97.5 us  [exchange(): return lax.all_to_all(tiles, 'exp', split_axis=0, concat_axis=0, tiled=True)]
    all_to_all x2 -> x1, blocking collectives: 101 us -> 22.5 us  [exchange(): return lax.all_to_all(tiles, 'exp', split_axis=0, concat_axis=0, tiled=True)]
    all_gather x2 -> x1, waiting for transfers between devices: 82.9 us -> 23.4 us  [body(): second_all = lax.all_gather(second_part, 'rep', axis=0, tiled=False)]
    pallas_call x0 -> x1, Pallas kernels: none -> 28.4 us  [body(): pl.pallas_call(join_kernel, in_specs=[HBM] * 3, out_specs=HBM, out_shape=...]
    all_to_all x2 -> x3, starting transfers between devices: 21.1 us -> 30.1 us  [exchange(): return lax.all_to_all(tiles, 'exp', split_axis=0, concat_axis=0, tiled=True)]
    pallas_call x6 -> x7, Pallas kernels: 36.1 us -> 27.4 us  [kernel_call(): pl.pallas_call(kernel, in_specs=ins, out_specs=[VMEM] * len(outs), out_sh...]
    all_to_all x1 -> x2, blocking collectives: 35.6 us -> 27.5 us  [share_out(): lax.all_to_all(pairs, axis, split_axis=0, concat_axis=0, tiled=True)]
    unnamed x10 -> x30, local copies, waits for them, and re-layouts: 1.13 us -> 7.13 us
  transfers between devices with their start and end apart: 5 -> 5, of which waited for: 3 -> 5; matrix products, arithmetic and copies ran while one was open for 2% -> 2% of each run, Pallas kernels for 4% -> 7%
where the time goes in v3:
time: 310 us; the launch traced here: 309 us
  waiting for transfers between devices  133 us (43%)
  blocking collectives  62.5 us (20%)
  Pallas kernels  55.8 us (18%)
  starting transfers between devices  30.2 us (10%)
  between operations  14.3 us (5%)
  local copies, waits for them, and re-layouts  9.27 us (3%)
  other arithmetic  3.58 us (1%)
    all_to_all x3, waiting for transfers between devices, exchange(): return lax.all_to_all(tiles, 'exp', split_axis=0, concat_axis=0, tiled=True)  97.5 us
    all_to_all x3, starting transfers between devices, exchange(): return lax.all_to_all(tiles, 'exp', split_axis=0, concat_axis=0, tiled=True)  30.1 us
    pallas_call x1, Pallas kernels, body(): pl.pallas_call(join_kernel, in_specs=[HBM] * 3, out_specs=HBM, out_shape=...  28.4 us
    all_to_all x2, blocking collectives, share_out(): lax.all_to_all(pairs, axis, split_axis=0, concat_axis=0, tiled=True)  27.5 us
    pallas_call x7, Pallas kernels, kernel_call(): pl.pallas_call(kernel, in_specs=ins, out_specs=[VMEM] * len(outs), out_sh...  27.4 us
    all_gather x1, waiting for transfers between devices, body(): second_all = lax.all_gather(second_part, 'rep', axis=0, tiled=False)  23.4 us
    all_to_all x1, blocking collectives, exchange(): return lax.all_to_all(tiles, 'exp', split_axis=0, concat_axis=0, tiled=True)  22.5 us
    all_to_all x1, blocking collectives, body(): lax.all_to_all(sent, 'rep', split_axis=0, concat_axis=0, tiled=True)  12.5 us
  transfers between devices with their start and end apart: 5, of which 5 were waited for; matrix products, arithmetic and copies ran while one was open for 2% of the time, Pallas kernels for 7%

profile of v3, /device:TPU:6, one launch (start us, length us, event | category | flops | bytes accessed | tf_op | source)
XLA Modules:
  0.0 308.5 jit_solution(4307404670154683586)
XLA Ops:
  7.2 28.4 %shard_map.113 = bf16[1760,256]{1,0:T(8,128)(2,1)} custom-call(bf16[704,256]{1,0:T(8,128)(2,1)} %bitcast.47, bf16[704,256]{1,0:T(8,128)(2,1)} %bitcast.48, bf16[704,256]{1,0:T(8,128)(2,1)} %bitcast.45), custom_call_target="tpu_custom_call" | custom-call | tf_op jit(solution)/shard_map/pallas_call | solution.py:348
  35.7 2.8 shard_map.112
  38.5 11.2 %all-to-all-start = ((bf16[64,22,8,128]{3,2,1,0:T(8,128)(2,1)}), bf16[64,22,8,128]{3,2,1,0:T(8,128)(2,1)}, u32[]{:S(2)}, u32[]{:S(2)}) async-start(bf16[64,22,8,128]{3,2,1,0:T(8,128)(2,1)} %shard_map.112), calls=%async_computation | async-start | bytes 5767168 | tf_op jit(solution)/shard_map/all_to_all | solution.py:380
  50.3 0.8 maximum_maximum_fusion
  51.0 64.3 %all-to-all-done.refs_0_ = bf16[64,22,8,128]{3,2,1,0:T(8,128)(2,1)} async-done(((bf16[64,22,8,128]{3,2,1,0:T(8,128)(2,1)}), bf16[64,22,8,128]{3,2,1,0:T(8,128)(2,1)}, u32[]{:S(2)}, u32[]{:S(2)}) %all-to-all-start) | async-done | bytes 2883616 | tf_op jit(solution)/shard_map/all_to_all | solution.py:380
  115.3 11.7 %all-gather.5.cloned.1.call-done = bf16[14080,256]{1,0:T(8,128)(2,1)} async-done(((bf16[1760,256]{1,0:T(8,128)(2,1)}), bf16[14080,256]{1,0:T(8,128)(2,1)}) %all-gather.5.cloned.1.call-update) | async-done | bytes 7208976 | tf_op jit(solution)/shard_map/all_gather | solution.py:356
  127.0 11.8 %shard_map.114 = (bf16[704,704]{1,0:T(8,128)(2,1)}, bf16[64,11,8,128]{3,2,1,0:T(8,128)(2,1)}) custom-call(bf16[64,22,8,128]{3,2,1,0:T(8,128)(2,1)} %all-to-all-done.refs_0_, bf16[8,1760,256]{2,1,0:T(8,128)(2,1)} %bitcast.41), custom_call_target="tpu_custom_call" | custom-call | tf_op jit(solution)/shard_map/pallas_call | solution.py:24
  138.8 10.5 %all-to-all-start.2 = ((bf16[64,11,8,128]{3,2,1,0:T(8,128)(2,1)}), bf16[64,11,8,128]{3,2,1,0:T(8,128)(2,1)S(1)}, u32[]{:S(2)}, u32[]{:S(2)}) async-start(bf16[64,11,8,128]{3,2,1,0:T(8,128)(2,1)} %get-tuple-element.19), calls=%async_computation.2 | async-start | bytes 2883584 | tf_op jit(solution)/shard_map/all_to_all | solution.py:380
  149.3 23.4 %all-gather.7.cloned.1.call-done = bf16[4864,256]{1,0:T(8,128)(2,1)} async-done(((bf16[608,256]{1,0:T(8,128)(2,1)}), bf16[4864,256]{1,0:T(8,128)(2,1)}) %all-gather.7.cloned.1.call-update) | async-done | bytes 2490384 | tf_op jit(solution)/shard_map/all_gather | solution.py:371
  172.7 5.2 %shard_map.115 = bf16[64,11,8,128]{3,2,1,0:T(8,128)(2,1)} custom-call(bf16[704,704]{1,0:T(8,128)(2,1)} %get-tuple-element.17.refs_0_, bf16[8,608,256]{2,1,0:T(8,128)(2,1)} %bitcast.42), custom_call_target="tpu_custom_call" | custom-call | tf_op jit(solution)/shard_map/pallas_call | solution.py:24
  178.0 6.2 %all-to-all-done.2.refs_0_ = bf16[64,11,8,128]{3,2,1,0:T(8,128)(2,1)S(1)} async-done(((bf16[64,11,8,128]{3,2,1,0:T(8,128)(2,1)}), bf16[64,11,8,128]{3,2,1,0:T(8,128)(2,1)S(1)}, u32[]{:S(2)}, u32[]{:S(2)}) %all-to-all-start.2) | async-done | bytes 1441824 | tf_op jit(solution)/shard_map/all_to_all | solution.py:380
  184.2 8.4 %all-to-all-start.1 = ((bf16[64,11,8,128]{3,2,1,0:T(8,128)(2,1)}), bf16[64,11,8,128]{3,2,1,0:T(8,128)(2,1)}, u32[]{:S(2)}, u32[]{:S(2)}) async-start(bf16[64,11,8,128]{3,2,1,0:T(8,128)(2,1)} %shard_map.115), calls=%async_computation.1 | async-start | bytes 2883584 | tf_op jit(solution)/shard_map/all_to_all | solution.py:380
  193.3 1.7 fusion.1
  195.1 1.4 fusion.6
  196.5 0.3 copy.19
  196.8 0.7 copy-done.3
  197.6 1.5 shard_map.116
  199.1 0.7 copy-done.6
  199.8 0.6 copy-done.8
  200.5 27.0 %all-to-all-done.1.refs_1_ = bf16[64,11,8,128]{3,2,1,0:T(8,128)(2,1)} async-done(((bf16[64,11,8,128]{3,2,1,0:T(8,128)(2,1)}), bf16[64,11,8,128]{3,2,1,0:T(8,128)(2,1)}, u32[]{:S(2)}, u32[]{:S(2)}) %all-to-all-start.1) | async-done | bytes 1441824 | tf_op jit(solution)/shard_map/all_to_all | solution.py:380
  227.4 1.0 copy-done.2
  228.4 1.0 copy-done.4
  229.4 1.0 copy-done.7
  230.4 0.9 copy-done.9
  231.3 4.4 %shard_map.117 = (bf16[180,2048]{1,0:T(8,128)(2,1)}, f32[180,4096]{1,0:T(8,128)S(1)}, f32[180,128]{1,0:T(8,128)S(1)}, f32[180,128]{1,0:T(8,128)S(1)}, f32[1,4096...) custom-call(s32[1,1]{1,0:T(1,128)} %bitcast.refs_0_, bf16[64,11,8,128]{3,2,1,0:T(8,128)(2,1)} %all-to-all-done.1.refs_1_, ...), custom_call_target="tpu_custom_call" | custom-call | tf_op jit(solution)/shard_map/pallas_call | solution.py:24
  235.8 15.8 %all_to_all.35 = f32[64,2,128]{2,1,0:T(2,128)S(1)} all-to-all(f32[64,2,128]{2,1,0:T(2,128)S(1)} %bitcast.34), channel_id=1, replica_groups=mesh['exp'=64,'rep'=8] {'exp'}, dimensions={0} | all-to-all | bytes 131072 | tf_op jit(solution)/shard_map/all_to_all | solution.py:459
  251.6 11.7 %all_to_all.36 = f32[8,2,128]{2,1,0:T(2,128)S(1)} all-to-all(f32[8,2,128]{2,1,0:T(2,128)S(1)} %bitcast.36), channel_id=1, replica_groups=mesh['exp'=64,'rep'=8] {'rep'}, dimensions={0} | all-to-all | bytes 16384 | tf_op jit(solution)/shard_map/all_to_all | solution.py:459
  263.2 1.1 copy-done.5
  264.3 1.6 shard_map.119
  265.9 22.5 %all_to_all.37 = bf16[64,32,128]{2,1,0:T(8,128)(2,1)S(1)} all-to-all(bf16[64,32,128]{2,1,0:T(8,128)(2,1)S(1)} %bitcast.32), channel_id=1, replica_groups=mesh['exp'=64,'rep'=8] {'exp'}, dimensions={0} | all-to-all | bytes 1048576 | tf_op jit(solution)/shard_map/all_to_all | solution.py:380
  288.6 12.5 %all_to_all.38 = f32[8,32,128]{2,1,0:T(8,128)S(1)} all-to-all(f32[8,32,128]{2,1,0:T(8,128)S(1)} %broadcast_in_dim.31), channel_id=1, replica_groups=mesh['exp'=64,'rep'=8] {'rep'}, dimensions={0} | all-to-all | bytes 262144 | tf_op jit(solution)/shard_map/all_to_all | solution.py:478
  301.1 0.6 reduce_sum.49
  (45 shorter events, 1.4 us)
Async XLA Ops:
  7.2 119.8 %all-gather.5.cloned.1.call-start = ((), (), s32[]{:S(2)}) async-start(), calls=%async_computation.7 | async-start | bytes 8110080 | tf_op jit(solution)/shard_map/all_gather | solution.py:356
  7.2 28.5 %copy-start = (bf16[180,2048]{1,0:T(8,128)(2,1)S(1)}, bf16[180,2048]{1,0:T(8,128)(2,1)}, u32[]{:S(2)}) copy-start(bf16[180,2048]{1,0:T(8,128)(2,1)} %refs_4_.3) | copy-start | bytes 2211844
  7.2 28.5 %copy-start.10 = (s32[180,2]{0,1:T(2,128)S(1)}, s32[180,2]{0,1:T(2,128)}, u32[]{:S(2)}) copy-start(s32[180,2]{0,1:T(2,128)} %param.10) | copy-start | bytes 4324
  38.5 11.3 %copy-start.13 = (bf16[16,32,128]{2,1,0:T(8,128)(2,1)S(1)}, bf16[16,32,128]{2,1,0:T(8,128)(2,1)}, u32[]{:S(2)}) copy-start(bf16[16,32,128]{2,1,0:T(8,128)(2,1)} %param.16) | copy-start | bytes 393220
  38.5 11.7 %copy-start.12 = (bf16[1,704,256]{2,1,0:T(8,128)(2,1)S(1)}, bf16[1,704,256]{2,1,0:T(8,128)(2,1)}, u32[]{:S(2)}) copy-start(bf16[1,704,256]{2,1,0:T(8,128)(2,1)} %param.14) | copy-start | bytes 1081348
  38.5 76.7 %all-to-all-start = ((bf16[64,22,8,128]{3,2,1,0:T(8,128)(2,1)}), bf16[64,22,8,128]{3,2,1,0:T(8,128)(2,1)}, u32[]{:S(2)}, u32[]{:S(2)}) async-start(bf16[64,22,8,128]{3,2,1,0:T(8,128)(2,1)} %shard_map.112), calls=%async_computation | async-start | bytes 5767168 | tf_op jit(solution)/shard_map/all_to_all | solution.py:380
  49.8 122.9 %all-gather.7.cloned.1.call-start = ((), (), s32[]{:S(2)}) async-start(), calls=%async_computation.8 | async-start | bytes 2801664 | tf_op jit(solution)/shard_map/all_gather | solution.py:371
  138.8 45.4 %all-to-all-start.2 = ((bf16[64,11,8,128]{3,2,1,0:T(8,128)(2,1)}), bf16[64,11,8,128]{3,2,1,0:T(8,128)(2,1)S(1)}, u32[]{:S(2)}, u32[]{:S(2)}) async-start(bf16[64,11,8,128]{3,2,1,0:T(8,128)(2,1)} %get-tuple-element.19), calls=%async_computation.2 | async-start | bytes 2883584 | tf_op jit(solution)/shard_map/all_to_all | solution.py:380
  177.9 14.7 %copy-start.14 = (f32[180,2]{0,1:T(2,128)S(1)}, f32[180,2]{0,1:T(2,128)}, u32[]{:S(2)}) copy-start(f32[180,2]{0,1:T(2,128)} %param.11) | copy-start | bytes 4324
  184.2 43.2 %all-to-all-start.1 = ((bf16[64,11,8,128]{3,2,1,0:T(8,128)(2,1)}), bf16[64,11,8,128]{3,2,1,0:T(8,128)(2,1)}, u32[]{:S(2)}, u32[]{:S(2)}) async-start(bf16[64,11,8,128]{3,2,1,0:T(8,128)(2,1)} %shard_map.115), calls=%async_computation.1 | async-start | bytes 2883584 | tf_op jit(solution)/shard_map/all_to_all | solution.py:380
  195.0 1.8 copy-start.1
  196.5 1.0 copy-start.3
  197.6 29.9 %copy-start.11 = (s32[128]{0:T(128)S(1)}, s32[128]{0:T(128)}, u32[]{:S(2)}) copy-start(s32[128]{0:T(128)} %param.17) | copy-start | bytes 1540
  199.1 0.7 copy-start.6
  199.8 0.6 copy-start.8
  227.4 1.0 copy-start.2
  228.4 1.0 copy-start.4
  229.4 1.0 copy-start.7
  230.4 0.9 copy-start.9
  263.2 1.1 copy-start.5
Sparse Core Ops, SparseCore 0:
  35.8 91.0 all-gather.4
  129.6 43.0 all-gather.6

commit v4 on v3

--- a/solution.py
+++ b/solution.py
@@ -17,14 +17,13 @@
 VMEM = pl.BlockSpec(memory_space=pltpu.VMEM)
 HBM = pl.BlockSpec(memory_space=pl.ANY)
 SMEM = pl.BlockSpec(memory_space=pltpu.SMEM)
-PARAMS = pltpu.CompilerParams(vmem_limit_bytes=56 * 2**20)
-
-
-def kernel_call(kernel, outs, ins, args, scratch=(), room=24):
+
+
+def kernel_call(kernel, outs, ins, args, scratch=(), room=24, out_specs=None):
     return pl.pallas_call(
         kernel,
         in_specs=ins,
-        out_specs=[VMEM] * len(outs),
+        out_specs=out_specs or [VMEM] * len(outs),
         out_shape=[jax.ShapeDtypeStruct(*o) for o in outs],
         scratch_shapes=scratch,
         compiler_params=pltpu.CompilerParams(vmem_limit_bytes=room * 2**20),
@@ -126,16 +125,30 @@
     return out
 
 
-def down_half(tail, hidden, wd_ref, out_ref, fold_ref):
-    experts = out_ref.shape[0]
+def down_half(tail, hidden, wd_ref, downs, tiles_ref, out_ref, fold_ref, sems):
+    experts = tiles_ref.shape[0]
     pairs = wd_ref.shape[0]
+    blocks = 2 * pairs
+    sent = []
+
+    def send(first, count):
+        part = (slice(None), pl.ds(first, count))
+        copy = pltpu.make_async_copy(tiles_ref.at[part], out_ref.at[part], sems.at[len(sent)])
+        copy.start()
+        sent.append(copy)
+
     for p in range(pairs):
+        for copy in downs[4 * p : 4 * p + 4]:
+            copy.wait()
         rows = jnp.dot(hidden, wd_ref[p], preferred_element_type=F32)
         for j in range(2):
-            c = 2 * p + j
-            put_head(out_ref, c, rows[: experts * HEAD, lane_block(j)])
-            put_tail(fold_ref, c, rows[experts * HEAD :, lane_block(j)])
-    store_tail(out_ref, fold_ref, 2 * pairs, tail)
+            put_head(tiles_ref, 2 * p + j, rows[: experts * HEAD, lane_block(j)])
+            put_tail(fold_ref, 2 * p + j, rows[experts * HEAD :, lane_block(j)])
+        send(2 * p, 2)
+    store_tail(tiles_ref, fold_ref, blocks, tail)
+    send(blocks, tiles_ref.shape[1] - blocks)
+    for copy in sent:
+        copy.wait()
 
 
 def down_copies(w_ref, base, wd_ref, sems):
@@ -152,48 +165,71 @@
     ]
 
 
-def expert_kernel(tail, in_ref, w_ref, hid_ref, out_ref, rows_ref, wv_ref, wd_ref, fold_ref, back_ref, sems, down_sems):
-    reps, wide, depth = wv_ref.shape
-    ff = wide // 2
-    experts = in_ref.shape[0]
+def unfold_kernel(tail, in_ref, rows_ref, fold_ref):
     blocks = rows_ref.shape[1] // LANES
-    first = experts * HEAD
-    count = rows_ref.shape[0]
-    copies = [
-        pltpu.make_async_copy(w_ref.at[r, pl.ds(0, wide)], wv_ref.at[r], sems.at[r]) for r in range(reps)
-    ]
-    downs = down_copies(w_ref, wide, wd_ref, down_sems)
-    for copy in copies + downs:
-        copy.start()
+    first = in_ref.shape[0] * HEAD
     load_tail(in_ref, fold_ref, blocks, tail)
     for c in range(blocks):
         rows_ref[:first, lane_block(c)] = get_head(in_ref, c)
-        rows_ref[first:, lane_block(c)] = get_tail(fold_ref, c, count - first)
+        rows_ref[first:, lane_block(c)] = get_tail(fold_ref, c, rows_ref.shape[0] - first)
+
+
+def expert_kernel(
+    tail, in_ref, w_ref, hid_ref, out_ref, rows_ref, hidden_ref, tiles_ref, wv_ref, wd_ref, fold_ref,
+    row_sems, sems, down_sems, hid_sems, send_sems,
+):
+    reps, wide, depth = wv_ref.shape
+    ff = wide // 2
+    count = rows_ref.shape[0]
+    copies = []
+    for r in range(reps):
+        columns = pl.ds(r * depth, depth)
+        copies.append(
+            (
+                pltpu.make_async_copy(w_ref.at[r, pl.ds(0, wide)], wv_ref.at[r], sems.at[r]),
+                pltpu.make_async_copy(in_ref.at[:, columns], rows_ref.at[:, columns], row_sems.at[r]),
+            )
+        )
+    downs = down_copies(w_ref, wide, wd_ref, down_sems)
+    for pair in copies:
+        for copy in pair:
+            copy.start()
+    for copy in downs:
+        copy.start()
     step = count // 2
+    kept = []
     for i in range(2):
         part = slice(i * step, (i + 1) * step)
         gate = up = None
         for r in range(reps):
             if i == 0:
-                copies[r].wait()
+                for copy in copies[r]:
+                    copy.wait()
             rows = rows_ref[part, r * depth : (r + 1) * depth]
             g = lax.dot_general(rows, wv_ref[r, :ff, :], NT, preferred_element_type=F32)
             u = lax.dot_general(rows, wv_ref[r, ff:, :], NT, preferred_element_type=F32)
             gate = g if gate is None else gate + g
             up = u if up is None else up + u
-        hid_ref[part, :] = (gate / (1.0 + jnp.exp(-gate)) * up).astype(BF16)
-    for copy in downs:
+        hidden_ref[part, :] = (gate / (1.0 + jnp.exp(-gate)) * up).astype(BF16)
+        span = pl.ds(i * step, step)
+        copy = pltpu.make_async_copy(hidden_ref.at[span], hid_ref.at[span], hid_sems.at[i])
+        copy.start()
+        kept.append(copy)
+    down_half(tail, hidden_ref[...], wd_ref, downs, tiles_ref, out_ref, fold_ref, send_sems)
+    for copy in kept:
         copy.wait()
-    down_half(tail, hid_ref[...], wd_ref, out_ref, back_ref)
-
-
-def second_kernel(tail, hid_ref, w_ref, out_ref, wd_ref, back_ref, down_sems):
+
+
+def second_kernel(
+    tail, hid_ref, w_ref, out_ref, hidden_ref, tiles_ref, wd_ref, fold_ref, hid_sem, down_sems, send_sems
+):
+    taken = pltpu.make_async_copy(hid_ref, hidden_ref, hid_sem)
+    taken.start()
     downs = down_copies(w_ref, 0, wd_ref, down_sems)
     for copy in downs:
         copy.start()
-    for copy in downs:
-        copy.wait()
-    down_half(tail, hid_ref[...], wd_ref, out_ref, back_ref)
+    taken.wait()
+    down_half(tail, hidden_ref[...], wd_ref, downs, tiles_ref, out_ref, fold_ref, send_sems)
 
 
 def mix_half(half, back_ref, high_ref, low_ref, x_ref, proj_ref, fold_ref, tail, store):
@@ -235,9 +271,18 @@
 
 
 def score_kernel(
-    tail, gain, owner_ref, back_ref, high_ref, low_ref, x_ref, proj_ref, half_ref, sum_ref, query_ref, positive_ref,
-    states_ref, weights_ref, unit_ref, radius_ref, totals_ref, logits_ref, shares_ref, fold_ref,
+    tail, gain, owner_ref, sum_ref, positive_ref, *refs,
 ):
+    far = refs[:7]
+    states_out_ref, weights_out_ref, unit_ref, radius_ref, totals_ref, logits_ref, shares_ref = refs[7:14]
+    back_ref, high_ref, low_ref, x_ref, proj_ref, half_ref, query_ref = near = refs[14:21]
+    fold_ref, states_ref, weights_ref, sems, out_sem, weight_sems = refs[21:]
+    loads = [pltpu.make_async_copy(f, n, sems.at[i]) for i, (f, n) in enumerate(zip(far, near))]
+    for copy in loads:
+        copy.start()
+    for copy in loads[:-1]:
+        copy.wait()
+
     def store(c, value):
         states_ref[:, lane_block(2 * c)] = half_ref[:, lane_block(c)]
         states_ref[:, lane_block(2 * c + 1)] = value
@@ -245,6 +290,9 @@
     projected = sum_ref[...] + mix_half(
         1, back_ref, high_ref, low_ref, x_ref, proj_ref, fold_ref, tail, store
     )
+    copy_out = pltpu.make_async_copy(states_ref, states_out_ref, out_sem)
+    copy_out.start()
+    loads[-1].wait()
     radius = jnp.sqrt(jnp.sum(projected * projected, axis=1, keepdims=True) + norm_eps)
     unit = projected / radius
     unit_ref[...] = unit
@@ -252,10 +300,15 @@
     unit_vec = unit.astype(BF16)
     step = 4 * LANES
     logits = jnp.zeros((1, LANES), F32)
+    kept = [copy_out]
     for n in range(0, query_ref.shape[0], step):
         scores = lax.dot_general(unit_vec, query_ref[n : n + step, :], NT, preferred_element_type=F32)
         weights = jnp.exp(scores * (1.0 / soft_temp))
         weights_ref[:, n : n + step] = weights
+        part = (slice(None), pl.ds(n, step))
+        copy = pltpu.make_async_copy(weights_ref.at[part], weights_out_ref.at[part], weight_sems.at[n // step])
+        copy.start()
+        kept.append(copy)
         totals = jnp.sum(weights, axis=0, keepdims=True)
         totals_ref[:, n : n + step] = totals
         logs = soft_temp * jnp.log(totals)
@@ -266,12 +319,23 @@
     held = jnp.where(positive_ref[...] == owner_ref[0, 0], logits, 0.0)
     odd = lax.broadcasted_iota(jnp.int32, shares_ref.shape, 0) % 2
     shares_ref[...] = jnp.where(odd == 0, jnp.exp(logits), held)
+    for copy in kept:
+        copy.wait()
 
 
 def grad_kernel(
-    gain, owner_ref, sums_ref, logits_ref, positive_ref, weights_ref, totals_ref, query_ref, unit_ref, radius_ref,
-    states_ref, share_ref, loss_ref,
+    gain, owner_ref, sums_ref, logits_ref, positive_ref, totals_ref, unit_ref, radius_ref,
+    weights_far, query_far, states_far, share_ref, loss_ref, weights_ref, query_ref, states_ref, sems, weight_sems,
 ):
+    step = 4 * LANES
+    loads = []
+    for i in range(weights_ref.shape[1] // step):
+        part = (slice(None), pl.ds(i * step, step))
+        loads.append(pltpu.make_async_copy(weights_far.at[part], weights_ref.at[part], weight_sems.at[i]))
+    load_query = pltpu.make_async_copy(query_far, query_ref, sems.at[0])
+    load_states = pltpu.make_async_copy(states_far, states_ref, sems.at[1])
+    for copy in [loads[0], load_query] + loads[1:] + [load_states]:
+        copy.start()
     senders = sums_ref.shape[0] // 2
     partition = jnp.sum(sums_ref[pl.ds(0, senders, stride=2), :], axis=0, keepdims=True)
     held = jnp.sum(sums_ref[pl.ds(1, senders, stride=2), :], axis=0, keepdims=True)
@@ -279,9 +343,10 @@
     loss_ref[...] = jnp.broadcast_to(loss, loss_ref.shape)
     positive = (positive_ref[...] == owner_ref[0, 0]).astype(F32)
     factor = gain * (jnp.exp(logits_ref[...]) / partition - positive)
-    step = 4 * LANES
     grad = None
+    load_query.wait()
     for n in range(0, query_ref.shape[0], step):
+        loads[n // step].wait()
         scale = jnp.concatenate([factor] * (step // LANES), axis=1) / totals_ref[:, n : n + step]
         coeffs = (weights_ref[:, n : n + step] * scale).astype(BF16)
         part = jnp.dot(coeffs, query_ref[n : n + step, :], preferred_element_type=F32)
@@ -289,29 +354,19 @@
     unit = unit_ref[...]
     along = jnp.sum(unit * grad, axis=1, keepdims=True)
     grad_vec = ((grad - unit * along) / radius_ref[...]).astype(BF16)
+    load_states.wait()
     share_ref[...] = lax.dot_general(
         states_ref[...], grad_vec, (((0,), (0,)), ((), ())), preferred_element_type=F32
     ).astype(BF16)
 
 
-def join_kernel(gate_ref, up_ref, down_ref, out_ref, sems):
+def join_kernel(gate_ref, up_ref, down_ref, out_ref):
     ff = gate_ref.shape[0]
     half = ff // 2
-    left = pl.ds(0, LANES)
-    copies = [
-        pltpu.make_async_copy(gate_ref, out_ref.at[pl.ds(0, ff)], sems.at[0]),
-        pltpu.make_async_copy(up_ref, out_ref.at[pl.ds(ff, ff)], sems.at[1]),
-        pltpu.make_async_copy(
-            down_ref.at[pl.ds(0, half), left], out_ref.at[pl.ds(2 * ff, half), left], sems.at[2]
-        ),
-        pltpu.make_async_copy(
-            down_ref.at[pl.ds(half, half), left], out_ref.at[pl.ds(2 * ff, half), pl.ds(LANES, LANES)], sems.at[3]
-        ),
-    ]
-    for copy in copies:
-        copy.start()
-    for copy in copies:
-        copy.wait()
+    out_ref[:ff, :] = gate_ref[...]
+    out_ref[ff : 2 * ff, :] = up_ref[...]
+    out_ref[2 * ff :, :LANES] = down_ref[:half, :LANES]
+    out_ref[2 * ff :, LANES:] = down_ref[half:, :LANES]
 
 
 def fan_kernel(copies, in_ref, out_ref):
@@ -345,14 +400,13 @@
     fold = experts * tail * 8
 
     down = down_weight[0]
-    first_part = pl.pallas_call(
+    (first_part,) = kernel_call(
         join_kernel,
-        in_specs=[HBM] * 3,
-        out_specs=HBM,
-        out_shape=jax.ShapeDtypeStruct((5 * ff // 2, 2 * LANES), BF16),
-        scratch_shapes=[pltpu.SemaphoreType.DMA((4,))],
-        compiler_params=PARAMS,
-    )(gate_weight[0].T, up_weight[0].T, down)
+        [((5 * ff // 2, 2 * LANES), BF16)],
+        [VMEM] * 3,
+        (gate_weight[0].T, up_weight[0].T, down),
+        room=56,
+    )
     first_all = lax.all_gather(first_part, "rep", axis=0, tiled=False)
     wide_queries = queries.astype(F32)
     query_radius = jnp.sqrt(jnp.sum(wide_queries * wide_queries, axis=-1, keepdims=True) + norm_eps)
@@ -382,35 +436,45 @@
     packed = pack(routes.T, passages_in, experts, tail)
     arrived = exchange(packed)
 
+    (rows_in,) = kernel_call(
+        lambda *refs: unfold_kernel(tail, *refs),
+        [((slots, model_width), BF16)],
+        [VMEM],
+        (arrived,),
+        [pltpu.VMEM((2 * fold, LANES), F32)],
+        room=56,
+    )
     half_tiles = ((experts, blocks // 2 + blocks // 16 * tail, 8, LANES), BF16)
+    down_room = [
+        pltpu.VMEM((slots, ff), BF16),
+        pltpu.VMEM(*half_tiles),
+    ]
+    pair_room = pltpu.VMEM((rep_count // 2, ff, 2 * LANES), BF16)
+    fold_room = pltpu.VMEM((fold, LANES), F32)
+    copy_sems = pltpu.SemaphoreType.DMA
     hidden, send_a = kernel_call(
         lambda *refs: expert_kernel(tail, *refs),
         [((slots, ff), BF16), half_tiles],
-        [VMEM, HBM],
-        (arrived, first_all),
-        [
-            pltpu.VMEM((slots, model_width), BF16),
-            pltpu.VMEM((rep_count, 2 * ff, model_width // rep_count), BF16),
-            pltpu.VMEM((rep_count // 2, ff, 2 * LANES), BF16),
-            pltpu.VMEM((2 * fold, LANES), F32),
-            pltpu.VMEM((fold, LANES), F32),
-            pltpu.SemaphoreType.DMA((rep_count,)),
-            pltpu.SemaphoreType.DMA((2 * rep_count,)),
-        ],
+        [HBM, HBM],
+        (rows_in, first_all),
+        [pltpu.VMEM((slots, model_width), BF16)]
+        + down_room
+        + [pltpu.VMEM((rep_count, 2 * ff, model_width // rep_count), BF16), pair_room, fold_room]
+        + [copy_sems((rep_count,)), copy_sems((rep_count,)), copy_sems((2 * rep_count,))]
+        + [copy_sems((2,)), copy_sems((rep_count // 2 + 1,))],
         room=56,
+        out_specs=[HBM, HBM],
     )
     back_a = exchange(send_a)
     (send_b,) = kernel_call(
         lambda *refs: second_kernel(tail, *refs),
         [half_tiles],
-        [VMEM, HBM],
+        [HBM, HBM],
         (hidden, second_all),
-        [
-            pltpu.VMEM((rep_count // 2, ff, 2 * LANES), BF16),
-            pltpu.VMEM((fold, LANES), F32),
-            pltpu.SemaphoreType.DMA((2 * rep_count,)),
-        ],
+        down_room
+        + [pair_room, fold_room, copy_sems, copy_sems((2 * rep_count,)), copy_sems((rep_count // 2 + 1,))],
         room=56,
+        out_specs=[HBM],
     )
     back_b = exchange(send_b)
 
@@ -439,6 +503,10 @@
         [pltpu.VMEM((fold, LANES), F32)],
     )
     columns = query_len * total_queries
+    far = (back_b, high, low, passages_in, projection, states_a, query_rows)
+    chunks = columns // (4 * LANES)
+    near_weights = pltpu.VMEM((tok_count, columns), F32)
+    near_states = pltpu.VMEM((tok_count, model_width), BF16)
     states, weights, unit, radius, totals, logits, shares = kernel_call(
         lambda *refs: score_kernel(tail, logit_gain, *refs),
         [
@@ -450,10 +518,15 @@
             ((1, total_queries), F32),
             ((2 * experts, total_queries), F32),
         ],
-        [SMEM] + [VMEM] * 9,
-        (owner, back_b, high, low, passages_in, projection, states_a, sum_a, query_rows, positive_row),
-        [pltpu.VMEM((fold, LANES), F32)],
-    )
+        [SMEM, VMEM, VMEM] + [HBM] * len(far),
+        (owner, sum_a, positive_row) + far,
+        [pltpu.VMEM(a.shape, a.dtype) for a in far]
+        + [fold_room, near_states, near_weights]
+        + [copy_sems((len(far),)), copy_sems, copy_sems((chunks,))],
+        room=56,
+        out_specs=[HBM] * 2 + [VMEM] * 5,
+    )
+
     def share_out(rows, axis):
         pairs = rows.reshape(-1, 2, total_queries)
         return lax.all_to_all(pairs, axis, split_axis=0, concat_axis=0, tiled=True).reshape(rows.shape)
@@ -468,8 +541,10 @@
     share, loss = kernel_call(
         lambda *refs: grad_kernel(logit_gain, *refs),
         [((model_width, unit_width), BF16), ((1, LANES), F32)],
-        [SMEM] + [VMEM] * 9,
-        (owner, sums, logits, positive_row, weights, totals, query_rows, unit, radius, states),
+        [SMEM] + [VMEM] * 6 + [HBM] * 3,
+        (owner, sums, logits, positive_row, totals, unit, radius, weights, query_rows, states),
+        [near_weights, pltpu.VMEM(query_rows.shape, BF16), near_states, copy_sems((2,)), copy_sems((chunks,))],
+        room=56,
     )
     rows_out = model_width // experts
     parts = exchange(share.reshape(experts, rows_out, unit_width))

time: 310 us -> 287 us (0.926)
  Pallas kernels: 55.8 us -> 41.6 us
  waiting for transfers between devices: 133 us -> 128 us
  local copies, waits for them, and re-layouts: 9.27 us -> 4.68 us
    pallas_call x8 -> x9, Pallas kernels: 55.8 us -> 41.6 us  [kernel_call(): pl.pallas_call(kernel, in_specs=ins, out_specs=out_specs or [VMEM] * len(...]
    unnamed x30 -> x20, local copies, waits for them, and re-layouts: 7.13 us -> 1.41 us
    all_gather x1, waiting for transfers between devices: 11.7 us -> 7.53 us  [body(): first_all = lax.all_gather(first_part, 'rep', axis=0, tiled=False)]
  transfers between devices with their start and end apart: 5 -> 5, of which waited for: 5 -> 5; matrix products, arithmetic and copies ran while one was open for 2% -> 2% of each run, Pallas kernels for 7% -> 9%
where the time goes in v4:
time: 287 us; the launch traced here: 286 us
  waiting for transfers between devices  128 us (45%)
  blocking collectives  63.5 us (22%)
  Pallas kernels  41.6 us (14%)
  starting transfers between devices  30.2 us (11%)
  between operations  14.3 us (5%)
  local copies, waits for them, and re-layouts  4.68 us (2%)
  other arithmetic  3.57 us (1%)
    all_to_all x3, waiting for transfers between devices, exchange(): return lax.all_to_all(tiles, 'exp', split_axis=0, concat_axis=0, tiled=True)  96.4 us
    pallas_call x9, Pallas kernels, kernel_call(): pl.pallas_call(kernel, in_specs=ins, out_specs=out_specs or [VMEM] * len(...  41.6 us
    all_to_all x3, starting transfers between devices, exchange(): return lax.all_to_all(tiles, 'exp', split_axis=0, concat_axis=0, tiled=True)  30.1 us
    all_to_all x2, blocking collectives, share_out(): lax.all_to_all(pairs, axis, split_axis=0, concat_axis=0, tiled=True)  27.6 us
    all_gather x1, waiting for transfers between devices, body(): second_all = lax.all_gather(second_part, 'rep', axis=0, tiled=False)  23.6 us
    all_to_all x1, blocking collectives, exchange(): return lax.all_to_all(tiles, 'exp', split_axis=0, concat_axis=0, tiled=True)  23.3 us
    all_to_all x1, blocking collectives, body(): lax.all_to_all(sent, 'rep', split_axis=0, concat_axis=0, tiled=True)  12.5 us
    all_gather x1, waiting for transfers between devices, body(): first_all = lax.all_gather(first_part, 'rep', axis=0, tiled=False)  7.53 us
  transfers between devices with their start and end apart: 5, of which 5 were waited for; matrix products, arithmetic and copies ran while one was open for 2% of the time, Pallas kernels for 9%

profile of v4, /device:TPU:6, one launch (start us, length us, event | category | flops | bytes accessed | tf_op | source)
XLA Modules:
  0.0 285.6 jit_solution(15089193810010497698)
XLA Ops:
  7.2 2.3 shard_map.114
  9.5 2.8 shard_map.112
  12.4 11.2 %all-to-all-start = ((bf16[64,22,8,128]{3,2,1,0:T(8,128)(2,1)}), bf16[64,22,8,128]{3,2,1,0:T(8,128)(2,1)}, u32[]{:S(2)}, u32[]{:S(2)}) async-start(bf16[64,22,8,128]{3,2,1,0:T(8,128)(2,1)} %shard_map.112), calls=%async_computation | async-start | bytes 5767168 | tf_op jit(solution)/shard_map/all_to_all | solution.py:434
  23.7 0.1 fusion.2
  23.9 0.1 fusion.4
  24.1 0.8 maximum_maximum_fusion
  24.9 64.3 %all-to-all-done.refs_0_ = bf16[64,22,8,128]{3,2,1,0:T(8,128)(2,1)} async-done(((bf16[64,22,8,128]{3,2,1,0:T(8,128)(2,1)}), bf16[64,22,8,128]{3,2,1,0:T(8,128)(2,1)}, u32[]{:S(2)}, u32[]{:S(2)}) %all-to-all-start) | async-done | bytes 2883616 | tf_op jit(solution)/shard_map/all_to_all | solution.py:434
  89.1 4.6 %shard_map.113.refs_0_ = bf16[704,2048]{1,0:T(8,128)(2,1)} custom-call(bf16[64,22,8,128]{3,2,1,0:T(8,128)(2,1)} %all-to-all-done.refs_0_), custom_call_target="tpu_custom_call" | custom-call | tf_op jit(solution)/shard_map/pallas_call | solution.py:23
  93.7 7.5 %all-gather.5.cloned.1.call-done = bf16[14080,256]{1,0:T(8,128)(2,1)} async-done(((bf16[1760,256]{1,0:T(8,128)(2,1)}), bf16[14080,256]{1,0:T(8,128)(2,1)}) %all-gather.5.cloned.1.call-update) | async-done | bytes 7208976 | tf_op jit(solution)/shard_map/all_gather | solution.py:410
  101.2 11.7 %shard_map.115 = (bf16[704,704]{1,0:T(8,128)(2,1)}, bf16[64,11,8,128]{3,2,1,0:T(8,128)(2,1)}) custom-call(bf16[704,2048]{1,0:T(8,128)(2,1)} %shard_map.113.refs_0_, bf16[8,1760,256]{2,1,0:T(8,128)(2,1)} %bitcast.36), custom_call_target="tpu_custom_call" | custom-call | tf_op jit(solution)/shard_map/pallas_call | solution.py:23
  112.9 10.5 %all-to-all-start.1 = ((bf16[64,11,8,128]{3,2,1,0:T(8,128)(2,1)}), bf16[64,11,8,128]{3,2,1,0:T(8,128)(2,1)S(1)}, u32[]{:S(2)}, u32[]{:S(2)}) async-start(bf16[64,11,8,128]{3,2,1,0:T(8,128)(2,1)} %get-tuple-element.17), calls=%async_computation.1 | async-start | bytes 2883584 | tf_op jit(solution)/shard_map/all_to_all | solution.py:434
  123.4 23.6 %all-gather.7.cloned.1.call-done = bf16[4864,256]{1,0:T(8,128)(2,1)} async-done(((bf16[608,256]{1,0:T(8,128)(2,1)}), bf16[4864,256]{1,0:T(8,128)(2,1)}) %all-gather.7.cloned.1.call-update) | async-done | bytes 2490384 | tf_op jit(solution)/shard_map/all_gather | solution.py:425
  147.0 5.7 %shard_map.117 = bf16[64,11,8,128]{3,2,1,0:T(8,128)(2,1)} custom-call(bf16[704,704]{1,0:T(8,128)(2,1)} %get-tuple-element.20.refs_0_, bf16[8,608,256]{2,1,0:T(8,128)(2,1)} %bitcast.37), custom_call_target="tpu_custom_call" | custom-call | tf_op jit(solution)/shard_map/pallas_call | solution.py:23
  152.7 5.6 %all-to-all-done.1.refs_0_ = bf16[64,11,8,128]{3,2,1,0:T(8,128)(2,1)S(1)} async-done(((bf16[64,11,8,128]{3,2,1,0:T(8,128)(2,1)}), bf16[64,11,8,128]{3,2,1,0:T(8,128)(2,1)S(1)}, u32[]{:S(2)}, u32[]{:S(2)}) %all-to-all-start.1) | async-done | bytes 1441824 | tf_op jit(solution)/shard_map/all_to_all | solution.py:434
  158.3 8.4 %all-to-all-start.2 = ((bf16[64,11,8,128]{3,2,1,0:T(8,128)(2,1)}), bf16[64,11,8,128]{3,2,1,0:T(8,128)(2,1)}, u32[]{:S(2)}, u32[]{:S(2)}) async-start(bf16[64,11,8,128]{3,2,1,0:T(8,128)(2,1)} %shard_map.117), calls=%async_computation.2 | async-start | bytes 2883584 | tf_op jit(solution)/shard_map/all_to_all | solution.py:434
  166.7 0.1 copy.16
  166.9 0.2 fusion
  167.3 0.1 copy.15
  167.4 1.7 fusion.1
  169.2 1.5 fusion.6
  170.7 1.3 copy.19
  172.1 1.5 shard_map.116
  173.6 0.7 copy-done.4
  174.3 0.6 copy-done.5
  175.0 26.6 %all-to-all-done.2.refs_3_ = bf16[64,11,8,128]{3,2,1,0:T(8,128)(2,1)} async-done(((bf16[64,11,8,128]{3,2,1,0:T(8,128)(2,1)}), bf16[64,11,8,128]{3,2,1,0:T(8,128)(2,1)}, u32[]{:S(2)}, u32[]{:S(2)}) %all-to-all-start.2) | async-done | bytes 1441824 | tf_op jit(solution)/shard_map/all_to_all | solution.py:434
  201.6 7.1 %shard_map.118 = (bf16[180,2048]{1,0:T(8,128)(2,1)}, f32[180,4096]{1,0:T(8,128)}, f32[180,128]{1,0:T(8,128)}, f32[180,128]{1,0:T(8,128)}, f32[1,4096]{1,0:T(1,12...) custom-call(s32[1,1]{1,0:T(1,128)} %bitcast.refs_0_, f32[180,128]{1,0:T(8,128)} %copy-done.5, s32[1,128]{1,0:T(1,128)} %bitcast.49, ...), custom_call_target="tpu_custom_call" | custom-call | tf_op jit(solution)/shard_map/pallas_call | solution.py:23
  208.7 16.0 %all_to_all.35 = f32[64,2,128]{2,1,0:T(2,128)S(1)} all-to-all(f32[64,2,128]{2,1,0:T(2,128)} %bitcast.47), channel_id=1, replica_groups=mesh['exp'=64,'rep'=8] {'exp'}, dimensions={0} | all-to-all | bytes 131072 | tf_op jit(solution)/shard_map/all_to_all | solution.py:532
  224.7 11.6 %all_to_all.36 = f32[8,2,128]{2,1,0:T(2,128)} all-to-all(f32[8,2,128]{2,1,0:T(2,128)S(1)} %bitcast.31), channel_id=1, replica_groups=mesh['exp'=64,'rep'=8] {'rep'}, dimensions={0} | all-to-all | bytes 16384 | tf_op jit(solution)/shard_map/all_to_all | solution.py:532
  236.3 5.9 %shard_map.120 = (bf16[2048,128]{1,0:T(8,128)(2,1)}, f32[1,128]{1,0:T(1,128)}) custom-call(s32[1,1]{1,0:T(1,128)} %bitcast.refs_0_, f32[16,128]{1,0:T(8,128)} %bitcast.48, f32[1,128]{1,0:T(1,128)} %get-tuple-element.24.refs_2_, s32[1,128]{1,0:T(1,128)} %bitcast.50, f32[1,4096]{1,0:T(1,128)} %get-tuple-element.25.refs_4_, ...), custom_call_target="tpu_custom_call" | custom-call | tf_op jit(solution)/shard_map/pallas_call | solution.py:23
  242.2 23.3 %all_to_all.37 = bf16[64,32,128]{2,1,0:T(8,128)(2,1)S(1)} all-to-all(bf16[64,32,128]{2,1,0:T(8,128)(2,1)} %bitcast.42), channel_id=1, replica_groups=mesh['exp'=64,'rep'=8] {'exp'}, dimensions={0} | all-to-all | bytes 1048576 | tf_op jit(solution)/shard_map/all_to_all | solution.py:434
  265.7 12.5 %all_to_all.38 = f32[8,32,128]{2,1,0:T(8,128)S(1)} all-to-all(f32[8,32,128]{2,1,0:T(8,128)S(1)} %broadcast_in_dim.31), channel_id=1, replica_groups=mesh['exp'=64,'rep'=8] {'rep'}, dimensions={0} | all-to-all | bytes 262144 | tf_op jit(solution)/shard_map/all_to_all | solution.py:553
  278.2 0.6 reduce_sum.49
  (36 shorter events, 0.7 us)
Async XLA Ops:
  7.2 2.4 copy-start.6
  7.2 2.4 copy-start
  7.2 94.1 %all-gather.5.cloned.1.call-start = ((), (), s32[]{:S(2)}) async-start(), calls=%async_computation.7 | async-start | bytes 8110080 | tf_op jit(solution)/shard_map/all_gather | solution.py:410
  12.4 11.3 %copy-start.8 = (bf16[16,32,128]{2,1,0:T(8,128)(2,1)S(1)}, bf16[16,32,128]{2,1,0:T(8,128)(2,1)}, u32[]{:S(2)}) copy-start(bf16[16,32,128]{2,1,0:T(8,128)(2,1)} %param.16) | copy-start | bytes 393220
  12.4 11.7 %copy-start.7 = (bf16[1,704,256]{2,1,0:T(8,128)(2,1)S(1)}, bf16[1,704,256]{2,1,0:T(8,128)(2,1)}, u32[]{:S(2)}) copy-start(bf16[1,704,256]{2,1,0:T(8,128)(2,1)} %param.14) | copy-start | bytes 1081348
  12.4 76.8 %all-to-all-start = ((bf16[64,22,8,128]{3,2,1,0:T(8,128)(2,1)}), bf16[64,22,8,128]{3,2,1,0:T(8,128)(2,1)}, u32[]{:S(2)}, u32[]{:S(2)}) async-start(bf16[64,22,8,128]{3,2,1,0:T(8,128)(2,1)} %shard_map.112), calls=%async_computation | async-start | bytes 5767168 | tf_op jit(solution)/shard_map/all_to_all | solution.py:434
  23.6 123.4 %all-gather.7.cloned.1.call-start = ((), (), s32[]{:S(2)}) async-start(), calls=%async_computation.8 | async-start | bytes 2801664 | tf_op jit(solution)/shard_map/all_gather | solution.py:425
  112.9 45.4 %all-to-all-start.1 = ((bf16[64,11,8,128]{3,2,1,0:T(8,128)(2,1)}), bf16[64,11,8,128]{3,2,1,0:T(8,128)(2,1)S(1)}, u32[]{:S(2)}, u32[]{:S(2)}) async-start(bf16[64,11,8,128]{3,2,1,0:T(8,128)(2,1)} %get-tuple-element.17), calls=%async_computation.1 | async-start | bytes 2883584 | tf_op jit(solution)/shard_map/all_to_all | solution.py:434
  152.7 14.0 %copy-start.9 = (f32[180,2]{0,1:T(2,128)S(1)}, f32[180,2]{0,1:T(2,128)}, u32[]{:S(2)}) copy-start(f32[180,2]{0,1:T(2,128)} %param.11) | copy-start | bytes 4324
  158.3 43.2 %all-to-all-start.2 = ((bf16[64,11,8,128]{3,2,1,0:T(8,128)(2,1)}), bf16[64,11,8,128]{3,2,1,0:T(8,128)(2,1)}, u32[]{:S(2)}, u32[]{:S(2)}) async-start(bf16[64,11,8,128]{3,2,1,0:T(8,128)(2,1)} %shard_map.117), calls=%async_computation.2 | async-start | bytes 2883584 | tf_op jit(solution)/shard_map/all_to_all | solution.py:434
  169.1 2.9 %copy-start.1 = (bf16[180,704]{1,0:T(8,128)(2,1)}, bf16[180,704]{1,0:T(8,128)(2,1)S(1)}, u32[]{:S(2)}) copy-start(bf16[180,704]{1,0:T(8,128)(2,1)S(1)} %get-tuple-element.31.refs_2_.refs_5_) | copy-start | bytes 760324
  169.2 2.9 %copy-start.2 = (bf16[180,704]{1,0:T(8,128)(2,1)}, bf16[180,704]{1,0:T(8,128)(2,1)S(1)}, u32[]{:S(2)}) copy-start(bf16[180,704]{1,0:T(8,128)(2,1)S(1)} %get-tuple-element.32.refs_1_.refs_4_) | copy-start | bytes 760324
  170.7 1.4 copy-start.3
  173.6 0.7 copy-start.4
  174.3 0.6 copy-start.5
Sparse Core Ops, SparseCore 0:
  10.1 91.0 all-gather.4
  103.9 43.0 all-gather.6

commit v5 on v4

--- a/solution.py
+++ b/solution.py
@@ -125,69 +125,52 @@
     return out
 
 
-def down_half(tail, hidden, wd_ref, downs, tiles_ref, out_ref, fold_ref, sems):
-    experts = tiles_ref.shape[0]
-    pairs = wd_ref.shape[0]
-    blocks = 2 * pairs
-    sent = []
-
-    def send(first, count):
-        part = (slice(None), pl.ds(first, count))
-        copy = pltpu.make_async_copy(tiles_ref.at[part], out_ref.at[part], sems.at[len(sent)])
-        copy.start()
-        sent.append(copy)
-
+def down_half(tail, hidden, wd_ref, downs, out_ref, fold_ref):
+    experts = out_ref.shape[0]
+    pairs = wd_ref.shape[0] // 2
     for p in range(pairs):
-        for copy in downs[4 * p : 4 * p + 4]:
+        for copy in downs[2 * p : 2 * p + 2]:
             copy.wait()
-        rows = jnp.dot(hidden, wd_ref[p], preferred_element_type=F32)
+        pair = (wd_ref[2 * p], wd_ref[2 * p + 1])
+        weight = jnp.concatenate(
+            [jnp.concatenate([w[:, lane_block(h)] for w in pair], axis=1) for h in range(2)], axis=0
+        )
+        rows = jnp.dot(hidden, weight, preferred_element_type=F32)
         for j in range(2):
-            put_head(tiles_ref, 2 * p + j, rows[: experts * HEAD, lane_block(j)])
+            put_head(out_ref, 2 * p + j, rows[: experts * HEAD, lane_block(j)])
             put_tail(fold_ref, 2 * p + j, rows[experts * HEAD :, lane_block(j)])
-        send(2 * p, 2)
-    store_tail(tiles_ref, fold_ref, blocks, tail)
-    send(blocks, tiles_ref.shape[1] - blocks)
-    for copy in sent:
-        copy.wait()
+    store_tail(out_ref, fold_ref, 2 * pairs, tail)
 
 
 def down_copies(w_ref, base, wd_ref, sems):
-    reps = w_ref.shape[0]
-    half = wd_ref.shape[1] // 2
+    reps, half, _ = wd_ref.shape
     return [
-        pltpu.make_async_copy(
-            w_ref.at[r, pl.ds(base, half), pl.ds(j * LANES, LANES)],
-            wd_ref.at[r // 2, pl.ds(j * half, half), pl.ds((r % 2) * LANES, LANES)],
-            sems.at[2 * r + j],
-        )
-        for r in range(reps)
-        for j in range(2)
+        pltpu.make_async_copy(w_ref.at[r, pl.ds(base, half)], wd_ref.at[r], sems.at[r]) for r in range(reps)
     ]
 
 
 def unfold_kernel(tail, in_ref, rows_ref, fold_ref):
-    blocks = rows_ref.shape[1] // LANES
+    reps, count, depth = rows_ref.shape
     first = in_ref.shape[0] * HEAD
-    load_tail(in_ref, fold_ref, blocks, tail)
-    for c in range(blocks):
-        rows_ref[:first, lane_block(c)] = get_head(in_ref, c)
-        rows_ref[first:, lane_block(c)] = get_tail(fold_ref, c, rows_ref.shape[0] - first)
+    load_tail(in_ref, fold_ref, reps * depth // LANES, tail)
+    for c in range(reps * depth // LANES):
+        r, lanes = c * LANES // depth, lane_block(c % (depth // LANES))
+        rows_ref[r, :first, lanes] = get_head(in_ref, c)
+        rows_ref[r, first:, lanes] = get_tail(fold_ref, c, count - first)
 
 
 def expert_kernel(
-    tail, in_ref, w_ref, hid_ref, out_ref, rows_ref, hidden_ref, tiles_ref, wv_ref, wd_ref, fold_ref,
-    row_sems, sems, down_sems, hid_sems, send_sems,
+    tail, in_ref, w_ref, hid_ref, out_ref, rows_ref, wv_ref, wd_ref, fold_ref, row_sems, sems, down_sems
 ):
     reps, wide, depth = wv_ref.shape
     ff = wide // 2
-    count = rows_ref.shape[0]
+    count = rows_ref.shape[1]
     copies = []
     for r in range(reps):
-        columns = pl.ds(r * depth, depth)
         copies.append(
             (
+                pltpu.make_async_copy(in_ref.at[r], rows_ref.at[r], row_sems.at[r]),
                 pltpu.make_async_copy(w_ref.at[r, pl.ds(0, wide)], wv_ref.at[r], sems.at[r]),
-                pltpu.make_async_copy(in_ref.at[:, columns], rows_ref.at[:, columns], row_sems.at[r]),
             )
         )
     downs = down_copies(w_ref, wide, wd_ref, down_sems)
@@ -197,102 +180,69 @@
     for copy in downs:
         copy.start()
     step = count // 2
-    kept = []
+    sums = [None] * 4
+    for r in range(reps):
+        for copy in copies[r]:
+            copy.wait()
+        for i in range(4):
+            rows = rows_ref[r, (i // 2) * step : (i // 2 + 1) * step, :]
+            weight = wv_ref[r, (i % 2) * ff : (i % 2 + 1) * ff, :]
+            part = lax.dot_general(rows, weight, NT, preferred_element_type=F32)
+            sums[i] = part if r == 0 else sums[i] + part
     for i in range(2):
-        part = slice(i * step, (i + 1) * step)
-        gate = up = None
-        for r in range(reps):
-            if i == 0:
-                for copy in copies[r]:
-                    copy.wait()
-            rows = rows_ref[part, r * depth : (r + 1) * depth]
-            g = lax.dot_general(rows, wv_ref[r, :ff, :], NT, preferred_element_type=F32)
-            u = lax.dot_general(rows, wv_ref[r, ff:, :], NT, preferred_element_type=F32)
-            gate = g if gate is None else gate + g
-            up = u if up is None else up + u
-        hidden_ref[part, :] = (gate / (1.0 + jnp.exp(-gate)) * up).astype(BF16)
-        span = pl.ds(i * step, step)
-        copy = pltpu.make_async_copy(hidden_ref.at[span], hid_ref.at[span], hid_sems.at[i])
-        copy.start()
-        kept.append(copy)
-    down_half(tail, hidden_ref[...], wd_ref, downs, tiles_ref, out_ref, fold_ref, send_sems)
-    for copy in kept:
-        copy.wait()
-
-
-def second_kernel(
-    tail, hid_ref, w_ref, out_ref, hidden_ref, tiles_ref, wd_ref, fold_ref, hid_sem, down_sems, send_sems
-):
-    taken = pltpu.make_async_copy(hid_ref, hidden_ref, hid_sem)
-    taken.start()
+        gate, up = sums[2 * i], sums[2 * i + 1]
+        hid_ref[i * step : (i + 1) * step, :] = (gate / (1.0 + jnp.exp(-gate)) * up).astype(BF16)
+    down_half(tail, hid_ref[...], wd_ref, downs, out_ref, fold_ref)
+
+
+def second_kernel(tail, hid_ref, w_ref, out_ref, wd_ref, fold_ref, down_sems):
     downs = down_copies(w_ref, 0, wd_ref, down_sems)
     for copy in downs:
         copy.start()
-    taken.wait()
-    down_half(tail, hidden_ref[...], wd_ref, downs, tiles_ref, out_ref, fold_ref, send_sems)
-
-
-def mix_half(half, back_ref, high_ref, low_ref, x_ref, proj_ref, fold_ref, tail, store):
+    down_half(tail, hid_ref[...], wd_ref, downs, out_ref, fold_ref)
+
+
+def mix_half(half, back_ref, mix_ref, base_ref, fold_ref, tail, store):
     experts = back_ref.shape[0]
-    blocks = x_ref.shape[1] // (2 * LANES)
+    blocks = base_ref.shape[1] // (2 * LANES)
     first = experts * HEAD
     load_tail(back_ref, fold_ref, blocks, tail)
-    projected = None
     for p in range(blocks // 2):
         cs = (2 * p, 2 * p + 1)
         head = jnp.concatenate([get_head(back_ref, c) for c in cs], axis=1)
         rest = jnp.concatenate([get_tail(fold_ref, c, experts * tail) for c in cs], axis=1)
-        added = (
-            jnp.dot(high_ref[:, :first], head, preferred_element_type=F32)
-            + jnp.dot(low_ref[:, :first], head, preferred_element_type=F32)
-            + jnp.dot(high_ref[:, first:], rest, preferred_element_type=F32)
-            + jnp.dot(low_ref[:, first:], rest, preferred_element_type=F32)
+        added = sum(
+            jnp.dot(mix_ref[i, :, :first], head, preferred_element_type=F32)
+            + jnp.dot(mix_ref[i, :, first:], rest, preferred_element_type=F32)
+            for i in range(2)
         )
-        states = []
-        projs = []
         for j, c in enumerate(cs):
             columns = lane_block(2 * c + half)
-            value = (x_ref[:, columns].astype(F32) + added[:, lane_block(j)]).astype(BF16)
-            store(c, value)
-            states.append(value)
-            projs.append(proj_ref[columns, :])
-        part = jnp.dot(
-            jnp.concatenate(states, axis=1), jnp.concatenate(projs, axis=0), preferred_element_type=F32
-        )
-        projected = part if projected is None else projected + part
-    return projected
-
-
-def mix_kernel(tail, back_ref, high_ref, low_ref, x_ref, proj_ref, half_ref, sum_ref, fold_ref):
-    def store(c, value):
-        half_ref[:, lane_block(c)] = value
-
-    sum_ref[...] = mix_half(0, back_ref, high_ref, low_ref, x_ref, proj_ref, fold_ref, tail, store)
-
-
-def score_kernel(
-    tail, gain, owner_ref, sum_ref, positive_ref, *refs,
-):
-    far = refs[:7]
-    states_out_ref, weights_out_ref, unit_ref, radius_ref, totals_ref, logits_ref, shares_ref = refs[7:14]
-    back_ref, high_ref, low_ref, x_ref, proj_ref, half_ref, query_ref = near = refs[14:21]
-    fold_ref, states_ref, weights_ref, sems, out_sem, weight_sems = refs[21:]
-    loads = [pltpu.make_async_copy(f, n, sems.at[i]) for i, (f, n) in enumerate(zip(far, near))]
-    for copy in loads:
-        copy.start()
-    for copy in loads[:-1]:
-        copy.wait()
-
-    def store(c, value):
-        states_ref[:, lane_block(2 * c)] = half_ref[:, lane_block(c)]
-        states_ref[:, lane_block(2 * c + 1)] = value
-
-    projected = sum_ref[...] + mix_half(
-        1, back_ref, high_ref, low_ref, x_ref, proj_ref, fold_ref, tail, store
-    )
+            store(columns, (base_ref[:, columns].astype(F32) + added[:, lane_block(j)]).astype(BF16))
+
+
+def mix_kernel(tail, back_ref, mix_ref, x_ref, out_ref, fold_ref):
+    def store(columns, value):
+        out_ref[:, columns] = value
+
+    for c in range(1, x_ref.shape[1] // LANES, 2):
+        out_ref[:, lane_block(c)] = x_ref[:, lane_block(c)]
+    mix_half(0, back_ref, mix_ref, x_ref, fold_ref, tail, store)
+
+
+def score_kernel(tail, gain, hit_ref, back_ref, mix_ref, base_ref, proj_ref, query_ref, *refs):
+    states_out_ref, states_ref, weights_ref, unit_ref, radius_ref, totals_ref, logits_ref, shares_ref = refs[:8]
+    fold_ref, out_sem = refs[8:]
+
+    def store(columns, value):
+        states_ref[:, columns] = value
+
+    for c in range(0, base_ref.shape[1] // LANES, 2):
+        states_ref[:, lane_block(c)] = base_ref[:, lane_block(c)]
+    mix_half(1, back_ref, mix_ref, base_ref, fold_ref, tail, store)
     copy_out = pltpu.make_async_copy(states_ref, states_out_ref, out_sem)
     copy_out.start()
-    loads[-1].wait()
+    projected = jnp.dot(states_ref[...], proj_ref[...], preferred_element_type=F32)
     radius = jnp.sqrt(jnp.sum(projected * projected, axis=1, keepdims=True) + norm_eps)
     unit = projected / radius
     unit_ref[...] = unit
@@ -300,15 +250,10 @@
     unit_vec = unit.astype(BF16)
     step = 4 * LANES
     logits = jnp.zeros((1, LANES), F32)
-    kept = [copy_out]
     for n in range(0, query_ref.shape[0], step):
         scores = lax.dot_general(unit_vec, query_ref[n : n + step, :], NT, preferred_element_type=F32)
         weights = jnp.exp(scores * (1.0 / soft_temp))
         weights_ref[:, n : n + step] = weights
-        part = (slice(None), pl.ds(n, step))
-        copy = pltpu.make_async_copy(weights_ref.at[part], weights_out_ref.at[part], weight_sems.at[n // step])
-        copy.start()
-        kept.append(copy)
         totals = jnp.sum(weights, axis=0, keepdims=True)
         totals_ref[:, n : n + step] = totals
         logs = soft_temp * jnp.log(totals)
@@ -316,37 +261,26 @@
             logits = logits + logs[:, lane_block(j)]
     logits = gain * logits
     logits_ref[...] = logits
-    held = jnp.where(positive_ref[...] == owner_ref[0, 0], logits, 0.0)
+    held = jnp.where(lax.broadcasted_iota(jnp.int32, logits.shape, 1) == hit_ref[0, 0], logits, 0.0)
     odd = lax.broadcasted_iota(jnp.int32, shares_ref.shape, 0) % 2
     shares_ref[...] = jnp.where(odd == 0, jnp.exp(logits), held)
-    for copy in kept:
-        copy.wait()
+    copy_out.wait()
 
 
 def grad_kernel(
-    gain, owner_ref, sums_ref, logits_ref, positive_ref, totals_ref, unit_ref, radius_ref,
-    weights_far, query_far, states_far, share_ref, loss_ref, weights_ref, query_ref, states_ref, sems, weight_sems,
+    gain, hit_ref, sums_ref, logits_ref, weights_ref, totals_ref, query_ref, unit_ref, radius_ref,
+    states_ref, share_ref, loss_ref,
 ):
     step = 4 * LANES
-    loads = []
-    for i in range(weights_ref.shape[1] // step):
-        part = (slice(None), pl.ds(i * step, step))
-        loads.append(pltpu.make_async_copy(weights_far.at[part], weights_ref.at[part], weight_sems.at[i]))
-    load_query = pltpu.make_async_copy(query_far, query_ref, sems.at[0])
-    load_states = pltpu.make_async_copy(states_far, states_ref, sems.at[1])
-    for copy in [loads[0], load_query] + loads[1:] + [load_states]:
-        copy.start()
     senders = sums_ref.shape[0] // 2
     partition = jnp.sum(sums_ref[pl.ds(0, senders, stride=2), :], axis=0, keepdims=True)
     held = jnp.sum(sums_ref[pl.ds(1, senders, stride=2), :], axis=0, keepdims=True)
     loss = jnp.sum(jnp.log(partition) - held, axis=1, keepdims=True) / partition.shape[1]
     loss_ref[...] = jnp.broadcast_to(loss, loss_ref.shape)
-    positive = (positive_ref[...] == owner_ref[0, 0]).astype(F32)
+    positive = (lax.broadcasted_iota(jnp.int32, partition.shape, 1) == hit_ref[0, 0]).astype(F32)
     factor = gain * (jnp.exp(logits_ref[...]) / partition - positive)
     grad = None
-    load_query.wait()
     for n in range(0, query_ref.shape[0], step):
-        loads[n // step].wait()
         scale = jnp.concatenate([factor] * (step // LANES), axis=1) / totals_ref[:, n : n + step]
         coeffs = (weights_ref[:, n : n + step] * scale).astype(BF16)
         part = jnp.dot(coeffs, query_ref[n : n + step, :], preferred_element_type=F32)
@@ -354,7 +288,6 @@
     unit = unit_ref[...]
     along = jnp.sum(unit * grad, axis=1, keepdims=True)
     grad_vec = ((grad - unit * along) / radius_ref[...]).astype(BF16)
-    load_states.wait()
     share_ref[...] = lax.dot_general(
         states_ref[...], grad_vec, (((0,), (0,)), ((), ())), preferred_element_type=F32
     ).astype(BF16)
@@ -438,18 +371,15 @@
 
     (rows_in,) = kernel_call(
         lambda *refs: unfold_kernel(tail, *refs),
-        [((slots, model_width), BF16)],
+        [((rep_count, slots, model_width // rep_count), BF16)],
         [VMEM],
         (arrived,),
         [pltpu.VMEM((2 * fold, LANES), F32)],
         room=56,
     )
     half_tiles = ((experts, blocks // 2 + blocks // 16 * tail, 8, LANES), BF16)
-    down_room = [
-        pltpu.VMEM((slots, ff), BF16),
-        pltpu.VMEM(*half_tiles),
-    ]
-    pair_room = pltpu.VMEM((rep_count // 2, ff, 2 * LANES), BF16)
+    depth = model_width // rep_count
+    down_room = pltpu.VMEM((rep_count, ff // 2, 2 * LANES), BF16)
     fold_room = pltpu.VMEM((fold, LANES), F32)
     copy_sems = pltpu.SemaphoreType.DMA
     hidden, send_a = kernel_call(
@@ -457,24 +387,19 @@
         [((slots, ff), BF16), half_tiles],
         [HBM, HBM],
         (rows_in, first_all),
-        [pltpu.VMEM((slots, model_width), BF16)]
-        + down_room
-        + [pltpu.VMEM((rep_count, 2 * ff, model_width // rep_count), BF16), pair_room, fold_room]
-        + [copy_sems((rep_count,)), copy_sems((rep_count,)), copy_sems((2 * rep_count,))]
-        + [copy_sems((2,)), copy_sems((rep_count // 2 + 1,))],
+        [pltpu.VMEM((rep_count, slots, depth), BF16), pltpu.VMEM((rep_count, 2 * ff, depth), BF16)]
+        + [down_room, fold_room]
+        + [copy_sems((rep_count,))] * 3,
         room=56,
-        out_specs=[HBM, HBM],
     )
     back_a = exchange(send_a)
     (send_b,) = kernel_call(
         lambda *refs: second_kernel(tail, *refs),
         [half_tiles],
-        [HBM, HBM],
+        [VMEM, HBM],
         (hidden, second_all),
-        down_room
-        + [pair_room, fold_room, copy_sems, copy_sems((2 * rep_count,)), copy_sems((rep_count // 2 + 1,))],
+        [down_room, fold_room, copy_sems((rep_count,))],
         room=56,
-        out_specs=[HBM],
     )
     back_b = exchange(send_b)
 
@@ -491,25 +416,24 @@
     mix = jnp.sum(jnp.where(hit, route_weights.T[:, :, None], 0.0), axis=0)
     high = mix.astype(BF16)
     low = (mix - high.astype(F32)).astype(BF16)
-
-    owner = lax.axis_index(("exp", "rep")).astype(jnp.int32).reshape(1, 1)
-    positive_row = positives.reshape(1, total_queries)
-
-    states_a, sum_a = kernel_call(
+    mix_parts = jnp.stack([high, low])
+
+    owner = lax.axis_index(("exp", "rep")).astype(jnp.int32)
+    hit_query = jnp.max(jnp.where(positives == owner, jnp.arange(total_queries, dtype=jnp.int32), -1)).reshape(1, 1)
+
+    (base,) = kernel_call(
         lambda *refs: mix_kernel(tail, *refs),
-        [((tok_count, model_width // 2), BF16), ((tok_count, unit_width), F32)],
-        [VMEM] * 5,
-        (back_a, high, low, passages_in, projection),
-        [pltpu.VMEM((fold, LANES), F32)],
+        [((tok_count, model_width), BF16)],
+        [VMEM] * 3,
+        (back_a, mix_parts, passages_in),
+        [fold_room],
+        room=56,
     )
     columns = query_len * total_queries
-    far = (back_b, high, low, passages_in, projection, states_a, query_rows)
-    chunks = columns // (4 * LANES)
-    near_weights = pltpu.VMEM((tok_count, columns), F32)
-    near_states = pltpu.VMEM((tok_count, model_width), BF16)
-    states, weights, unit, radius, totals, logits, shares = kernel_call(
+    states, states_near, weights, unit, radius, totals, logits, shares = kernel_call(
         lambda *refs: score_kernel(tail, logit_gain, *refs),
         [
+            ((tok_count, model_width), BF16),
             ((tok_count, model_width), BF16),
             ((tok_count, columns), F32),
             ((tok_count, unit_width), F32),
@@ -518,13 +442,11 @@
             ((1, total_queries), F32),
             ((2 * experts, total_queries), F32),
         ],
-        [SMEM, VMEM, VMEM] + [HBM] * len(far),
-        (owner, sum_a, positive_row) + far,
-        [pltpu.VMEM(a.shape, a.dtype) for a in far]
-        + [fold_room, near_states, near_weights]
-        + [copy_sems((len(far),)), copy_sems, copy_sems((chunks,))],
-        room=56,
-        out_specs=[HBM] * 2 + [VMEM] * 5,
+        [SMEM] + [VMEM] * 5,
+        (hit_query, back_b, mix_parts, base, projection, query_rows),
+        [fold_room, copy_sems],
+        room=24,
+        out_specs=[HBM] + [VMEM] * 7,
     )
 
     def share_out(rows, axis):
@@ -541,10 +463,9 @@
     share, loss = kernel_call(
         lambda *refs: grad_kernel(logit_gain, *refs),
         [((model_width, unit_width), BF16), ((1, LANES), F32)],
-        [SMEM] + [VMEM] * 6 + [HBM] * 3,
-        (owner, sums, logits, positive_row, totals, unit, radius, weights, query_rows, states),
-        [near_weights, pltpu.VMEM(query_rows.shape, BF16), near_states, copy_sems((2,)), copy_sems((chunks,))],
-        room=56,
+        [SMEM] + [VMEM] * 8,
+        (hit_query, sums, logits, weights, totals, query_rows, unit, radius, states_near),
+        room=24,
     )
     rows_out = model_width // experts
     parts = exchange(share.reshape(experts, rows_out, unit_width))

time: 287 us -> 282 us (0.983)
  Pallas kernels: 41.6 us -> 37 us
    pallas_call x9, Pallas kernels: 41.6 us -> 37 us  [kernel_call(): pl.pallas_call(kernel, in_specs=ins, out_specs=out_specs or [VMEM] * len(...]
  transfers between devices with their start and end apart: 5 -> 5, of which waited for: 5 -> 5; matrix products, arithmetic and copies ran while one was open for 2% -> 2% of each run, Pallas kernels for 9% -> 11%
where the time goes in v5:
time: 282 us; the launch traced here: 281 us
  waiting for transfers between devices  126 us (45%)
  blocking collectives  62.5 us (22%)
  Pallas kernels  37 us (13%)
  starting transfers between devices  30 us (11%)
  between operations  14.3 us (5%)
  local copies, waits for them, and re-layouts  5.34 us (2%)
  other arithmetic  5.07 us (2%)
    all_to_all x3, waiting for transfers between devices, exchange(): return lax.all_to_all(tiles, 'exp', split_axis=0, concat_axis=0, tiled=True)  95.7 us
    pallas_call x9, Pallas kernels, kernel_call(): pl.pallas_call(kernel, in_specs=ins, out_specs=out_specs or [VMEM] * len(...  37 us
    all_to_all x3, starting transfers between devices, exchange(): return lax.all_to_all(tiles, 'exp', split_axis=0, concat_axis=0, tiled=True)  30 us
    all_to_all x2, blocking collectives, share_out(): lax.all_to_all(pairs, axis, split_axis=0, concat_axis=0, tiled=True)  27.5 us
    all_gather x1, waiting for transfers between devices, body(): second_all = lax.all_gather(second_part, 'rep', axis=0, tiled=False)  22.8 us
    all_to_all x1, blocking collectives, exchange(): return lax.all_to_all(tiles, 'exp', split_axis=0, concat_axis=0, tiled=True)  22.6 us
    all_to_all x1, blocking collectives, body(): lax.all_to_all(sent, 'rep', split_axis=0, concat_axis=0, tiled=True)  12.5 us
    all_gather x1, waiting for transfers between devices, body(): first_all = lax.all_gather(first_part, 'rep', axis=0, tiled=False)  7.71 us
  transfers between devices with their start and end apart: 5, of which 5 were waited for; matrix products, arithmetic and copies ran while one was open for 2% of the time, Pallas kernels for 11%

profile of v5, /device:TPU:6, one launch (start us, length us, event | category | flops | bytes accessed | tf_op | source)
XLA Modules:
  0.0 280.8 jit_solution(17004178023760339213)
XLA Ops:
  7.2 2.3 shard_map.114
  9.6 2.8 %shard_map.112 = bf16[64,22,8,128]{3,2,1,0:T(8,128)(2,1)} custom-call(s32[2,180]{1,0:T(2,128)S(1)} %bitcast.42, bf16[180,2048]{1,0:T(8,128)(2,1)S(1)} %copy-done.1), custom_call_target="tpu_custom_call" | custom-call | tf_op jit(solution)/shard_map/pallas_call | solution.py:23
  12.4 11.3 %all-to-all-start = ((bf16[64,22,8,128]{3,2,1,0:T(8,128)(2,1)}), bf16[64,22,8,128]{3,2,1,0:T(8,128)(2,1)}, u32[]{:S(2)}, u32[]{:S(2)}) async-start(bf16[64,22,8,128]{3,2,1,0:T(8,128)(2,1)} %shard_map.112), calls=%async_computation | async-start | bytes 5767168 | tf_op jit(solution)/shard_map/all_to_all | solution.py:367
  23.9 0.1 fusion.5
  24.1 0.8 maximum_maximum_fusion
  24.9 64.3 %all-to-all-done.refs_0_ = bf16[64,22,8,128]{3,2,1,0:T(8,128)(2,1)} async-done(((bf16[64,22,8,128]{3,2,1,0:T(8,128)(2,1)}), bf16[64,22,8,128]{3,2,1,0:T(8,128)(2,1)}, u32[]{:S(2)}, u32[]{:S(2)}) %all-to-all-start) | async-done | bytes 2883616 | tf_op jit(solution)/shard_map/all_to_all | solution.py:367
  89.2 4.4 %shard_map.113.refs_0_ = bf16[8,704,256]{2,1,0:T(8,128)(2,1)} custom-call(bf16[64,22,8,128]{3,2,1,0:T(8,128)(2,1)} %all-to-all-done.refs_0_), custom_call_target="tpu_custom_call" | custom-call | tf_op jit(solution)/shard_map/pallas_call | solution.py:23
  93.5 7.7 %all-gather.5.cloned.1.call-done = bf16[14080,256]{1,0:T(8,128)(2,1)} async-done(((bf16[1760,256]{1,0:T(8,128)(2,1)}), bf16[14080,256]{1,0:T(8,128)(2,1)}) %all-gather.5.cloned.1.call-update) | async-done | bytes 7208976 | tf_op jit(solution)/shard_map/all_gather | solution.py:343
  101.2 12.4 %shard_map.115 = (bf16[704,704]{1,0:T(8,128)(2,1)}, bf16[64,11,8,128]{3,2,1,0:T(8,128)(2,1)}) custom-call(bf16[8,704,256]{2,1,0:T(8,128)(2,1)} %shard_map.113.refs_0_, bf16[8,1760,256]{2,1,0:T(8,128)(2,1)} %bitcast.44), custom_call_target="tpu_custom_call" | custom-call | tf_op jit(solution)/shard_map/pallas_call | solution.py:23
  113.7 10.5 %all-to-all-start.2 = ((bf16[64,11,8,128]{3,2,1,0:T(8,128)(2,1)}), bf16[64,11,8,128]{3,2,1,0:T(8,128)(2,1)S(1)}, u32[]{:S(2)}, u32[]{:S(2)}) async-start(bf16[64,11,8,128]{3,2,1,0:T(8,128)(2,1)} %get-tuple-element.18), calls=%async_computation.2 | async-start | bytes 2883584 | tf_op jit(solution)/shard_map/all_to_all | solution.py:367
  124.2 22.8 %all-gather.7.cloned.1.call-done = bf16[4864,256]{1,0:T(8,128)(2,1)} async-done(((bf16[608,256]{1,0:T(8,128)(2,1)}), bf16[4864,256]{1,0:T(8,128)(2,1)}) %all-gather.7.cloned.1.call-update) | async-done | bytes 2490384 | tf_op jit(solution)/shard_map/all_gather | solution.py:358
  147.0 6.3 %shard_map.116 = bf16[64,11,8,128]{3,2,1,0:T(8,128)(2,1)} custom-call(bf16[704,704]{1,0:T(8,128)(2,1)} %get-tuple-element.16.refs_0_, bf16[8,608,256]{2,1,0:T(8,128)(2,1)} %bitcast.45), custom_call_target="tpu_custom_call" | custom-call | tf_op jit(solution)/shard_map/pallas_call | solution.py:23
  153.3 5.7 %all-to-all-done.2.refs_0_ = bf16[64,11,8,128]{3,2,1,0:T(8,128)(2,1)S(1)} async-done(((bf16[64,11,8,128]{3,2,1,0:T(8,128)(2,1)}), bf16[64,11,8,128]{3,2,1,0:T(8,128)(2,1)S(1)}, u32[]{:S(2)}, u32[]{:S(2)}) %all-to-all-start.2) | async-done | bytes 1441824 | tf_op jit(solution)/shard_map/all_to_all | solution.py:367
  159.1 1.1 copy-done.5
  160.2 8.2 %all-to-all-start.1 = ((bf16[64,11,8,128]{3,2,1,0:T(8,128)(2,1)}), bf16[64,11,8,128]{3,2,1,0:T(8,128)(2,1)S(1)}, u32[]{:S(2)}, u32[]{:S(2)}) async-start(bf16[64,11,8,128]{3,2,1,0:T(8,128)(2,1)} %shard_map.116), calls=%async_computation.1 | async-start | bytes 2883584 | tf_op jit(solution)/shard_map/all_to_all | solution.py:367
  168.6 0.2 fusion
  169.1 0.6 fusion.7
  169.7 1.7 fusion.1
  171.5 0.9 pad_maximum_fusion.1.refs_1_.refs_2_
  172.3 1.3 fusion.8
  173.7 0.3 copy.19
  174.0 3.6 %shard_map.117.refs_3_ = bf16[180,2048]{1,0:T(8,128)(2,1)} custom-call(bf16[64,11,8,128]{3,2,1,0:T(8,128)(2,1)} %copy-done.5, bf16[2,180,704]{2,1,0:T(8,128)(2,1)} %pad_maximum_fusion.1.refs_1_.refs_2_, bf16[180,2048]{1,0:T(8,128)(2,1)} %refs_2_.1), custom_call_target="tpu_custom_call" | custom-call | tf_op jit(solution)/shard_map/pallas_call | solution.py:23
  177.6 25.7 %all-to-all-done.1.refs_1_ = bf16[64,11,8,128]{3,2,1,0:T(8,128)(2,1)S(1)} async-done(((bf16[64,11,8,128]{3,2,1,0:T(8,128)(2,1)}), bf16[64,11,8,128]{3,2,1,0:T(8,128)(2,1)S(1)}, u32[]{:S(2)}, u32[]{:S(2)}) %all-to-all-start.1) | async-done | bytes 1441824 | tf_op jit(solution)/shard_map/all_to_all | solution.py:367
  203.3 1.1 copy-done.2
  204.4 1.0 copy-done.3
  205.5 3.0 %shard_map.118 = (bf16[180,2048]{1,0:T(8,128)(2,1)}, bf16[180,2048]{1,0:T(8,128)(2,1)S(1)}, f32[180,4096]{1,0:T(8,128)S(1)}, f32[180,128]{1,0:T(8,128)S(1)}, f32...) custom-call(s32[1,1]{1,0:T(1,128)} %bitcast.refs_0_, ...), custom_call_target="tpu_custom_call" | custom-call | tf_op jit(solution)/shard_map/pallas_call | solution.py:23
  208.5 15.8 %all_to_all.35 = f32[64,2,128]{2,1,0:T(2,128)S(1)} all-to-all(f32[64,2,128]{2,1,0:T(2,128)S(1)} %bitcast.39), channel_id=1, replica_groups=mesh['exp'=64,'rep'=8] {'exp'}, dimensions={0} | all-to-all | bytes 131072 | tf_op jit(solution)/shard_map/all_to_all | solution.py:454
  224.3 11.7 %all_to_all.36 = f32[8,2,128]{2,1,0:T(2,128)S(1)} all-to-all(f32[8,2,128]{2,1,0:T(2,128)S(1)} %bitcast.41), channel_id=1, replica_groups=mesh['exp'=64,'rep'=8] {'rep'}, dimensions={0} | all-to-all | bytes 16384 | tf_op jit(solution)/shard_map/all_to_all | solution.py:454
  236.0 2.2 shard_map.120
  238.2 22.6 %all_to_all.37 = bf16[64,32,128]{2,1,0:T(8,128)(2,1)S(1)} all-to-all(bf16[64,32,128]{2,1,0:T(8,128)(2,1)S(1)} %bitcast.37), channel_id=1, replica_groups=mesh['exp'=64,'rep'=8] {'exp'}, dimensions={0} | all-to-all | bytes 1048576 | tf_op jit(solution)/shard_map/all_to_all | solution.py:367
  260.9 12.5 %all_to_all.38 = f32[8,32,128]{2,1,0:T(8,128)S(1)} all-to-all(f32[8,32,128]{2,1,0:T(8,128)S(1)} %broadcast_in_dim.36), channel_id=1, replica_groups=mesh['exp'=64,'rep'=8] {'rep'}, dimensions={0} | all-to-all | bytes 262144 | tf_op jit(solution)/shard_map/all_to_all | solution.py:474
  273.4 0.6 reduce_sum.52
  (38 shorter events, 1.0 us)
Async XLA Ops:
  7.2 2.4 copy-start.4
  7.2 2.4 copy-start.1
  7.2 94.1 %all-gather.5.cloned.1.call-start = ((), (), s32[]{:S(2)}) async-start(), calls=%async_computation.7 | async-start | bytes 8110080 | tf_op jit(solution)/shard_map/all_gather | solution.py:343
  12.4 11.3 %copy-start.7 = (bf16[16,32,128]{2,1,0:T(8,128)(2,1)S(1)}, bf16[16,32,128]{2,1,0:T(8,128)(2,1)}, u32[]{:S(2)}) copy-start(bf16[16,32,128]{2,1,0:T(8,128)(2,1)} %param.16) | copy-start | bytes 393220
  12.4 11.7 %copy-start.6 = (bf16[1,704,256]{2,1,0:T(8,128)(2,1)S(1)}, bf16[1,704,256]{2,1,0:T(8,128)(2,1)}, u32[]{:S(2)}) copy-start(bf16[1,704,256]{2,1,0:T(8,128)(2,1)} %param.14) | copy-start | bytes 1081348
  12.4 76.8 %all-to-all-start = ((bf16[64,22,8,128]{3,2,1,0:T(8,128)(2,1)}), bf16[64,22,8,128]{3,2,1,0:T(8,128)(2,1)}, u32[]{:S(2)}, u32[]{:S(2)}) async-start(bf16[64,22,8,128]{3,2,1,0:T(8,128)(2,1)} %shard_map.112), calls=%async_computation | async-start | bytes 5767168 | tf_op jit(solution)/shard_map/all_to_all | solution.py:367
  23.7 123.3 %all-gather.7.cloned.1.call-start = ((), (), s32[]{:S(2)}) async-start(), calls=%async_computation.8 | async-start | bytes 2801664 | tf_op jit(solution)/shard_map/all_gather | solution.py:358
  113.7 45.4 %all-to-all-start.2 = ((bf16[64,11,8,128]{3,2,1,0:T(8,128)(2,1)}), bf16[64,11,8,128]{3,2,1,0:T(8,128)(2,1)S(1)}, u32[]{:S(2)}, u32[]{:S(2)}) async-start(bf16[64,11,8,128]{3,2,1,0:T(8,128)(2,1)} %get-tuple-element.18), calls=%async_computation.2 | async-start | bytes 2883584 | tf_op jit(solution)/shard_map/all_to_all | solution.py:367
  153.3 15.1 %copy-start.8 = (f32[180,2]{0,1:T(2,128)S(1)}, f32[180,2]{0,1:T(2,128)}, u32[]{:S(2)}) copy-start(f32[180,2]{0,1:T(2,128)} %param.11) | copy-start | bytes 4324
  153.3 15.8 %copy-start.9 = (s32[128]{0:T(128)S(1)}, s32[128]{0:T(128)}, u32[]{:S(2)}) copy-start(s32[128]{0:T(128)} %param.17) | copy-start | bytes 1540
  159.1 1.1 copy-start.5
  160.2 43.1 %all-to-all-start.1 = ((bf16[64,11,8,128]{3,2,1,0:T(8,128)(2,1)}), bf16[64,11,8,128]{3,2,1,0:T(8,128)(2,1)S(1)}, u32[]{:S(2)}, u32[]{:S(2)}) async-start(bf16[64,11,8,128]{3,2,1,0:T(8,128)(2,1)} %shard_map.116), calls=%async_computation.1 | async-start | bytes 2883584 | tf_op jit(solution)/shard_map/all_to_all | solution.py:367
  174.0 29.3 %copy-start = (bf16[2,180,704]{2,1,0:T(8,128)(2,1)S(1)}, bf16[2,180,704]{2,1,0:T(8,128)(2,1)}, u32[]{:S(2)}) copy-start(bf16[2,180,704]{2,1,0:T(8,128)(2,1)} %pad_maximum_fusion.1.refs_1_.refs_2_) | copy-start | bytes 1520644
  203.3 1.1 copy-start.2
  204.4 1.0 copy-start.3
Sparse Core Ops, SparseCore 0:
  10.1 91.0 all-gather.4
  103.9 43.0 all-gather.6

commit v6 on v5

--- a/solution.py
+++ b/solution.py
@@ -128,9 +128,9 @@
 def down_half(tail, hidden, wd_ref, downs, out_ref, fold_ref):
     experts = out_ref.shape[0]
     pairs = wd_ref.shape[0] // 2
+    for copy in downs:
+        copy.wait()
     for p in range(pairs):
-        for copy in downs[2 * p : 2 * p + 2]:
-            copy.wait()
         pair = (wd_ref[2 * p], wd_ref[2 * p + 1])
         weight = jnp.concatenate(
             [jnp.concatenate([w[:, lane_block(h)] for w in pair], axis=1) for h in range(2)], axis=0
@@ -160,7 +160,7 @@
 
 
 def expert_kernel(
-    tail, in_ref, w_ref, hid_ref, out_ref, rows_ref, wv_ref, wd_ref, fold_ref, row_sems, sems, down_sems
+    tail, in_ref, w_ref, far_ref, out_ref, rows_ref, hid_ref, wv_ref, wd_ref, fold_ref, row_sems, sems, down_sems, hid_sem
 ):
     reps, wide, depth = wv_ref.shape
     ff = wide // 2
@@ -174,16 +174,22 @@
             )
         )
     downs = down_copies(w_ref, wide, wd_ref, down_sems)
-    for pair in copies:
-        for copy in pair:
+    sizes = (2, 3, 3)
+    firsts = [sum(sizes[:i]) for i in range(len(sizes))]
+    queue = [sum(copies[r : r + n], ()) for r, n in zip(firsts, sizes)] + [downs]
+    ahead = 2
+    for group in queue[:ahead]:
+        for copy in group:
             copy.start()
-    for copy in downs:
-        copy.start()
     step = count // 2
     sums = [None] * 4
     for r in range(reps):
-        for copy in copies[r]:
-            copy.wait()
+        if r in firsts:
+            for copy in queue[firsts.index(r)]:
+                copy.wait()
+            for group in queue[firsts.index(r) + ahead :][:1]:
+                for copy in group:
+                    copy.start()
         for i in range(4):
             rows = rows_ref[r, (i // 2) * step : (i // 2 + 1) * step, :]
             weight = wv_ref[r, (i % 2) * ff : (i % 2 + 1) * ff, :]
@@ -192,7 +198,10 @@
     for i in range(2):
         gate, up = sums[2 * i], sums[2 * i + 1]
         hid_ref[i * step : (i + 1) * step, :] = (gate / (1.0 + jnp.exp(-gate)) * up).astype(BF16)
+    kept = pltpu.make_async_copy(hid_ref, far_ref, hid_sem)
+    kept.start()
     down_half(tail, hid_ref[...], wd_ref, downs, out_ref, fold_ref)
+    kept.wait()
 
 
 def second_kernel(tail, hid_ref, w_ref, out_ref, wd_ref, fold_ref, down_sems):
@@ -202,7 +211,13 @@
     down_half(tail, hid_ref[...], wd_ref, downs, out_ref, fold_ref)
 
 
+def part_rows(rows):
+    return (rows + 63) // 64 * 64
+
+
 def mix_half(half, back_ref, mix_ref, base_ref, fold_ref, tail, store):
+    tokens = base_ref.shape[0]
+    spread = part_rows(tokens)
     experts = back_ref.shape[0]
     blocks = base_ref.shape[1] // (2 * LANES)
     first = experts * HEAD
@@ -212,8 +227,8 @@
         head = jnp.concatenate([get_head(back_ref, c) for c in cs], axis=1)
         rest = jnp.concatenate([get_tail(fold_ref, c, experts * tail) for c in cs], axis=1)
         added = sum(
-            jnp.dot(mix_ref[i, :, :first], head, preferred_element_type=F32)
-            + jnp.dot(mix_ref[i, :, first:], rest, preferred_element_type=F32)
+            jnp.dot(mix_ref[i * spread : i * spread + tokens, :first], head, preferred_element_type=F32)
+            + jnp.dot(mix_ref[i * spread : i * spread + tokens, first:], rest, preferred_element_type=F32)
             for i in range(2)
         )
         for j, c in enumerate(cs):
@@ -230,7 +245,7 @@
     mix_half(0, back_ref, mix_ref, x_ref, fold_ref, tail, store)
 
 
-def score_kernel(tail, gain, hit_ref, back_ref, mix_ref, base_ref, proj_ref, query_ref, *refs):
+def score_kernel(tail, gain, hit_ref, back_ref, mix_ref, base_ref, query_ref, *refs):
     states_out_ref, states_ref, weights_ref, unit_ref, radius_ref, totals_ref, logits_ref, shares_ref = refs[:8]
     fold_ref, out_sem = refs[8:]
 
@@ -242,7 +257,14 @@
     mix_half(1, back_ref, mix_ref, base_ref, fold_ref, tail, store)
     copy_out = pltpu.make_async_copy(states_ref, states_out_ref, out_sem)
     copy_out.start()
-    projected = jnp.dot(states_ref[...], proj_ref[...], preferred_element_type=F32)
+    first = 2 * part_rows(states_ref.shape[0])
+    depth = mix_ref.shape[0] - first
+    projected = sum(
+        jnp.dot(
+            states_ref[:, b * depth : (b + 1) * depth], mix_ref[first:, lane_block(b)], preferred_element_type=F32
+        )
+        for b in range(states_ref.shape[1] // depth)
+    )
     radius = jnp.sqrt(jnp.sum(projected * projected, axis=1, keepdims=True) + norm_eps)
     unit = projected / radius
     unit_ref[...] = unit
@@ -387,10 +409,12 @@
         [((slots, ff), BF16), half_tiles],
         [HBM, HBM],
         (rows_in, first_all),
-        [pltpu.VMEM((rep_count, slots, depth), BF16), pltpu.VMEM((rep_count, 2 * ff, depth), BF16)]
-        + [down_room, fold_room]
-        + [copy_sems((rep_count,))] * 3,
+        [pltpu.VMEM((rep_count, slots, depth), BF16), pltpu.VMEM((slots, ff), BF16)]
+        + [pltpu.VMEM((rep_count, 2 * ff, depth), BF16), down_room, fold_room]
+        + [copy_sems((rep_count,))] * 3
+        + [copy_sems],
         room=56,
+        out_specs=[HBM, VMEM],
     )
     back_a = exchange(send_a)
     (send_b,) = kernel_call(
@@ -416,7 +440,10 @@
     mix = jnp.sum(jnp.where(hit, route_weights.T[:, :, None], 0.0), axis=0)
     high = mix.astype(BF16)
     low = (mix - high.astype(F32)).astype(BF16)
-    mix_parts = jnp.stack([high, low])
+    spare = ((0, part_rows(tok_count) - tok_count), (0, 0))
+    side = projection.reshape(4, model_width // 4, unit_width).transpose(1, 0, 2).reshape(model_width // 4, -1)
+    side = jnp.pad(side, ((0, 0), (0, slots - side.shape[1])))
+    mix_parts = jnp.concatenate([jnp.pad(high, spare), jnp.pad(low, spare), side], axis=0)
 
     owner = lax.axis_index(("exp", "rep")).astype(jnp.int32)
     hit_query = jnp.max(jnp.where(positives == owner, jnp.arange(total_queries, dtype=jnp.int32), -1)).reshape(1, 1)
@@ -442,8 +469,8 @@
             ((1, total_queries), F32),
             ((2 * experts, total_queries), F32),
         ],
-        [SMEM] + [VMEM] * 5,
-        (hit_query, back_b, mix_parts, base, projection, query_rows),
+        [SMEM] + [VMEM] * 4,
+        (hit_query, back_b, mix_parts, base, query_rows),
         [fold_room, copy_sems],
         room=24,
         out_specs=[HBM] + [VMEM] * 7,

time: 282 us -> 279 us (0.989)
  transfers between devices with their start and end apart: 5 -> 5, of which waited for: 5 -> 5; matrix products, arithmetic and copies ran while one was open for 2% -> 3% of each run, Pallas kernels for 11% -> 9%
where the time goes in v6:
time: 279 us; the launch traced here: 278 us
  waiting for transfers between devices  125 us (45%)
  blocking collectives  62.5 us (22%)
  Pallas kernels  35.2 us (13%)
  starting transfers between devices  29.9 us (11%)
  between operations  14.4 us (5%)
  other arithmetic  5.41 us (2%)
  local copies, waits for them, and re-layouts  5.3 us (2%)
    all_to_all x3, waiting for transfers between devices, exchange(): return lax.all_to_all(tiles, 'exp', split_axis=0, concat_axis=0, tiled=True)  93.4 us
    pallas_call x9, Pallas kernels, kernel_call(): pl.pallas_call(kernel, in_specs=ins, out_specs=out_specs or [VMEM] * len(...  35.2 us
    all_to_all x3, starting transfers between devices, exchange(): return lax.all_to_all(tiles, 'exp', split_axis=0, concat_axis=0, tiled=True)  29.8 us
    all_to_all x2, blocking collectives, share_out(): lax.all_to_all(pairs, axis, split_axis=0, concat_axis=0, tiled=True)  27.5 us
    all_gather x1, waiting for transfers between devices, body(): second_all = lax.all_gather(second_part, 'rep', axis=0, tiled=False)  25.1 us
    all_to_all x1, blocking collectives, exchange(): return lax.all_to_all(tiles, 'exp', split_axis=0, concat_axis=0, tiled=True)  22.6 us
    all_to_all x1, blocking collectives, body(): lax.all_to_all(sent, 'rep', split_axis=0, concat_axis=0, tiled=True)  12.5 us
    all_gather x1, waiting for transfers between devices, body(): first_all = lax.all_gather(first_part, 'rep', axis=0, tiled=False)  6.41 us
  transfers between devices with their start and end apart: 5, of which 5 were waited for; matrix products, arithmetic and copies ran while one was open for 3% of the time, Pallas kernels for 9%

profile of v6, /device:TPU:6, one launch (start us, length us, event | category | flops | bytes accessed | tf_op | source)
XLA Modules:
  0.0 277.9 jit_solution(3121445727000392285)
XLA Ops:
  7.2 2.3 shard_map.114
  9.6 2.8 %shard_map.112 = bf16[64,22,8,128]{3,2,1,0:T(8,128)(2,1)} custom-call(s32[2,180]{1,0:T(2,128)S(1)} %bitcast.42, bf16[180,2048]{1,0:T(8,128)(2,1)S(1)} %copy-done.1), custom_call_target="tpu_custom_call" | custom-call | tf_op jit(solution)/shard_map/pallas_call | solution.py:23
  12.4 10.9 %all-to-all-start = ((bf16[64,22,8,128]{3,2,1,0:T(8,128)(2,1)}), bf16[64,22,8,128]{3,2,1,0:T(8,128)(2,1)S(1)}, u32[]{:S(2)}, u32[]{:S(2)}) async-start(bf16[64,22,8,128]{3,2,1,0:T(8,128)(2,1)} %shard_map.112), calls=%async_computation | async-start | bytes 5767168 | tf_op jit(solution)/shard_map/all_to_all | solution.py:389
  23.6 0.1 fusion.10
  23.8 0.8 maximum_maximum_fusion
  24.6 64.3 %all-to-all-done.refs_0_ = bf16[64,22,8,128]{3,2,1,0:T(8,128)(2,1)S(1)} async-done(((bf16[64,22,8,128]{3,2,1,0:T(8,128)(2,1)}), bf16[64,22,8,128]{3,2,1,0:T(8,128)(2,1)S(1)}, u32[]{:S(2)}, u32[]{:S(2)}) %all-to-all-start) | async-done | bytes 2883616 | tf_op jit(solution)/shard_map/all_to_all | solution.py:389
  88.9 1.6 copy-done.4
  90.5 4.3 %shard_map.113.refs_0_ = bf16[8,704,256]{2,1,0:T(8,128)(2,1)} custom-call(bf16[64,22,8,128]{3,2,1,0:T(8,128)(2,1)} %copy-done.4), custom_call_target="tpu_custom_call" | custom-call | tf_op jit(solution)/shard_map/pallas_call | solution.py:23
  94.8 6.4 %all-gather.5.cloned.1.call-done = bf16[14080,256]{1,0:T(8,128)(2,1)} async-done(((bf16[1760,256]{1,0:T(8,128)(2,1)}), bf16[14080,256]{1,0:T(8,128)(2,1)}) %all-gather.5.cloned.1.call-update) | async-done | bytes 7208976 | tf_op jit(solution)/shard_map/all_gather | solution.py:365
  101.2 10.1 %shard_map.115 = (bf16[704,704]{1,0:T(8,128)(2,1)}, bf16[64,11,8,128]{3,2,1,0:T(8,128)(2,1)}) custom-call(bf16[8,704,256]{2,1,0:T(8,128)(2,1)} %shard_map.113.refs_0_, bf16[8,1760,256]{2,1,0:T(8,128)(2,1)} %bitcast.44), custom_call_target="tpu_custom_call" | custom-call | tf_op jit(solution)/shard_map/pallas_call | solution.py:23
  111.4 10.5 %all-to-all-start.2 = ((bf16[64,11,8,128]{3,2,1,0:T(8,128)(2,1)}), bf16[64,11,8,128]{3,2,1,0:T(8,128)(2,1)S(1)}, u32[]{:S(2)}, u32[]{:S(2)}) async-start(bf16[64,11,8,128]{3,2,1,0:T(8,128)(2,1)} %get-tuple-element.18), calls=%async_computation.2 | async-start | bytes 2883584 | tf_op jit(solution)/shard_map/all_to_all | solution.py:389
  121.9 25.1 %all-gather.7.cloned.1.call-done = bf16[4864,256]{1,0:T(8,128)(2,1)} async-done(((bf16[608,256]{1,0:T(8,128)(2,1)}), bf16[4864,256]{1,0:T(8,128)(2,1)}) %all-gather.7.cloned.1.call-update) | async-done | bytes 2490384 | tf_op jit(solution)/shard_map/all_gather | solution.py:380
  147.0 5.2 %shard_map.116 = bf16[64,11,8,128]{3,2,1,0:T(8,128)(2,1)} custom-call(bf16[704,704]{1,0:T(8,128)(2,1)} %get-tuple-element.16.refs_0_, bf16[8,608,256]{2,1,0:T(8,128)(2,1)} %bitcast.45), custom_call_target="tpu_custom_call" | custom-call | tf_op jit(solution)/shard_map/pallas_call | solution.py:23
  152.2 4.6 %all-to-all-done.2.refs_0_ = bf16[64,11,8,128]{3,2,1,0:T(8,128)(2,1)S(1)} async-done(((bf16[64,11,8,128]{3,2,1,0:T(8,128)(2,1)}), bf16[64,11,8,128]{3,2,1,0:T(8,128)(2,1)S(1)}, u32[]{:S(2)}, u32[]{:S(2)}) %all-to-all-start.2) | async-done | bytes 1441824 | tf_op jit(solution)/shard_map/all_to_all | solution.py:389
  156.8 8.4 %all-to-all-start.1 = ((bf16[64,11,8,128]{3,2,1,0:T(8,128)(2,1)}), bf16[64,11,8,128]{3,2,1,0:T(8,128)(2,1)}, u32[]{:S(2)}, u32[]{:S(2)}) async-start(bf16[64,11,8,128]{3,2,1,0:T(8,128)(2,1)} %shard_map.116), calls=%async_computation.1 | async-start | bytes 2883584 | tf_op jit(solution)/shard_map/all_to_all | solution.py:389
  165.2 0.4 copy.20
  165.9 0.2 fusion.6
  166.4 0.6 fusion.12
  167.0 1.7 fusion.7
  168.8 1.2 fusion.5.refs_1_.refs_2_
  170.0 1.3 fusion.13
  171.3 0.3 copy.21
  171.6 3.9 %shard_map.117.refs_3_ = bf16[180,2048]{1,0:T(8,128)(2,1)} custom-call(bf16[64,11,8,128]{3,2,1,0:T(8,128)(2,1)} %copy-done.5, bf16[896,704]{1,0:T(8,128)(2,1)} %fusion.5.refs_1_.refs_2_, bf16[180,2048]{1,0:T(8,128)(2,1)} %refs_2_.1), custom_call_target="tpu_custom_call" | custom-call | tf_op jit(solution)/shard_map/pallas_call | solution.py:23
  175.5 24.5 %all-to-all-done.1.refs_1_ = bf16[64,11,8,128]{3,2,1,0:T(8,128)(2,1)} async-done(((bf16[64,11,8,128]{3,2,1,0:T(8,128)(2,1)}), bf16[64,11,8,128]{3,2,1,0:T(8,128)(2,1)}, u32[]{:S(2)}, u32[]{:S(2)}) %all-to-all-start.1) | async-done | bytes 1441824 | tf_op jit(solution)/shard_map/all_to_all | solution.py:389
  200.0 1.1 copy-done.2
  201.1 4.4 %shard_map.118 = (bf16[180,2048]{1,0:T(8,128)(2,1)}, bf16[180,2048]{1,0:T(8,128)(2,1)S(1)}, f32[180,4096]{1,0:T(8,128)S(1)}, f32[180,128]{1,0:T(8,128)S(1)}, f32...) custom-call(s32[1,1]{1,0:T(1,128)} %bitcast.refs_0_, ...), custom_call_target="tpu_custom_call" | custom-call | tf_op jit(solution)/shard_map/pallas_call | solution.py:23
  205.5 15.8 %all_to_all.35 = f32[64,2,128]{2,1,0:T(2,128)S(1)} all-to-all(f32[64,2,128]{2,1,0:T(2,128)S(1)} %bitcast.39), channel_id=1, replica_groups=mesh['exp'=64,'rep'=8] {'exp'}, dimensions={0} | all-to-all | bytes 131072 | tf_op jit(solution)/shard_map/all_to_all | solution.py:481
  221.4 11.7 %all_to_all.36 = f32[8,2,128]{2,1,0:T(2,128)S(1)} all-to-all(f32[8,2,128]{2,1,0:T(2,128)S(1)} %bitcast.41), channel_id=1, replica_groups=mesh['exp'=64,'rep'=8] {'rep'}, dimensions={0} | all-to-all | bytes 16384 | tf_op jit(solution)/shard_map/all_to_all | solution.py:481
  233.0 2.2 shard_map.120
  235.2 22.6 %all_to_all.37 = bf16[64,32,128]{2,1,0:T(8,128)(2,1)S(1)} all-to-all(bf16[64,32,128]{2,1,0:T(8,128)(2,1)S(1)} %bitcast.37), channel_id=1, replica_groups=mesh['exp'=64,'rep'=8] {'exp'}, dimensions={0} | all-to-all | bytes 1048576 | tf_op jit(solution)/shard_map/all_to_all | solution.py:389
  257.9 12.5 %all_to_all.38 = f32[8,32,128]{2,1,0:T(8,128)S(1)} all-to-all(f32[8,32,128]{2,1,0:T(8,128)S(1)} %broadcast_in_dim.36), channel_id=1, replica_groups=mesh['exp'=64,'rep'=8] {'rep'}, dimensions={0} | all-to-all | bytes 262144 | tf_op jit(solution)/shard_map/all_to_all | solution.py:501
  270.4 0.6 reduce_sum.49
  (42 shorter events, 1.1 us)
Async XLA Ops:
  7.2 2.4 copy-start.3
  7.2 2.4 copy-start.1
  7.2 94.1 %all-gather.5.cloned.1.call-start = ((), (), s32[]{:S(2)}) async-start(), calls=%async_computation.7 | async-start | bytes 8110080 | tf_op jit(solution)/shard_map/all_gather | solution.py:365
  12.4 11.0 %copy-start.8 = (bf16[16,32,128]{2,1,0:T(8,128)(2,1)S(1)}, bf16[16,32,128]{2,1,0:T(8,128)(2,1)}, u32[]{:S(2)}) copy-start(bf16[16,32,128]{2,1,0:T(8,128)(2,1)} %param.16) | copy-start | bytes 393220
  12.4 11.4 %copy-start.6 = (bf16[1,704,256]{2,1,0:T(8,128)(2,1)S(1)}, bf16[1,704,256]{2,1,0:T(8,128)(2,1)}, u32[]{:S(2)}) copy-start(bf16[1,704,256]{2,1,0:T(8,128)(2,1)} %param.14) | copy-start | bytes 1081348
  12.4 76.5 %all-to-all-start = ((bf16[64,22,8,128]{3,2,1,0:T(8,128)(2,1)}), bf16[64,22,8,128]{3,2,1,0:T(8,128)(2,1)S(1)}, u32[]{:S(2)}, u32[]{:S(2)}) async-start(bf16[64,22,8,128]{3,2,1,0:T(8,128)(2,1)} %shard_map.112), calls=%async_computation | async-start | bytes 5767168 | tf_op jit(solution)/shard_map/all_to_all | solution.py:389
  23.3 123.7 %all-gather.7.cloned.1.call-start = ((), (), s32[]{:S(2)}) async-start(), calls=%async_computation.8 | async-start | bytes 2801664 | tf_op jit(solution)/shard_map/all_gather | solution.py:380
  88.9 1.6 copy-start.4
  111.4 45.4 %all-to-all-start.2 = ((bf16[64,11,8,128]{3,2,1,0:T(8,128)(2,1)}), bf16[64,11,8,128]{3,2,1,0:T(8,128)(2,1)S(1)}, u32[]{:S(2)}, u32[]{:S(2)}) async-start(bf16[64,11,8,128]{3,2,1,0:T(8,128)(2,1)} %get-tuple-element.18), calls=%async_computation.2 | async-start | bytes 2883584 | tf_op jit(solution)/shard_map/all_to_all | solution.py:389
  152.2 13.0 %copy-start.7 = (bf16[2048,128]{1,0:T(8,128)(2,1)S(1)}, bf16[2048,128]{1,0:T(8,128)(2,1)}, u32[]{:S(2)}) copy-start(bf16[2048,128]{1,0:T(8,128)(2,1)} %param.15) | copy-start | bytes 1572868
  152.2 13.5 %copy-start.9 = (f32[180,2]{0,1:T(2,128)S(1)}, f32[180,2]{0,1:T(2,128)}, u32[]{:S(2)}) copy-start(f32[180,2]{0,1:T(2,128)} %param.11) | copy-start | bytes 4324
  152.2 14.2 %copy-start.10 = (s32[128]{0:T(128)S(1)}, s32[128]{0:T(128)}, u32[]{:S(2)}) copy-start(s32[128]{0:T(128)} %param.17) | copy-start | bytes 1540
  156.8 8.9 %copy-start.5 = (bf16[64,11,8,128]{3,2,1,0:T(8,128)(2,1)}, bf16[64,11,8,128]{3,2,1,0:T(8,128)(2,1)S(1)}, u32[]{:S(2)}) copy-start(bf16[64,11,8,128]{3,2,1,0:T(8,128)(2,1)S(1)} %all-to-all-done.2.refs_0_) | copy-start | bytes 4325380
  156.8 43.2 %all-to-all-start.1 = ((bf16[64,11,8,128]{3,2,1,0:T(8,128)(2,1)}), bf16[64,11,8,128]{3,2,1,0:T(8,128)(2,1)}, u32[]{:S(2)}, u32[]{:S(2)}) async-start(bf16[64,11,8,128]{3,2,1,0:T(8,128)(2,1)} %shard_map.116), calls=%async_computation.1 | async-start | bytes 2883584 | tf_op jit(solution)/shard_map/all_to_all | solution.py:389
  171.6 28.4 %copy-start = (bf16[896,704]{1,0:T(8,128)(2,1)S(1)}, bf16[896,704]{1,0:T(8,128)(2,1)}, u32[]{:S(2)}) copy-start(bf16[896,704]{1,0:T(8,128)(2,1)} %fusion.5.refs_1_.refs_2_) | copy-start | bytes 3784708
  200.0 1.1 copy-start.2
Sparse Core Ops, SparseCore 0:
  10.1 91.0 all-gather.4
  103.9 43.0 all-gather.6
